TPU v7x, 512 devices: a whole 4x4x16 slice. The times are simulated.
512 devices in a mesh: seq: 64 (over y, z), tp: 8 (over x, core).
Axes of the slice: x: 4, y: 4, z: 16, core: 2. Of those that a mesh axis runs over, the one named last changes fastest.
Arguments:
- queries: bfloat16 [32768, 2048], P('seq', 'tp'), may hold values from -5 to 5
- key_vectors: bfloat16 [32768, 2048], P('seq', 'tp'), may hold values from -5 to 5
- value_vectors: bfloat16 [32768, 2048], P('seq', 'tp'), may hold values from -5 to 5
- out_weight: bfloat16 [2048, 2048], P('tp'), may hold values from -0.125 to 0.125
- attn_grad: bfloat16 [32768, 2048], P('seq', 'tp'), may hold values from -5 to 5
- tile_column_mask: int32 [4, 64, 64], replicated, may hold values from 0 to 1, as said below
Outputs:
- projected: bfloat16 [32768, 2048], P('seq', 'tp')
- grad_queries: bfloat16 [32768, 2048], P('seq', 'tp')
- grad_keys: bfloat16 [32768, 2048], P('seq', 'tp')
- grad_values: bfloat16 [32768, 2048], P('seq', 'tp')
Inputs may be any that keep to these rules, and one draw needn't show every extreme that they name: tile_column_mask[b, r, r'] is 0 where r' >= r and 1 where r - 2 <= r' < r.
All inputs are finite; a program needn't handle non-finite values.
Results may differ from a plain program's by a relative error of at most 0.02.
Values may be sent and summed in bfloat16 or wider, within the bound.
No kernel may reach another device: no remote copies, remote signals or barrier semaphores. Data moves between devices by JAX's collectives and lax.ppermute only.
A program may use at most 64 MiB of HBM per device.

v0:
```python
import jax
import jax.numpy as jnp
from jax import lax
from jax.sharding import PartitionSpec as P

HEAD_DIM = 128
COLS = 512
TILE = 128


negative_fill = -1e30


def partial_attention(scores, allowed, value_block, out_form):
    masked = jnp.where(allowed, scores, negative_fill)
    maxima = jnp.max(masked, axis=-1)
    weights = jnp.where(allowed, jnp.exp(masked - maxima[..., None]), 0.0)
    totals = jnp.sum(weights, axis=-1)
    outputs = jnp.einsum(
        out_form, weights.astype(jnp.bfloat16), value_block, preferred_element_type=jnp.float32
    )
    return (outputs, maxima, totals)


def partial_grads(
    scores,
    allowed,
    log_norms,
    gradient_dot_scores,
    grad_block,
    query_block,
    key_block,
    value_block,
    einsum_forms,
    score_scale,
):
    score_form, out_form, back_form = einsum_forms
    masked = jnp.where(allowed, scores, negative_fill)
    weights = jnp.where(allowed, jnp.exp(masked - log_norms[..., None]), 0.0)
    grad_values = jnp.einsum(
        back_form, weights.astype(jnp.bfloat16), grad_block, preferred_element_type=jnp.float32
    )
    grad_weights = jnp.einsum(
        score_form, grad_block, value_block, preferred_element_type=jnp.float32
    )
    grad_scores = (weights * (grad_weights - gradient_dot_scores[..., None])).astype(jnp.bfloat16)
    grad_queries = (
        jnp.einsum(out_form, grad_scores, key_block, preferred_element_type=jnp.float32)
        * score_scale
    )
    grad_keys = (
        jnp.einsum(back_form, grad_scores, query_block, preferred_element_type=jnp.float32)
        * score_scale
    )
    return (grad_queries, grad_keys, grad_values)


def local(queries, key_vectors, value_vectors, out_weight, attn_grad, tile_column_mask):
    tokens_dev, features = queries.shape
    head_count = features // HEAD_DIM
    rows_dev = tokens_dev // COLS
    seq_count = lax.axis_size("seq")
    total_rows = tile_column_mask.shape[1]
    cols_dev = COLS // seq_count
    block_count = tile_column_mask.shape[0]
    score_scale = HEAD_DIM ** (-0.5)
    row_forms = ("rqhd,rkhd->rhqk", "rhqk,rkhd->rqhd", "rhqk,rqhd->rkhd")
    col_forms = ("qchd,kchd->chqk", "chqk,kchd->qchd", "chqk,qchd->kchd")
    row_shape = (rows_dev, COLS, head_count, HEAD_DIM)
    slab_shape = (rows_dev, COLS, features)
    col_shape = (total_rows, cols_dev, head_count, HEAD_DIM)
    query_grid = queries.reshape(row_shape)
    key_grid = key_vectors.reshape(row_shape)
    value_grid = value_vectors.reshape(row_shape)
    grad_grid = attn_grad.reshape(row_shape)
    causal_row = lax.broadcasted_iota(jnp.int32, (COLS, COLS), 1) <= lax.broadcasted_iota(
        jnp.int32, (COLS, COLS), 0
    )
    row_logit_scores = (
        jnp.einsum(row_forms[0], query_grid, key_grid, preferred_element_type=jnp.float32)
        * score_scale
    )
    row_out, row_max, row_sum = partial_attention(
        row_logit_scores, causal_row, value_grid, row_forms[1]
    )
    row_max = jnp.transpose(row_max, (0, 2, 1))
    row_sum = jnp.transpose(row_sum, (0, 2, 1))
    column_query_rows, col_key, col_value, col_grad = (
        lax.all_to_all(queries.reshape(slab_shape), "seq", split_axis=1, concat_axis=0, tiled=True),
        lax.all_to_all(
            key_vectors.reshape(slab_shape), "seq", split_axis=1, concat_axis=0, tiled=True
        ),
        lax.all_to_all(
            value_vectors.reshape(slab_shape), "seq", split_axis=1, concat_axis=0, tiled=True
        ),
        lax.all_to_all(
            attn_grad.reshape(slab_shape), "seq", split_axis=1, concat_axis=0, tiled=True
        ),
    )
    column_query_rows = column_query_rows.reshape(col_shape)
    col_key = col_key.reshape(col_shape)
    col_value = col_value.reshape(col_shape)
    col_grad = col_grad.reshape(col_shape)
    position = lax.axis_index("seq") * cols_dev + jnp.arange(cols_dev, dtype=jnp.int32)
    block_ids = position // TILE
    single_hot_vector = (
        block_ids[:, None] == jnp.arange(block_count, dtype=jnp.int32)[None, :]
    ).astype(jnp.float32)
    column_allowed_mask = (
        jnp.einsum("ed,dtx->etx", single_hot_vector, tile_column_mask.astype(jnp.float32)) > 0.5
    )
    earlier = lax.broadcasted_iota(jnp.int32, (total_rows, total_rows), 1) < lax.broadcasted_iota(
        jnp.int32, (total_rows, total_rows), 0
    )
    col_allowed = (column_allowed_mask & earlier[None])[:, None]
    col_scores = (
        jnp.einsum(col_forms[0], column_query_rows, col_key, preferred_element_type=jnp.float32)
        * score_scale
    )
    col_out, col_max, col_sum = partial_attention(col_scores, col_allowed, col_value, col_forms[1])
    back_out, back_max, back_sum = (
        lax.all_to_all(
            col_out.reshape(total_rows, cols_dev, features),
            "seq",
            split_axis=0,
            concat_axis=1,
            tiled=True,
        ),
        lax.all_to_all(
            jnp.transpose(col_max, (2, 0, 1)), "seq", split_axis=0, concat_axis=1, tiled=True
        ),
        lax.all_to_all(
            jnp.transpose(col_sum, (2, 0, 1)), "seq", split_axis=0, concat_axis=1, tiled=True
        ),
    )
    back_out = back_out.reshape(row_shape)
    merged = jnp.maximum(row_max, back_max)
    row_factor = jnp.exp(row_max - merged)
    col_factor = jnp.exp(back_max - merged)
    denominator = row_sum * row_factor + back_sum * col_factor
    log_norms = merged + jnp.log(denominator)
    attention = (
        (row_out * row_factor[..., None] + back_out * col_factor[..., None])
        / denominator[..., None]
    ).astype(jnp.bfloat16)
    attention_flat = attention.reshape(tokens_dev, features)
    local_term = jnp.dot(attention_flat, out_weight, preferred_element_type=jnp.float32)
    projected = lax.psum_scatter(
        local_term.astype(jnp.bfloat16), "tp", scatter_dimension=1, tiled=True
    )
    gradient_dot_scores = jnp.sum(
        attention.astype(jnp.float32) * grad_grid.astype(jnp.float32), axis=-1
    )
    row_again = (
        jnp.einsum(row_forms[0], query_grid, key_grid, preferred_element_type=jnp.float32)
        * score_scale
    )
    col_again = (
        jnp.einsum(col_forms[0], column_query_rows, col_key, preferred_element_type=jnp.float32)
        * score_scale
    )
    row_grad_query, row_grad_key, row_grad_value = partial_grads(
        row_again,
        causal_row,
        jnp.transpose(log_norms, (0, 2, 1)),
        jnp.transpose(gradient_dot_scores, (0, 2, 1)),
        grad_grid,
        query_grid,
        key_grid,
        value_grid,
        row_forms,
        score_scale,
    )
    col_log, col_dots = (
        lax.all_to_all(log_norms, "seq", split_axis=1, concat_axis=0, tiled=True),
        lax.all_to_all(gradient_dot_scores, "seq", split_axis=1, concat_axis=0, tiled=True),
    )
    col_grad_query, col_grad_key, col_grad_value = partial_grads(
        col_again,
        col_allowed,
        jnp.transpose(col_log, (1, 2, 0)),
        jnp.transpose(col_dots, (1, 2, 0)),
        col_grad,
        column_query_rows,
        col_key,
        col_value,
        col_forms,
        score_scale,
    )
    back_query, back_key, back_value = (
        lax.all_to_all(
            col_grad_query.astype(jnp.bfloat16).reshape(total_rows, cols_dev, features),
            "seq",
            split_axis=0,
            concat_axis=1,
            tiled=True,
        ),
        lax.all_to_all(
            col_grad_key.astype(jnp.bfloat16).reshape(total_rows, cols_dev, features),
            "seq",
            split_axis=0,
            concat_axis=1,
            tiled=True,
        ),
        lax.all_to_all(
            col_grad_value.astype(jnp.bfloat16).reshape(total_rows, cols_dev, features),
            "seq",
            split_axis=0,
            concat_axis=1,
            tiled=True,
        ),
    )

    def finish(row_part, back_part):
        restored_layout = back_part.reshape(tokens_dev, features)
        return (
            row_part.reshape(tokens_dev, features) + restored_layout.astype(jnp.float32)
        ).astype(jnp.bfloat16)

    grad_queries = finish(row_grad_query, back_query)
    grad_keys = finish(row_grad_key, back_key)
    grad_values = finish(row_grad_value, back_value)
    return (projected, grad_queries, grad_keys, grad_values)


def solution(mesh):
    return jax.shard_map(
        local,
        mesh=mesh,
        in_specs=(
            P("seq", "tp"),
            P("seq", "tp"),
            P("seq", "tp"),
            P("tp", None),
            P("seq", "tp"),
            P(),
        ),
        out_specs=(P("seq", "tp"), P("seq", "tp"), P("seq", "tp"), P("seq", "tp")),
        check_vma=False,
    )
```

profile of v0, /device:TPU:6, one launch (start us, length us, event | category | flops | bytes accessed | tf_op | source)
XLA Modules:
  0.0 332.3 jit_solution(17171477576062789373)
XLA Ops:
  7.2 1.5 copy.286
  9.2 2.2 reduce.5
  12.1 18.7 %all-to-all-start.1 = ((bf16[64,2,1024]{2,1,0:T(2,128)(2,1)}), bf16[64,2,1024]{2,1,0:T(2,128)(2,1)S(1)}, u32[]{:S(2)}, u32[]{:S(2)}) async-start(bf16[64,2,1024]{2,1,0:T(2,128)(2,1)} %reshape.275), calls=%async_computation.1 | async-start | bytes 524288 | tf_op jit(solution)/shard_map/all_to_all | solution.py:90
  31.3 2.2 reduce.6
  34.3 17.6 %all-to-all-done.1 = bf16[64,2,1024]{2,1,0:T(2,128)(2,1)S(1)} async-done(((bf16[64,2,1024]{2,1,0:T(2,128)(2,1)}), bf16[64,2,1024]{2,1,0:T(2,128)(2,1)S(1)}, u32[]{:S(2)}, u32[]{:S(2)}) %all-to-all-start.1) | async-done | bytes 262176 | tf_op jit(solution)/shard_map/all_to_all | solution.py:90
  51.9 6.4 %all-to-all-start = ((bf16[64,2,1024]{2,1,0:T(2,128)(2,1)}), bf16[64,2,1024]{2,1,0:T(2,128)(2,1)S(1)}, u32[]{:S(2)}, u32[]{:S(2)}) async-start(bf16[64,2,1024]{2,1,0:T(2,128)(2,1)} %reshape.277), calls=%async_computation | async-start | bytes 524288 | tf_op jit(solution)/shard_map/all_to_all | solution.py:89
  58.8 2.1 reduce.7
  61.7 16.9 %all-to-all-done = bf16[64,2,1024]{2,1,0:T(2,128)(2,1)S(1)} async-done(((bf16[64,2,1024]{2,1,0:T(2,128)(2,1)}), bf16[64,2,1024]{2,1,0:T(2,128)(2,1)S(1)}, u32[]{:S(2)}, u32[]{:S(2)}) %all-to-all-start) | async-done | bytes 262176 | tf_op jit(solution)/shard_map/all_to_all | solution.py:89
  78.6 6.4 %all-to-all-start.3 = ((bf16[64,2,1024]{2,1,0:T(2,128)(2,1)}), bf16[64,2,1024]{2,1,0:T(2,128)(2,1)S(1)}, u32[]{:S(2)}, u32[]{:S(2)}) async-start(bf16[64,2,1024]{2,1,0:T(2,128)(2,1)} %reshape.279), calls=%async_computation.3 | async-start | bytes 524288 | tf_op jit(solution)/shard_map/all_to_all | solution.py:93
  88.0 16.6 %all-to-all-done.3 = bf16[64,2,1024]{2,1,0:T(2,128)(2,1)S(1)} async-done(((bf16[64,2,1024]{2,1,0:T(2,128)(2,1)}), bf16[64,2,1024]{2,1,0:T(2,128)(2,1)S(1)}, u32[]{:S(2)}, u32[]{:S(2)}) %all-to-all-start.3) | async-done | bytes 262176 | tf_op jit(solution)/shard_map/all_to_all | solution.py:93
  104.6 6.7 %all-to-all-start.5 = ((f32[64,8,2]{1,2,0:T(2,128)}), f32[64,8,2]{1,2,0:T(2,128)S(1)}, u32[]{:S(2)}, u32[]{:S(2)}) async-start(f32[64,8,2]{1,2,0:T(2,128)} %copy.195), calls=%async_computation.5 | async-start | bytes 131072 | tf_op jit(solution)/shard_map/all_to_all | solution.py:132
  112.3 13.5 %all-to-all-done.5 = f32[64,8,2]{1,2,0:T(2,128)S(1)} async-done(((f32[64,8,2]{1,2,0:T(2,128)}), f32[64,8,2]{1,2,0:T(2,128)S(1)}, u32[]{:S(2)}, u32[]{:S(2)}) %all-to-all-start.5) | async-done | bytes 4128 | tf_op jit(solution)/shard_map/all_to_all | solution.py:132
  125.8 4.6 %all-to-all-start.2 = ((f32[64,8,2]{1,2,0:T(2,128)}), f32[64,8,2]{1,2,0:T(2,128)S(1)}, u32[]{:S(2)}, u32[]{:S(2)}) async-start(f32[64,8,2]{1,2,0:T(2,128)} %copy.187), calls=%async_computation.2 | async-start | bytes 131072 | tf_op jit(solution)/shard_map/all_to_all | solution.py:129
  130.8 1.1 copy.278
  131.9 13.2 %all-to-all-done.2 = f32[64,8,2]{1,2,0:T(2,128)S(1)} async-done(((f32[64,8,2]{1,2,0:T(2,128)}), f32[64,8,2]{1,2,0:T(2,128)S(1)}, u32[]{:S(2)}, u32[]{:S(2)}) %all-to-all-start.2) | async-done | bytes 4128 | tf_op jit(solution)/shard_map/all_to_all | solution.py:129
  145.1 5.5 %all-to-all-start.4 = ((f32[64,8,256]{2,1,0:T(8,128)}), f32[64,8,256]{2,1,0:T(8,128)}, u32[]{:S(2)}, u32[]{:S(2)}) async-start(f32[64,8,256]{2,1,0:T(8,128)} %bitcast.163), calls=%async_computation.4 | async-start | bytes 1048576 | tf_op jit(solution)/shard_map/all_to_all | solution.py:122
  154.5 2.1 reduce.8
  157.6 1.7 fusion.60
  162.3 16.0 %all-to-all-done.4 = f32[64,8,256]{2,1,0:T(8,128)} async-done(((f32[64,8,256]{2,1,0:T(8,128)}), f32[64,8,256]{2,1,0:T(8,128)}, u32[]{:S(2)}, u32[]{:S(2)}) %all-to-all-start.4) | async-done | bytes 524320 | tf_op jit(solution)/shard_map/all_to_all | solution.py:122
  178.3 6.9 %all-to-all-start.7 = ((bf16[64,2,1024]{2,1,0:T(2,128)(2,1)}), bf16[64,2,1024]{2,1,0:T(2,128)(2,1)}, u32[]{:S(2)}, u32[]{:S(2)}) async-start(bf16[64,2,1024]{2,1,0:T(2,128)(2,1)} %reshape.281), calls=%async_computation.8 | async-start | bytes 524288 | tf_op jit(solution)/shard_map/all_to_all | solution.py:96
  185.3 2.1 reshape.259
  187.4 2.0 copy.194
  189.5 2.0 multiply_reduce_fusion
  191.5 2.1 convolution_convert_fusion
  194.5 8.2 %all-to-all-done.7 = bf16[64,2,1024]{2,1,0:T(2,128)(2,1)} async-done(((bf16[64,2,1024]{2,1,0:T(2,128)(2,1)}), bf16[64,2,1024]{2,1,0:T(2,128)(2,1)}, u32[]{:S(2)}, u32[]{:S(2)}) %all-to-all-start.7) | async-done | bytes 262176 | tf_op jit(solution)/shard_map/all_to_all | solution.py:96
  202.7 7.1 %all-to-all-start.6 = ((f32[1,512,2]{2,0,1:T(1,128)}), f32[1,512,2]{2,0,1:T(1,128)}, u32[]{:S(2)}, u32[]{:S(2)}) async-start(f32[1,512,2]{2,0,1:T(1,128)} %copy.203), calls=%async_computation.7 | async-start | bytes 524288 | tf_op jit(solution)/shard_map/all_to_all | solution.py:175
  209.8 2.8 reshape.282
  212.6 1.8 copy.282
  214.4 12.3 %all-to-all-done.6 = f32[1,512,2]{2,0,1:T(1,128)} async-done(((f32[1,512,2]{2,0,1:T(1,128)}), f32[1,512,2]{2,0,1:T(1,128)}, u32[]{:S(2)}, u32[]{:S(2)}) %all-to-all-start.6) | async-done | bytes 4128 | tf_op jit(solution)/shard_map/all_to_all | solution.py:175
  228.7 6.9 %all-to-all-start.8 = ((f32[1,512,2]{2,0,1:T(1,128)}), f32[1,512,2]{2,0,1:T(1,128)}, u32[]{:S(2)}, u32[]{:S(2)}) async-start(f32[1,512,2]{2,0,1:T(1,128)} %copy.210), calls=%async_computation.9 | async-start | bytes 524288 | tf_op jit(solution)/shard_map/all_to_all | solution.py:176
  235.6 1.4 fusion.14
  237.8 14.3 %all-to-all-done.8 = f32[1,512,2]{2,0,1:T(1,128)} async-done(((f32[1,512,2]{2,0,1:T(1,128)}), f32[1,512,2]{2,0,1:T(1,128)}, u32[]{:S(2)}, u32[]{:S(2)}) %all-to-all-start.8) | async-done | bytes 4128 | tf_op jit(solution)/shard_map/all_to_all | solution.py:176
  252.2 6.9 %all-to-all-start.11 = ((bf16[64,8,256]{2,1,0:T(8,128)(2,1)}), bf16[64,8,256]{2,1,0:T(8,128)(2,1)}, u32[]{:S(2)}, u32[]{:S(2)}) async-start(bf16[64,8,256]{2,1,0:T(8,128)(2,1)} %bitcast.196), calls=%async_computation.12 | async-start | bytes 524288 | tf_op jit(solution)/shard_map/all_to_all | solution.py:205
  260.2 1.5 fusion.8
  262.4 1.2 fusion.13
  264.5 11.2 %all-to-all-done.11 = bf16[64,8,256]{2,1,0:T(8,128)(2,1)} async-done(((bf16[64,8,256]{2,1,0:T(8,128)(2,1)}), bf16[64,8,256]{2,1,0:T(8,128)(2,1)}, u32[]{:S(2)}, u32[]{:S(2)}) %all-to-all-start.11) | async-done | bytes 262176 | tf_op jit(solution)/shard_map/all_to_all | solution.py:205
  275.6 6.8 %all-to-all-start.9 = ((bf16[64,8,256]{2,1,0:T(8,128)(2,1)}), bf16[64,8,256]{2,1,0:T(8,128)(2,1)}, u32[]{:S(2)}, u32[]{:S(2)}) async-start(bf16[64,8,256]{2,1,0:T(8,128)(2,1)} %bitcast.197), calls=%async_computation.10 | async-start | bytes 524288 | tf_op jit(solution)/shard_map/all_to_all | solution.py:191
  283.3 2.4 fusion.16
  285.8 2.1 copy.227
  287.9 1.9 fusion.25
  289.7 1.2 fusion.12
  291.8 7.1 %all-to-all-done.9 = bf16[64,8,256]{2,1,0:T(8,128)(2,1)} async-done(((bf16[64,8,256]{2,1,0:T(8,128)(2,1)}), bf16[64,8,256]{2,1,0:T(8,128)(2,1)}, u32[]{:S(2)}, u32[]{:S(2)}) %all-to-all-start.9) | async-done | bytes 262176 | tf_op jit(solution)/shard_map/all_to_all | solution.py:191
  299.0 8.2 %all-to-all-start.10 = ((bf16[64,8,256]{2,1,0:T(8,128)(2,1)}), bf16[64,8,256]{2,1,0:T(8,128)(2,1)}, u32[]{:S(2)}, u32[]{:S(2)}) async-start(bf16[64,8,256]{2,1,0:T(8,128)(2,1)} %bitcast.195), calls=%async_computation.11 | async-start | bytes 524288 | tf_op jit(solution)/shard_map/all_to_all | solution.py:198
  307.2 1.9 multiply_convert_fusion
  311.0 1.7 convolution_multiply_fusion.1
  312.9 1.7 fusion.27
  314.6 9.1 %all-to-all-done.10 = bf16[64,8,256]{2,1,0:T(8,128)(2,1)} async-done(((bf16[64,8,256]{2,1,0:T(8,128)(2,1)}), bf16[64,8,256]{2,1,0:T(8,128)(2,1)}, u32[]{:S(2)}, u32[]{:S(2)}) %all-to-all-start.10) | async-done | bytes 262176 | tf_op jit(solution)/shard_map/all_to_all | solution.py:198
  323.7 1.7 fusion.26
  (82 shorter events, 26.0 us)
Async XLA Ops:
  7.2 184.3 %copy-start = (bf16[256,2048]{1,0:T(8,128)(2,1)S(1)}, bf16[256,2048]{1,0:T(8,128)(2,1)}, u32[]{:S(2)}) copy-start(bf16[256,2048]{1,0:T(8,128)(2,1)} %param.9) | copy-start | bytes 3145732
  7.2 23.7 %copy-start.9 = (bf16[512,256]{1,0:T(8,128)(2,1)S(1)}, bf16[512,256]{1,0:T(8,128)(2,1)}, u32[]{:S(2)}) copy-start(bf16[512,256]{1,0:T(8,128)(2,1)} %param.6) | copy-start | bytes 786436
  9.2 49.2 %copy-start.11 = (bf16[512,256]{1,0:T(8,128)(2,1)S(1)}, bf16[512,256]{1,0:T(8,128)(2,1)}, u32[]{:S(2)}) copy-start(bf16[512,256]{1,0:T(8,128)(2,1)} %param.8) | copy-start | bytes 786436
  12.1 39.7 %all-to-all-start.1 = ((bf16[64,2,1024]{2,1,0:T(2,128)(2,1)}), bf16[64,2,1024]{2,1,0:T(2,128)(2,1)S(1)}, u32[]{:S(2)}, u32[]{:S(2)}) async-start(bf16[64,2,1024]{2,1,0:T(2,128)(2,1)} %reshape.275), calls=%async_computation.1 | async-start | bytes 524288 | tf_op jit(solution)/shard_map/all_to_all | solution.py:90
  31.3 53.7 %copy-start.16 = (s32[4,64,64]{2,1,0:T(8,128)S(1)}, s32[4,64,64]{2,1,0:T(8,128)}, u32[]{:S(2)}) copy-start(s32[4,64,64]{2,1,0:T(8,128)} %param.11) | copy-start | bytes 196612
  51.9 26.7 %all-to-all-start = ((bf16[64,2,1024]{2,1,0:T(2,128)(2,1)}), bf16[64,2,1024]{2,1,0:T(2,128)(2,1)S(1)}, u32[]{:S(2)}, u32[]{:S(2)}) async-start(bf16[64,2,1024]{2,1,0:T(2,128)(2,1)} %reshape.277), calls=%async_computation | async-start | bytes 524288 | tf_op jit(solution)/shard_map/all_to_all | solution.py:89
  78.6 26.0 %all-to-all-start.3 = ((bf16[64,2,1024]{2,1,0:T(2,128)(2,1)}), bf16[64,2,1024]{2,1,0:T(2,128)(2,1)S(1)}, u32[]{:S(2)}, u32[]{:S(2)}) async-start(bf16[64,2,1024]{2,1,0:T(2,128)(2,1)} %reshape.279), calls=%async_computation.3 | async-start | bytes 524288 | tf_op jit(solution)/shard_map/all_to_all | solution.py:93
  86.1 0.7 copy-start.13
  86.1 18.5 %copy-start.12 = (bf16[64,8,2,128]{3,1,2,0:T(8,128)(2,1)}, bf16[64,8,2,128]{3,1,2,0:T(8,128)(2,1)S(1)}, u32[]{:S(2)}) copy-start(bf16[64,8,2,128]{3,1,2,0:T(8,128)(2,1)S(1)} %get-tuple-element.15) | copy-start | bytes 786436
  87.1 44.8 %copy-start.1 = (f32[8,2,64,64]{2,3,1,0:T(8,128)}, f32[8,2,64,64]{2,3,1,0:T(8,128)S(1)}, u32[]{:S(2)}) copy-start(f32[8,2,64,64]{2,3,1,0:T(8,128)S(1)} %get-tuple-element.11) | copy-start | bytes 786436
  104.6 21.3 %all-to-all-start.5 = ((f32[64,8,2]{1,2,0:T(2,128)}), f32[64,8,2]{1,2,0:T(2,128)S(1)}, u32[]{:S(2)}, u32[]{:S(2)}) async-start(f32[64,8,2]{1,2,0:T(2,128)} %copy.195), calls=%async_computation.5 | async-start | bytes 131072 | tf_op jit(solution)/shard_map/all_to_all | solution.py:132
  111.6 18.9 %copy-start.14 = (bf16[1,512,256]{2,1,0:T(8,128)(2,1)}, bf16[1,512,256]{2,1,0:T(8,128)(2,1)S(1)}, u32[]{:S(2)}) copy-start(bf16[1,512,256]{2,1,0:T(8,128)(2,1)S(1)} %copy.283) | copy-start | bytes 786436
  111.6 39.9 %copy-start.10 = (bf16[512,256]{1,0:T(8,128)(2,1)S(1)}, bf16[512,256]{1,0:T(8,128)(2,1)}, u32[]{:S(2)}) copy-start(bf16[512,256]{1,0:T(8,128)(2,1)} %param.7) | copy-start | bytes 786436
  125.8 19.3 %all-to-all-start.2 = ((f32[64,8,2]{1,2,0:T(2,128)}), f32[64,8,2]{1,2,0:T(2,128)S(1)}, u32[]{:S(2)}, u32[]{:S(2)}) async-start(f32[64,8,2]{1,2,0:T(2,128)} %copy.187), calls=%async_computation.2 | async-start | bytes 131072 | tf_op jit(solution)/shard_map/all_to_all | solution.py:129
  130.8 22.4 %copy-start.3 = (bf16[512,256]{1,0:T(8,128)(2,1)S(1)}, bf16[512,256]{1,0:T(8,128)(2,1)}, u32[]{:S(2)}) copy-start(bf16[512,256]{1,0:T(8,128)(2,1)} %param.10) | copy-start | bytes 786436
  145.1 9.4 %copy-start.15 = (f32[64,8,2]{1,2,0:T(2,128)}, f32[64,8,2]{1,2,0:T(2,128)S(1)}, u32[]{:S(2)}) copy-start(f32[64,8,2]{1,2,0:T(2,128)S(1)} %all-to-all-done.2) | copy-start | bytes 12292
  145.1 33.2 %all-to-all-start.4 = ((f32[64,8,256]{2,1,0:T(8,128)}), f32[64,8,256]{2,1,0:T(8,128)}, u32[]{:S(2)}, u32[]{:S(2)}) async-start(f32[64,8,256]{2,1,0:T(8,128)} %bitcast.163), calls=%async_computation.4 | async-start | bytes 1048576 | tf_op jit(solution)/shard_map/all_to_all | solution.py:122
  157.5 2.2 copy-start.6
  178.3 24.3 %all-to-all-start.7 = ((bf16[64,2,1024]{2,1,0:T(2,128)(2,1)}), bf16[64,2,1024]{2,1,0:T(2,128)(2,1)}, u32[]{:S(2)}, u32[]{:S(2)}) async-start(bf16[64,2,1024]{2,1,0:T(2,128)(2,1)} %reshape.281), calls=%async_computation.8 | async-start | bytes 524288 | tf_op jit(solution)/shard_map/all_to_all | solution.py:96
  185.3 140.2 %reduce-scatter.2.cloned.1.call-start = ((), (), s32[]{:S(2)}) async-start(), calls=%async_computation.13 | async-start | bytes 2359296 | tf_op jit(solution)/shard_map/reduce_scatter | solution.py:148
  202.7 24.0 %all-to-all-start.6 = ((f32[1,512,2]{2,0,1:T(1,128)}), f32[1,512,2]{2,0,1:T(1,128)}, u32[]{:S(2)}, u32[]{:S(2)}) async-start(f32[1,512,2]{2,0,1:T(1,128)} %copy.203), calls=%async_computation.7 | async-start | bytes 524288 | tf_op jit(solution)/shard_map/all_to_all | solution.py:175
  228.7 23.5 %all-to-all-start.8 = ((f32[1,512,2]{2,0,1:T(1,128)}), f32[1,512,2]{2,0,1:T(1,128)}, u32[]{:S(2)}, u32[]{:S(2)}) async-start(f32[1,512,2]{2,0,1:T(1,128)} %copy.210), calls=%async_computation.9 | async-start | bytes 524288 | tf_op jit(solution)/shard_map/all_to_all | solution.py:176
  252.2 23.5 %all-to-all-start.11 = ((bf16[64,8,256]{2,1,0:T(8,128)(2,1)}), bf16[64,8,256]{2,1,0:T(8,128)(2,1)}, u32[]{:S(2)}, u32[]{:S(2)}) async-start(bf16[64,8,256]{2,1,0:T(8,128)(2,1)} %bitcast.196), calls=%async_computation.12 | async-start | bytes 524288 | tf_op jit(solution)/shard_map/all_to_all | solution.py:205
  261.7 0.7 copy-start.8
  275.6 23.3 %all-to-all-start.9 = ((bf16[64,8,256]{2,1,0:T(8,128)(2,1)}), bf16[64,8,256]{2,1,0:T(8,128)(2,1)}, u32[]{:S(2)}, u32[]{:S(2)}) async-start(bf16[64,8,256]{2,1,0:T(8,128)(2,1)} %bitcast.197), calls=%async_computation.10 | async-start | bytes 524288 | tf_op jit(solution)/shard_map/all_to_all | solution.py:191
  285.8 21.4 %copy-start.7 = (pred[512,512]{0,1:T(8,128)(4,1)S(1)}, pred[512,512]{0,1:T(8,128)(4,1)}, u32[]{:S(2)}) copy-start(pred[512,512]{0,1:T(8,128)(4,1)} %copy-done.6) | copy-start | bytes 786436
  299.0 24.8 %all-to-all-start.10 = ((bf16[64,8,256]{2,1,0:T(8,128)(2,1)}), bf16[64,8,256]{2,1,0:T(8,128)(2,1)}, u32[]{:S(2)}, u32[]{:S(2)}) async-start(bf16[64,8,256]{2,1,0:T(8,128)(2,1)} %bitcast.195), calls=%async_computation.11 | async-start | bytes 524288 | tf_op jit(solution)/shard_map/all_to_all | solution.py:198
  307.2 2.9 copy-start.5
  309.1 1.0 copy-start.2
  310.0 1.0 copy-start.4
Sparse Core Ops, SparseCore 0:
  193.7 39.2 reduce-scatter.1
where the time goes:
time: 334 us; the launch traced here: 332 us
  waiting for transfers between devices  156 us (47%)
  starting transfers between devices  91.3 us (27%)
  local copies, waits for them, and re-layouts  37.5 us (11%)
  matrix products  18.3 us (5%)
  other arithmetic  14.6 us (4%)
  between operations  14.5 us (4%)
    all_to_all x1, starting transfers between devices, local(): lax.all_to_all(key_vectors.reshape(slab_shape), 'seq', split_axis=1, conc...  18.7 us
    all_to_all x1, waiting for transfers between devices, local(): lax.all_to_all(key_vectors.reshape(slab_shape), 'seq', split_axis=1, conc...  17.6 us
    all_to_all x1, waiting for transfers between devices, local(): lax.all_to_all(queries.reshape(slab_shape), 'seq', split_axis=1, concat_a...  16.9 us
    all_to_all x1, waiting for transfers between devices, local(): lax.all_to_all(value_vectors.reshape(slab_shape), 'seq', split_axis=1, co...  16.6 us
    all_to_all x1, waiting for transfers between devices, local(): lax.all_to_all(col_out.reshape(total_rows, cols_dev, features), 'seq', sp...  16 us
    all_to_all x1, waiting for transfers between devices, local(): lax.all_to_all(gradient_dot_scores, 'seq', split_axis=1, concat_axis=0, t...  14.3 us
    all_to_all x1, waiting for transfers between devices, local(): lax.all_to_all(jnp.transpose(col_sum, (2, 0, 1)), 'seq', split_axis=0, co...  13.5 us
    all_to_all x1, waiting for transfers between devices, local(): lax.all_to_all(jnp.transpose(col_max, (2, 0, 1)), 'seq', split_axis=0, co...  13.2 us
  transfers between devices with their start and end apart: 13, of which 12 were waited for; matrix products, arithmetic and copies ran while one was open for 19% of the time, Pallas kernels for 0%

commit v1 on v0

v1 whole, which is shorter than its diff:
```python
import jax
import jax.numpy as jnp
from jax import lax
from jax.experimental import pallas as pl
from jax.experimental.pallas import tpu as pltpu
from jax.sharding import PartitionSpec as P

HEAD_DIM = 128
COLS = 512
TILE = 128
SCALE = HEAD_DIM ** (-0.5)
NEG = -1e30
BLOCK = 256
CSTAT = 64

bf16 = jnp.bfloat16
f32 = jnp.float32


def dot_nt(a, b):
    return lax.dot_general(a, b, (((1,), (1,)), ((), ())), preferred_element_type=f32)


def dot_tn(a, b):
    return lax.dot_general(a, b, (((0,), (0,)), ((), ())), preferred_element_type=f32)


def dot_nn(a, b):
    return jnp.dot(a, b, preferred_element_type=f32)


def head(h):
    return slice(h * HEAD_DIM, (h + 1) * HEAD_DIM)


def lanes_like(rows):
    return lax.broadcasted_iota(jnp.int32, (rows, 128), 1)


def put_pieces(tile, lanes, first, x):
    hi = x.astype(bf16).astype(f32)
    rest = x - hi
    mid = rest.astype(bf16).astype(f32)
    low = rest - mid
    for n, piece in enumerate((hi, mid, low)):
        tile = jnp.where(lanes == first + n, piece, tile)
    return tile


def take_lanes(tile, first):
    return tile[:, first : first + 1] + (tile[:, first + 1 : first + 2] + tile[:, first + 2 : first + 3])


def take_rows(tile, first):
    return tile[first : first + 1] + (tile[first + 1 : first + 2] + tile[first + 2 : first + 3])


def row_forward(q_ref, k_ref, v_ref, g_ref, mask_ref, out_ref, stat_ref, bias_ref, bias_t_ref):
    heads = q_ref.shape[1] // HEAD_DIM
    for start in range(0, COLS, BLOCK):
        rows = slice(start, start + BLOCK)
        keys = slice(0, start + BLOCK)
        allowed = lax.broadcasted_iota(jnp.int32, (BLOCK, start + BLOCK), 1) <= (
            lax.broadcasted_iota(jnp.int32, (BLOCK, start + BLOCK), 0) + start
        )
        lanes = lanes_like(BLOCK)
        tile = jnp.zeros((BLOCK, 128), f32)
        for h in range(heads):
            s = dot_nt(q_ref[rows, head(h)], k_ref[keys, head(h)]) * SCALE
            s = jnp.where(allowed, s, NEG)
            m = jnp.max(s, axis=1, keepdims=True)
            p = jnp.exp(s - m)
            total = jnp.sum(p, axis=1, keepdims=True)
            out = dot_nn(p.astype(bf16), v_ref[keys, head(h)]) / total
            out_ref[rows, head(h)] = out
            dots = jnp.sum(out * g_ref[rows, head(h)].astype(f32), axis=1, keepdims=True)
            tile = put_pieces(tile, lanes, 6 * h, m + jnp.log(total))
            tile = put_pieces(tile, lanes, 6 * h + 3, dots)
        stat_ref[rows, :] = tile.astype(bf16)
    total_rows = mask_ref.shape[0]
    width = COLS // total_rows
    mask = mask_ref[...].astype(f32).astype(bf16)
    spread = (
        lax.broadcasted_iota(jnp.int32, (COLS, total_rows), 0) // width
        == lax.broadcasted_iota(jnp.int32, (COLS, total_rows), 1)
    )
    spread = jnp.where(spread, 1.0, 0.0).astype(bf16)
    first = lax.broadcasted_iota(jnp.int32, (COLS, COLS), 0)
    second = lax.broadcasted_iota(jnp.int32, (COLS, COLS), 1)
    same = (first % width) == (second % width)
    whole = dot_nt(dot_nn(spread, mask).astype(bf16), spread)
    whole_t = dot_nt(spread, dot_nn(spread, mask).astype(bf16))
    bias_ref[...] = jnp.where((whole > 0.5) & same & (second < first), 0.0, NEG)
    bias_t_ref[...] = jnp.where((whole_t > 0.5) & same & (first < second), 0.0, NEG)


def col_forward(y_ref, bias_ref, g_ref, stat_ref, send_ref):
    features = g_ref.shape[1]
    heads = features // HEAD_DIM
    send_ref[:, :features] = g_ref[...]
    for start in range(0, COLS, BLOCK):
        rows = slice(start, start + BLOCK)
        keys = slice(0, start + BLOCK)
        lanes = lanes_like(BLOCK)
        tile = stat_ref[rows, :].astype(f32)
        for h in range(heads):
            q = y_ref[rows, head(h)]
            k = y_ref[keys, head(heads + h)]
            v = y_ref[keys, head(2 * heads + h)]
            s = dot_nt(q, k) * SCALE + bias_ref[rows, keys]
            m = jnp.max(s, axis=1, keepdims=True)
            p = jnp.exp(s - m)
            total = jnp.sum(p, axis=1, keepdims=True)
            out = dot_nn(p.astype(bf16), v) / total
            send_ref[rows, head(heads + h)] = out.astype(bf16)
            tile = put_pieces(tile, lanes, CSTAT + 3 * h, m + jnp.log(total))
        send_ref[rows, 2 * features :] = tile.astype(bf16)


def col_backward(y_ref, got_ref, sent_ref, bias_t_ref, send_ref):
    features = y_ref.shape[1] // 3
    heads = features // HEAD_DIM
    lanes = lanes_like(COLS)
    tile = jnp.where(
        lanes < CSTAT,
        got_ref[:, 2 * features :].astype(f32),
        sent_ref[:, 2 * features :].astype(f32),
    )
    for h in range(heads):
        product = got_ref[:, head(h)].astype(f32) * sent_ref[:, head(heads + h)].astype(f32)
        tile = jnp.where(lanes == 32 + h, jnp.sum(product, axis=1, keepdims=True), tile)
    tile = tile.T
    for h in range(heads):
        row_lse = take_rows(tile, 6 * h)
        row_dots = take_rows(tile, 6 * h + 3)
        col_lse = take_rows(tile, CSTAT + 3 * h)
        col_dots = tile[32 + h : 33 + h]
        top = jnp.maximum(row_lse, col_lse)
        row_factor = jnp.exp(row_lse - top)
        col_factor = jnp.exp(col_lse - top)
        both = row_factor + col_factor
        lse = top + jnp.log(both)
        dots = (row_dots * row_factor + col_dots * col_factor) / both
        gradients(
            lambda at: y_ref[at, head(h)],
            lambda at: y_ref[at, head(heads + h)],
            lambda at: y_ref[at, head(2 * heads + h)],
            lambda at: got_ref[at, head(h)],
            lse,
            dots,
            lambda s, keys, rows: s + bias_t_ref[keys, rows],
            send_ref,
            h,
            heads,
            bf16,
        )


def gradients(q, k, v, g, lse, dots, masked, out_ref, h, heads, kind):
    grad_q = None
    for start in range(COLS - BLOCK, -1, -BLOCK):
        keys = slice(start, start + BLOCK)
        rows = slice(start, COLS)
        s = masked(dot_nt(k(keys), q(rows)) * SCALE, keys, rows)
        p = jnp.exp(s - lse[:, start:])
        d = dot_nt(v(keys), g(rows))
        ds = (p * (d - dots[:, start:])).astype(bf16)
        out_ref[keys, head(2 * heads + h)] = dot_nn(p.astype(bf16), g(rows)).astype(kind)
        out_ref[keys, head(heads + h)] = (dot_nn(ds, q(rows)) * SCALE).astype(kind)
        term = dot_tn(ds, k(keys)) * SCALE
        if grad_q is not None:
            term = term + jnp.concatenate([jnp.zeros((BLOCK, HEAD_DIM), f32), grad_q], axis=0)
        grad_q = term
    out_ref[:, head(h)] = grad_q.astype(kind)


def row_merge(out_ref, stat_ref, got_ref, g_ref, weight_ref, part_ref, merged_ref):
    features = g_ref.shape[1]
    heads = features // HEAD_DIM
    lanes = lanes_like(COLS)
    row_tile = stat_ref[...].astype(f32)
    col_tile = got_ref[:, 2 * features :].astype(f32)
    merged = jnp.zeros((COLS, 128), f32)
    parts = []
    for h in range(heads):
        row_lse = take_lanes(row_tile, 6 * h)
        col_lse = take_lanes(col_tile, CSTAT + 3 * h)
        top = jnp.maximum(row_lse, col_lse)
        row_factor = jnp.exp(row_lse - top)
        col_factor = jnp.exp(col_lse - top)
        both = row_factor + col_factor
        att = (
            out_ref[:, head(h)] * row_factor + got_ref[:, head(heads + h)].astype(f32) * col_factor
        ) / both
        att = att.astype(bf16)
        parts.append(att)
        dots = jnp.sum(att.astype(f32) * g_ref[:, head(h)].astype(f32), axis=1, keepdims=True)
        merged = jnp.where(lanes == 2 * h, top + jnp.log(both), merged)
        merged = jnp.where(lanes == 2 * h + 1, dots, merged)
    merged_ref[...] = merged
    att = jnp.concatenate(parts, axis=1)
    step = 512
    for start in range(0, weight_ref.shape[1], step):
        at = slice(start, start + step)
        part_ref[:, at] = dot_nn(att, weight_ref[:, at]).astype(bf16)


def row_backward(q_ref, k_ref, v_ref, g_ref, merged_ref, grad_ref):
    heads = q_ref.shape[1] // HEAD_DIM
    tile = merged_ref[...].T

    def masked(s, keys, rows):
        allowed = (lax.broadcasted_iota(jnp.int32, s.shape, 0) + keys.start) <= (
            lax.broadcasted_iota(jnp.int32, s.shape, 1) + rows.start
        )
        return jnp.where(allowed, s, NEG)

    for h in range(heads):
        gradients(
            lambda at: q_ref[at, head(h)],
            lambda at: k_ref[at, head(h)],
            lambda at: v_ref[at, head(h)],
            lambda at: g_ref[at, head(h)],
            tile[2 * h : 2 * h + 1],
            tile[2 * h + 1 : 2 * h + 2],
            masked,
            grad_ref,
            h,
            heads,
            f32,
        )


def finish(grad_ref, back_ref, q_ref, k_ref, v_ref):
    features = q_ref.shape[1]
    for n, ref in enumerate((q_ref, k_ref, v_ref)):
        at = slice(n * features, (n + 1) * features)
        ref[...] = (grad_ref[:, at] + back_ref[:, at].astype(f32)).astype(bf16)


def call(kernel, outs, cost, *args):
    spec = pl.BlockSpec(memory_space=pltpu.VMEM)
    flops, exps = cost
    moved = sum(a.size * a.dtype.itemsize for a in args)
    moved += sum(o.size * o.dtype.itemsize for o in outs)
    return pl.pallas_call(
        kernel,
        out_shape=outs,
        in_specs=[spec] * len(args),
        out_specs=[spec] * len(outs),
        cost_estimate=pl.CostEstimate(flops=flops, bytes_accessed=moved, transcendentals=exps),
        compiler_params=pltpu.CompilerParams(vmem_limit_bytes=32 * 1024 * 1024),
        name=kernel.__name__,
    )(*args)


def exchange(x):
    return lax.all_to_all(x, "seq", split_axis=0, concat_axis=0, tiled=True)


def local(queries, key_vectors, value_vectors, out_weight, attn_grad, tile_column_mask):
    tokens, features = queries.shape
    heads = features // HEAD_DIM
    width = COLS // lax.axis_size("seq")
    block = (lax.axis_index("seq") * width) // TILE
    mask = lax.dynamic_index_in_dim(tile_column_mask, block, 0, keepdims=False)
    product = 2 * COLS * COLS * HEAD_DIM * heads
    exps = COLS * COLS * heads

    def arr(columns, kind):
        return jax.ShapeDtypeStruct((tokens, columns), kind)

    qkv = exchange(jnp.concatenate([queries, key_vectors, value_vectors], axis=1))
    row_out, row_stat, bias, bias_t = call(
        row_forward,
        [arr(features, f32), arr(128, bf16), arr(COLS, f32), arr(COLS, f32)],
        (2 * product, exps),
        queries, key_vectors, value_vectors, attn_grad, mask,
    )
    (sent,) = call(
        col_forward,
        [arr(2 * features + 128, bf16)],
        (2 * product, exps),
        qkv, bias, attn_grad, row_stat,
    )
    got = exchange(sent)
    (col_grads,) = call(
        col_backward, [arr(3 * features, bf16)], (5 * product, exps), qkv, got, sent, bias_t
    )
    back = exchange(col_grads)
    part, merged = call(
        row_merge,
        [arr(out_weight.shape[1], bf16), arr(128, f32)],
        (2 * tokens * features * out_weight.shape[1], tokens),
        row_out, row_stat, got, attn_grad, out_weight,
    )
    projected = lax.psum_scatter(part, "tp", scatter_dimension=1, tiled=True)
    (row_grads,) = call(
        row_backward, [arr(3 * features, f32)], (5 * product, exps),
        queries, key_vectors, value_vectors, attn_grad, merged,
    )
    grads = call(finish, [arr(features, bf16)] * 3, (3 * tokens * features, 0), row_grads, back)
    return (projected, *grads)


def solution(mesh):
    return jax.shard_map(
        local,
        mesh=mesh,
        in_specs=(
            P("seq", "tp"),
            P("seq", "tp"),
            P("seq", "tp"),
            P("tp", None),
            P("seq", "tp"),
            P(),
        ),
        out_specs=(P("seq", "tp"), P("seq", "tp"), P("seq", "tp"), P("seq", "tp")),
        check_vma=False,
    )
```

time: 334 us -> 183 us (0.55)
  waiting for transfers between devices: 156 us -> 77.9 us
  starting transfers between devices: 91.3 us -> 25.4 us
  blocking collectives: 0 us -> 43.5 us
  local copies, waits for them, and re-layouts: 37.5 us -> 8.21 us
  matrix products: 18.3 us -> 0 us
  other arithmetic: 14.6 us -> 2.16 us
  Pallas kernels: 0 us -> 10.7 us
    all_to_all x12 -> x2, waiting for transfers between devices: 156 us -> 77.9 us  [exchange(): return lax.all_to_all(x, 'seq', split_axis=0, concat_axis=0, tiled=True)]
    all_to_all x12 -> x2, starting transfers between devices: 91.2 us -> 25.3 us  [exchange(): return lax.all_to_all(x, 'seq', split_axis=0, concat_axis=0, tiled=True)]
    all_to_all x0 -> x1, blocking collectives: none -> 43.5 us  [exchange(): return lax.all_to_all(x, 'seq', split_axis=0, concat_axis=0, tiled=True)]
    dot_general x14 -> x0, matrix products: 18.3 us -> none  [the longest x2 3.82 us: partial_grads(): jnp.einsum(back_form, weights.astype(jnp.bfloat16), grad_block, preferred...]
    pallas_call x0 -> x6, Pallas kernels: none -> 10.7 us  [call(): pl.pallas_call(kernel, out_shape=outs, in_specs=[spec] * len(args), out_s...]
    reshape x11 -> x0, local copies, waits for them, and re-layouts: 10.2 us -> none  [the longest x2 4.16 us: local(): back_out = back_out.reshape(row_shape)]
    unnamed x4 -> x0, other arithmetic: 8.57 us -> none
    convert_element_type x4 -> x0, other arithmetic: 5.29 us -> none  [the longest x3 5.28 us: finish(): return (row_part.reshape(tokens_dev, features) + restored_layout.astype(j...]
  transfers between devices with their start and end apart: 13 -> 3, of which waited for: 12 -> 2; matrix products, arithmetic and copies ran while one was open for 19% -> 0% of each run, Pallas kernels for 0% -> 4%
where the time goes in v1:
time: 183 us; the launch traced here: 182 us
  waiting for transfers between devices  77.9 us (43%)
  blocking collectives  43.5 us (24%)
  starting transfers between devices  25.4 us (14%)
  between operations  14.2 us (8%)
  Pallas kernels  10.7 us (6%)
  local copies, waits for them, and re-layouts  8.21 us (4%)
  other arithmetic  2.16 us (1%)
    all_to_all x2, waiting for transfers between devices, exchange(): return lax.all_to_all(x, 'seq', split_axis=0, concat_axis=0, tiled=True)  77.9 us
    all_to_all x1, blocking collectives, exchange(): return lax.all_to_all(x, 'seq', split_axis=0, concat_axis=0, tiled=True)  43.5 us
    all_to_all x2, starting transfers between devices, exchange(): return lax.all_to_all(x, 'seq', split_axis=0, concat_axis=0, tiled=True)  25.3 us
    pallas_call x6, Pallas kernels, call(): pl.pallas_call(kernel, out_shape=outs, in_specs=[spec] * len(args), out_s...  10.7 us
    unnamed x30, local copies, waits for them, and re-layouts  8.2 us
  transfers between devices with their start and end apart: 3, of which 2 were waited for; matrix products, arithmetic and copies ran while one was open for 0% of the time, Pallas kernels for 4%

profile of v1, /device:TPU:6, one launch (start us, length us, event | category | flops | bytes accessed | tf_op | source)
XLA Modules:
  0.0 182.1 jit_solution(3256589981282574047)
XLA Ops:
  7.2 0.0 copy-start
  7.2 0.0 copy-start.4
  7.2 0.0 copy-start.3
  7.2 0.0 copy-start.2
  7.2 0.0 copy-start.1
  7.2 2.2 %maximum_bitcast_fusion = bf16[64,8,768]{2,1,0:T(8,128)(2,1)} fusion(bf16[512,256]{1,0:T(8,128)(2,1)} %v_ref.3, bf16[512,256]{1,0:T(8,128)(2,1)} %k_ref.3, bf16[512,256]{1,0:T(8,128)(2,1)} %q_ref.3), kind=kLoop, calls=%fused_computation | loop fusion | flops 2359296 | bytes 1572864 | tf_op jit(solution)/shard_map/all_to_all | solution.py:258
  9.4 18.7 %all-to-all-start = ((bf16[64,8,768]{2,1,0:T(8,128)(2,1)}), bf16[64,8,768]{2,1,0:T(8,128)(2,1)S(1)}, u32[]{:S(2)}, u32[]{:S(2)}) async-start(bf16[64,8,768]{2,1,0:T(8,128)(2,1)} %maximum_bitcast_fusion), calls=%async_computation | async-start | bytes 1572864 | tf_op jit(solution)/shard_map/all_to_all | solution.py:258
  28.1 0.0 reduce-scatter.2.cloned.1.call-start
  28.2 0.0 copy-done
  28.2 0.0 copy-done.4
  28.2 0.0 copy-done.3
  28.2 0.0 copy-done.2
  28.2 0.0 copy-done.1
  28.3 2.1 %row_forward.1 = (f32[512,256]{1,0:T(8,128)S(1)}, bf16[512,128]{1,0:T(8,128)(2,1)S(1)}, f32[512,512]{1,0:T(8,128)S(1)}, f32[512,512]{1,0:T(8,128)S(1)}) custom-call(bf16[512,256]{1,0:T(8,128)(2,1)S(1)} %copy-done.2, bf16[512,256]{1,0:T(8,128)(2,1)S(1)} %copy-done.3, bf16[512,256]{1,0:T(8,128)(2,1)S(1)} %copy-done.4, bf16[512,256]{1,0:T(8,128)(2,1)S(1)} %copy-done.1, ...), custom_call_target="tpu_custom_call" | custom-call | flops 268435456 | bytes 3817472 | tf_op jit(solution)/shard_map/row_forward/pallas_call | solution.py:246
  30.3 0.0 copy-start.7
  30.4 1.0 copy-done.7
  31.3 0.0 copy-start.9
  31.4 1.0 copy-done.9
  32.4 0.0 copy-start.11
  32.4 0.8 copy-done.11
  33.1 37.9 %all-to-all-done = bf16[64,8,768]{2,1,0:T(8,128)(2,1)S(1)} async-done(((bf16[64,8,768]{2,1,0:T(8,128)(2,1)}), bf16[64,8,768]{2,1,0:T(8,128)(2,1)S(1)}, u32[]{:S(2)}, u32[]{:S(2)}) %all-to-all-start) | async-done | bytes 786464 | tf_op jit(solution)/shard_map/all_to_all | solution.py:258
  71.0 0.0 copy-start.10
  71.0 1.2 copy-done.10
  72.2 0.0 copy-start.6
  72.2 0.0 copy-start.12
  72.2 1.5 col_forward.1.sent_ref
  73.7 43.5 %all_to_all.33 = bf16[64,8,640]{2,1,0:T(8,128)(2,1)S(1)} all-to-all(bf16[64,8,640]{2,1,0:T(8,128)(2,1)S(1)} %bitcast.13), channel_id=1, replica_groups=mesh['seq'=64,'tp'=8] {'seq'}, dimensions={0} | all-to-all | bytes 1310720 | tf_op jit(solution)/shard_map/all_to_all | solution.py:258
  117.2 0.0 copy-done.6
  117.2 0.0 copy-done.12
  117.2 2.1 %row_merge.1 = (bf16[512,2048]{1,0:T(8,128)(2,1)S(1)}, f32[512,128]{1,0:T(8,128)S(1)}) custom-call(f32[512,256]{1,0:T(8,128)S(1)} %copy-done.12, bf16[512,128]{1,0:T(8,128)(2,1)S(1)} %get-tuple-element.14.stat_ref, bf16[512,640]{1,0:T(8,128)(2,1)S(1)} %bitcast.11, bf16[512,256]{1,0:T(8,128)(2,1)S(1)} %copy-done.1, bf16[256,2048]{1,0:T(8,128)(2,1)S(1)} %copy-done.6), custom_call_target="tpu_custom_call" | custom-call | flops 536870912 | bytes 4980736 | tf_op jit(solution)/shard_map/row_merge/pallas_call | solution.py:246
  119.3 0.0 copy-start.5
  119.3 1.3 copy-done.5
  120.6 0.0 copy-start.13
  120.6 0.7 copy-done.13
  121.3 0.0 reduce-scatter.2.cloned.1.call-update
  121.3 0.0 copy-start.8
  121.3 1.2 copy-done.8
  122.5 2.5 %col_backward.1 = bf16[512,768]{1,0:T(8,128)(2,1)} custom-call(bf16[512,768]{1,0:T(8,128)(2,1)S(1)} %bitcast.10, bf16[512,640]{1,0:T(8,128)(2,1)S(1)} %bitcast.12, bf16[512,640]{1,0:T(8,128)(2,1)S(1)} %col_forward.1.sent_ref, f32[512,512]{1,0:T(8,128)S(1)} %copy-done.8), custom_call_target="tpu_custom_call" | custom-call | flops 671088640 | bytes 3932160 | tf_op jit(solution)/shard_map/col_backward/pallas_call | solution.py:246
  125.1 6.6 %all-to-all-start.2 = ((bf16[64,8,768]{2,1,0:T(8,128)(2,1)}), bf16[64,8,768]{2,1,0:T(8,128)(2,1)S(1)}, u32[]{:S(2)}, u32[]{:S(2)}) async-start(bf16[64,8,768]{2,1,0:T(8,128)(2,1)} %bitcast.5), calls=%async_computation.3 | async-start | bytes 1572864 | tf_op jit(solution)/shard_map/all_to_all | solution.py:258
  131.7 0.0 copy-start.14
  131.7 0.9 copy-done.14
  132.7 1.5 row_backward.1.grad_ref
  134.2 40.1 %all-to-all-done.2 = bf16[64,8,768]{2,1,0:T(8,128)(2,1)S(1)} async-done(((bf16[64,8,768]{2,1,0:T(8,128)(2,1)}), bf16[64,8,768]{2,1,0:T(8,128)(2,1)S(1)}, u32[]{:S(2)}, u32[]{:S(2)}) %all-to-all-start.2) | async-done | bytes 786464 | tf_op jit(solution)/shard_map/all_to_all | solution.py:258
  174.2 1.0 finish.1
  175.2 0.0 reduce-scatter.2.cloned.1.call-done
  (1 shorter events, 0.0 us)
Async XLA Ops:
  7.2 21.0 %copy-start = (s32[4,64,64]{2,1,0:T(8,128)S(1)}, s32[4,64,64]{2,1,0:T(8,128)}, u32[]{:S(2)}) copy-start(s32[4,64,64]{2,1,0:T(8,128)} %param.11) | copy-start | bytes 196612
  7.2 21.0 %copy-start.4 = (bf16[512,256]{1,0:T(8,128)(2,1)S(1)}, bf16[512,256]{1,0:T(8,128)(2,1)}, u32[]{:S(2)}) copy-start(bf16[512,256]{1,0:T(8,128)(2,1)} %v_ref.3) | copy-start | bytes 786436
  7.2 21.0 %copy-start.3 = (bf16[512,256]{1,0:T(8,128)(2,1)S(1)}, bf16[512,256]{1,0:T(8,128)(2,1)}, u32[]{:S(2)}) copy-start(bf16[512,256]{1,0:T(8,128)(2,1)} %k_ref.3) | copy-start | bytes 786436
  7.2 21.0 %copy-start.2 = (bf16[512,256]{1,0:T(8,128)(2,1)S(1)}, bf16[512,256]{1,0:T(8,128)(2,1)}, u32[]{:S(2)}) copy-start(bf16[512,256]{1,0:T(8,128)(2,1)} %q_ref.3) | copy-start | bytes 786436
  7.2 21.0 %copy-start.1 = (bf16[512,256]{1,0:T(8,128)(2,1)S(1)}, bf16[512,256]{1,0:T(8,128)(2,1)}, u32[]{:S(2)}) copy-start(bf16[512,256]{1,0:T(8,128)(2,1)} %g_ref.7) | copy-start | bytes 786436
  9.4 61.6 %all-to-all-start = ((bf16[64,8,768]{2,1,0:T(8,128)(2,1)}), bf16[64,8,768]{2,1,0:T(8,128)(2,1)S(1)}, u32[]{:S(2)}, u32[]{:S(2)}) async-start(bf16[64,8,768]{2,1,0:T(8,128)(2,1)} %maximum_bitcast_fusion), calls=%async_computation | async-start | bytes 1572864 | tf_op jit(solution)/shard_map/all_to_all | solution.py:258
  28.1 147.1 %reduce-scatter.2.cloned.1.call-start = ((), (), s32[]{:S(2)}) async-start(), calls=%async_computation.4 | async-start | bytes 2359296 | tf_op jit(solution)/shard_map/reduce_scatter | solution.py:297
  30.3 1.0 copy-start.7
  31.3 1.0 copy-start.9
  32.4 0.8 copy-start.11
  71.0 1.2 copy-start.10
  72.2 45.0 %copy-start.6 = (bf16[256,2048]{1,0:T(8,128)(2,1)S(1)}, bf16[256,2048]{1,0:T(8,128)(2,1)}, u32[]{:S(2)}) copy-start(bf16[256,2048]{1,0:T(8,128)(2,1)} %weight_ref.1) | copy-start | bytes 3145732
  72.2 45.0 %copy-start.12 = (f32[512,256]{1,0:T(8,128)S(1)}, f32[512,256]{1,0:T(8,128)}, u32[]{:S(2)}) copy-start(f32[512,256]{1,0:T(8,128)} %copy-done.11) | copy-start | bytes 1572868
  119.3 1.3 copy-start.5
  120.6 0.7 copy-start.13
  121.3 1.2 copy-start.8
  125.1 49.1 %all-to-all-start.2 = ((bf16[64,8,768]{2,1,0:T(8,128)(2,1)}), bf16[64,8,768]{2,1,0:T(8,128)(2,1)S(1)}, u32[]{:S(2)}, u32[]{:S(2)}) async-start(bf16[64,8,768]{2,1,0:T(8,128)(2,1)} %bitcast.5), calls=%async_computation.3 | async-start | bytes 1572864 | tf_op jit(solution)/shard_map/all_to_all | solution.py:258
  131.7 1.0 copy-start.14
Sparse Core Ops, SparseCore 0:
  121.4 30.7 reduce-scatter.1

commit v2 on v1

--- a/solution.py
+++ b/solution.py
@@ -90,8 +90,16 @@
     same = (first % width) == (second % width)
     whole = dot_nt(dot_nn(spread, mask).astype(bf16), spread)
     whole_t = dot_nt(spread, dot_nn(spread, mask).astype(bf16))
-    bias_ref[...] = jnp.where((whole > 0.5) & same & (second < first), 0.0, NEG)
-    bias_t_ref[...] = jnp.where((whole_t > 0.5) & same & (first < second), 0.0, NEG)
+    bias_ref[...] = jnp.where((whole > 0.5) & same & (second < first), 0.0, NEG).astype(bf16)
+    bias_t_ref[...] = jnp.where((whole_t > 0.5) & same & (first < second), 0.0, NEG).astype(bf16)
+
+
+def col_forward_joined(key_ref, rest_ref, bias_ref, g_ref, stat_ref, send_ref, y_ref):
+    features = g_ref.shape[1]
+    y_ref[:, :features] = rest_ref[:, :features]
+    y_ref[:, features : 2 * features] = key_ref[...]
+    y_ref[:, 2 * features :] = rest_ref[:, features:]
+    col_forward(y_ref, bias_ref, g_ref, stat_ref, send_ref)
 
 
 def col_forward(y_ref, bias_ref, g_ref, stat_ref, send_ref):
@@ -107,7 +115,7 @@
             q = y_ref[rows, head(h)]
             k = y_ref[keys, head(heads + h)]
             v = y_ref[keys, head(2 * heads + h)]
-            s = dot_nt(q, k) * SCALE + bias_ref[rows, keys]
+            s = dot_nt(q, k) * SCALE + bias_ref[rows, keys].astype(f32)
             m = jnp.max(s, axis=1, keepdims=True)
             p = jnp.exp(s - m)
             total = jnp.sum(p, axis=1, keepdims=True)
@@ -148,7 +156,7 @@
             lambda at: got_ref[at, head(h)],
             lse,
             dots,
-            lambda s, keys, rows: s + bias_t_ref[keys, rows],
+            lambda s, keys, rows: s + bias_t_ref[keys, rows].astype(f32),
             send_ref,
             h,
             heads,
@@ -174,7 +182,7 @@
     out_ref[:, head(h)] = grad_q.astype(kind)
 
 
-def row_merge(out_ref, stat_ref, got_ref, g_ref, weight_ref, part_ref, merged_ref):
+def row_merge(core_ref, out_ref, stat_ref, got_ref, g_ref, weight_ref, keep_ref, give_ref, merged_ref):
     features = g_ref.shape[1]
     heads = features // HEAD_DIM
     lanes = lanes_like(COLS)
@@ -199,10 +207,20 @@
         merged = jnp.where(lanes == 2 * h + 1, dots, merged)
     merged_ref[...] = merged
     att = jnp.concatenate(parts, axis=1)
-    step = 512
-    for start in range(0, weight_ref.shape[1], step):
-        at = slice(start, start + step)
-        part_ref[:, at] = dot_nn(att, weight_ref[:, at]).astype(bf16)
+    core = core_ref[0]
+    for n in range(weight_ref.shape[1] // (2 * features)):
+        for ref, side in ((keep_ref, core), (give_ref, 1 - core)):
+            at = pl.ds(pl.multiple_of((2 * n + side) * features, 128), features)
+            ref[:, n * features : (n + 1) * features] = dot_nn(att, weight_ref[:, at]).astype(bf16)
+
+
+def pair_sum(x_ref, keep_ref, got_ref, own_ref, *send_refs):
+    features = own_ref.shape[1]
+    count = 1 + len(send_refs)
+    for n, ref in enumerate((own_ref, *send_refs)):
+        chip = lax.rem(x_ref[0] + n, count)
+        at = pl.ds(pl.multiple_of(chip * features, 128), features)
+        ref[...] = (keep_ref[:, at].astype(f32) + got_ref[:, at].astype(f32)).astype(ref.dtype)
 
 
 def row_backward(q_ref, k_ref, v_ref, g_ref, merged_ref, grad_ref):
@@ -231,25 +249,30 @@
         )
 
 
-def finish(grad_ref, back_ref, q_ref, k_ref, v_ref):
+def finish(grad_ref, back_ref, own_ref, p1_ref, p2_ref, p3_ref, projected_ref, q_ref, k_ref, v_ref):
     features = q_ref.shape[1]
     for n, ref in enumerate((q_ref, k_ref, v_ref)):
         at = slice(n * features, (n + 1) * features)
         ref[...] = (grad_ref[:, at] + back_ref[:, at].astype(f32)).astype(bf16)
+    total = own_ref[...]
+    for ref in (p1_ref, p2_ref, p3_ref):
+        total = total + ref[...].astype(f32)
+    projected_ref[...] = total.astype(bf16)
 
 
 def call(kernel, outs, cost, *args):
-    spec = pl.BlockSpec(memory_space=pltpu.VMEM)
+    vmem = pl.BlockSpec(memory_space=pltpu.VMEM)
+    smem = pl.BlockSpec(memory_space=pltpu.SMEM)
     flops, exps = cost
     moved = sum(a.size * a.dtype.itemsize for a in args)
     moved += sum(o.size * o.dtype.itemsize for o in outs)
     return pl.pallas_call(
         kernel,
         out_shape=outs,
-        in_specs=[spec] * len(args),
-        out_specs=[spec] * len(outs),
+        in_specs=[smem if a.ndim == 1 else vmem for a in args],
+        out_specs=[vmem] * len(outs),
         cost_estimate=pl.CostEstimate(flops=flops, bytes_accessed=moved, transcendentals=exps),
-        compiler_params=pltpu.CompilerParams(vmem_limit_bytes=32 * 1024 * 1024),
+        compiler_params=pltpu.CompilerParams(vmem_limit_bytes=16 * 1024 * 1024),
         name=kernel.__name__,
     )(*args)
 
@@ -270,37 +293,76 @@
     def arr(columns, kind):
         return jax.ShapeDtypeStruct((tokens, columns), kind)
 
-    qkv = exchange(jnp.concatenate([queries, key_vectors, value_vectors], axis=1))
-    row_out, row_stat, bias, bias_t = call(
-        row_forward,
-        [arr(features, f32), arr(128, bf16), arr(COLS, f32), arr(COLS, f32)],
-        (2 * product, exps),
-        queries, key_vectors, value_vectors, attn_grad, mask,
-    )
-    (sent,) = call(
-        col_forward,
-        [arr(2 * features + 128, bf16)],
-        (2 * product, exps),
-        qkv, bias, attn_grad, row_stat,
+    def forward(queries, key_vectors, value_vectors, attn_grad, mask):
+        return call(
+            row_forward,
+            [arr(features, f32), arr(128, bf16), arr(COLS, bf16), arr(COLS, bf16)],
+            (2 * product, exps),
+            queries, key_vectors, value_vectors, attn_grad, mask,
+        )
+
+    def at_once(queries, key_vectors, value_vectors, attn_grad, mask):
+        qkv = exchange(jnp.concatenate([queries, key_vectors, value_vectors], axis=1))
+        row_out, row_stat, bias, bias_t = forward(queries, key_vectors, value_vectors, attn_grad, mask)
+        (sent,) = call(
+            col_forward,
+            [arr(2 * features + 128, bf16)],
+            (2 * product, exps),
+            qkv, bias, attn_grad, row_stat,
+        )
+        return qkv, sent, row_out, row_stat, bias_t
+
+    def in_two(queries, key_vectors, value_vectors, attn_grad, mask):
+        keys = exchange(key_vectors)
+        row_out, row_stat, bias, bias_t = forward(queries, key_vectors, value_vectors, attn_grad, mask)
+        rest, keys = lax.optimization_barrier((jnp.concatenate([queries, value_vectors], axis=1), keys))
+        rest = exchange(rest)
+        sent, qkv = call(
+            col_forward_joined,
+            [arr(2 * features + 128, bf16), arr(3 * features, bf16)],
+            (2 * product, exps),
+            keys, rest, bias, attn_grad, row_stat,
+        )
+        return qkv, sent, row_out, row_stat, bias_t
+
+    place = lax.axis_index("tp")
+    core = lax.rem(place, 2)
+    qkv, sent, row_out, row_stat, bias_t = lax.cond(
+        core == 1, in_two, at_once, queries, key_vectors, value_vectors, attn_grad, mask
     )
     got = exchange(sent)
     (col_grads,) = call(
         col_backward, [arr(3 * features, bf16)], (5 * product, exps), qkv, got, sent, bias_t
     )
     back = exchange(col_grads)
-    part, merged = call(
+    got, col_grads = lax.optimization_barrier((got, col_grads))
+    half = out_weight.shape[1] // 2
+    keep, give, merged = call(
         row_merge,
-        [arr(out_weight.shape[1], bf16), arr(128, f32)],
+        [arr(half, bf16), arr(half, bf16), arr(128, f32)],
         (2 * tokens * features * out_weight.shape[1], tokens),
-        row_out, row_stat, got, attn_grad, out_weight,
-    )
-    projected = lax.psum_scatter(part, "tp", scatter_dimension=1, tiled=True)
+        core.reshape(1), row_out, row_stat, got, attn_grad, out_weight,
+    )
+    count = lax.axis_size("tp")
+    chips = count // 2
+    pair = lax.ppermute(give, "tp", [(t, t ^ 1) for t in range(count)])
+    own, *sends = call(
+        pair_sum,
+        [arr(features, f32)] + [arr(features, bf16)] * (chips - 1),
+        (tokens * half, 0),
+        (place // 2).reshape(1), keep, pair,
+    )
+    parts = [
+        lax.ppermute(x, "tp", [(t, (t + 2 * n) % count) for t in range(count)])
+        for n, x in enumerate(sends, 1)
+    ]
     (row_grads,) = call(
         row_backward, [arr(3 * features, f32)], (5 * product, exps),
         queries, key_vectors, value_vectors, attn_grad, merged,
     )
-    grads = call(finish, [arr(features, bf16)] * 3, (3 * tokens * features, 0), row_grads, back)
-    return (projected, *grads)
+    return tuple(
+        call(finish, [arr(features, bf16)] * 4, (6 * tokens * features, 0), row_grads, back, own, *parts)
+    )
 
 
 def solution(mesh):

time: 183 us -> 146 us (0.80)
  waiting for transfers between devices: 77.9 us -> 36.8 us
  starting transfers between devices: 25.4 us -> 50.4 us
  between operations: 14.2 us -> 0.79 us
  blocking collectives: 43.5 us -> 31.3 us
  Pallas kernels: 10.7 us -> 17.3 us
  local copies, waits for them, and re-layouts: 8.21 us -> 5.29 us
    all_to_all x2, waiting for transfers between devices: 77.9 us -> 26 us  [exchange(): return lax.all_to_all(x, 'seq', split_axis=0, concat_axis=0, tiled=True)]
    ppermute x0 -> x4, starting transfers between devices: none -> 23.1 us  [the longest x1 14.3 us: local(): pair = lax.ppermute(give, 'tp', [(t, t ^ 1) for t in range(count)])]
    all_to_all x1, blocking collectives: 43.5 us -> 31.3 us  [exchange(): return lax.all_to_all(x, 'seq', split_axis=0, concat_axis=0, tiled=True)]
    ppermute x0 -> x4, waiting for transfers between devices: none -> 10.8 us  [the longest x3 8.32 us: local(): lax.ppermute(x, 'tp', [(t, (t + 2 * n) % count) for t in range(count)])]
    pallas_call x6 -> x7, Pallas kernels: 10.7 us -> 17.3 us  [call(): pl.pallas_call(kernel, out_shape=outs, in_specs=[smem if a.ndim == 1 else...]
    unnamed x30 -> x20, local copies, waits for them, and re-layouts: 8.2 us -> 5.26 us
    all_to_all x2, starting transfers between devices: 25.3 us -> 27.3 us  [exchange(): return lax.all_to_all(x, 'seq', split_axis=0, concat_axis=0, tiled=True)]
  transfers between devices with their start and end apart: 3 -> 6, of which waited for: 2 -> 4; matrix products, arithmetic and copies ran while one was open for 0% -> 0% of each run, Pallas kernels for 4% -> 7%
where the time goes in v2:
time: 146 us; the launch traced here: 144 us
  starting transfers between devices  50.4 us (35%)
  waiting for transfers between devices  36.8 us (25%)
  blocking collectives  31.3 us (21%)
  Pallas kernels  17.3 us (12%)
  local copies, waits for them, and re-layouts  5.29 us (4%)
  other arithmetic  2.13 us (1%)
    all_to_all x1, blocking collectives, exchange(): return lax.all_to_all(x, 'seq', split_axis=0, concat_axis=0, tiled=True)  31.3 us
    all_to_all x2, starting transfers between devices, exchange(): return lax.all_to_all(x, 'seq', split_axis=0, concat_axis=0, tiled=True)  27.3 us
    all_to_all x2, waiting for transfers between devices, exchange(): return lax.all_to_all(x, 'seq', split_axis=0, concat_axis=0, tiled=True)  26 us
    pallas_call x7, Pallas kernels, call(): pl.pallas_call(kernel, out_shape=outs, in_specs=[smem if a.ndim == 1 else...  17.3 us
    ppermute x1, starting transfers between devices, local(): pair = lax.ppermute(give, 'tp', [(t, t ^ 1) for t in range(count)])  14.3 us
    ppermute x3, starting transfers between devices, local(): lax.ppermute(x, 'tp', [(t, (t + 2 * n) % count) for t in range(count)])  8.77 us
    ppermute x3, waiting for transfers between devices, local(): lax.ppermute(x, 'tp', [(t, (t + 2 * n) % count) for t in range(count)])  8.32 us
    unnamed x20, local copies, waits for them, and re-layouts  5.26 us
  transfers between devices with their start and end apart: 6, of which 4 were waited for; matrix products, arithmetic and copies ran while one was open for 0% of the time, Pallas kernels for 7%

profile of v2, /device:TPU:6, one launch (start us, length us, event | category | flops | bytes accessed | tf_op | source)
XLA Modules:
  0.0 144.1 jit_solution(16196238107599820566)
XLA Ops:
  0.6 0.0 copy-start
  0.7 0.9 copy-done
  1.5 52.4 %conditional.1 = (bf16[512,768]{1,0:T(8,128)(2,1)}, bf16[512,640]{1,0:T(8,128)(2,1)S(1)}, f32[512,256]{1,0:T(8,128)}, bf16[512,128]{1,0:T(8,128)(2,1)}, bf16[512,512]{1,0:T(8,128)(2,1)}) conditional(s32[]{:T(128)} %convert_element_type.3, (bf16[512,256]{1,0:T(8,128)(2,1)}, bf16[512,256]{1,0:T(8,128)(2,1)}, bf16[512,256]{1,0:T(8,128)(2,1)}, ...), branch_computations={%region_0.1_spmd, %region_1.2_spmd} | conditional | flops 539230208 | bytes 16400596 | solution.py:330
  1.5 0.0 copy-start.9
  1.5 0.0 copy-start.13
  1.6 0.0 copy-start.15
  1.6 0.0 copy-start.17
  1.6 2.1 %maximum_bitcast_fusion = bf16[64,8,768]{2,1,0:T(8,128)(2,1)} fusion(bf16[512,256]{1,0:T(8,128)(2,1)} %get-tuple-element.22.v_ref, bf16[512,256]{1,0:T(8,128)(2,1)} %get-tuple-element.21.k_ref, bf16[512,256]{1,0:T(8,128)(2,1)} %get-tuple-element.20.q_ref), kind=kLoop, calls=%fused_computation | loop fusion | flops 2359296 | bytes 1572864 | tf_op jit(solution)/shard_map/cond/branch_0_fun/all_to_all | solution.py:281
  3.7 18.7 %all-to-all-start = ((bf16[64,8,768]{2,1,0:T(8,128)(2,1)}), bf16[64,8,768]{2,1,0:T(8,128)(2,1)S(1)}, u32[]{:S(2)}, u32[]{:S(2)}) async-start(bf16[64,8,768]{2,1,0:T(8,128)(2,1)} %maximum_bitcast_fusion), calls=%async_computation | async-start | bytes 1572864 | tf_op jit(solution)/shard_map/cond/branch_0_fun/all_to_all | solution.py:281
  22.4 0.0 copy-done.9
  22.5 0.0 copy-done.13
  22.5 0.0 copy-done.15
  22.5 0.0 copy-done.17
  22.5 3.0 %row_forward.2 = (f32[512,256]{1,0:T(8,128)}, bf16[512,128]{1,0:T(8,128)(2,1)}, bf16[512,512]{1,0:T(8,128)(2,1)S(1)}, bf16[512,512]{1,0:T(8,128)(2,1)}) custom-call(bf16[512,256]{1,0:T(8,128)(2,1)S(1)} %copy-done.13, bf16[512,256]{1,0:T(8,128)(2,1)S(1)} %copy-done.15, bf16[512,256]{1,0:T(8,128)(2,1)S(1)} %copy-done.17, bf16[512,256]{1,0:T(8,128)(2,1)S(1)} %copy-done.9, ...), custom_call_target="tpu_custom_call" | custom-call | flops 268435456 | bytes 2768896 | tf_op jit(solution)/shard_map/cond/branch_0_fun/row_forward/pallas_call | solution.py:269
  25.4 26.0 %all-to-all-done = bf16[64,8,768]{2,1,0:T(8,128)(2,1)S(1)} async-done(((bf16[64,8,768]{2,1,0:T(8,128)(2,1)}), bf16[64,8,768]{2,1,0:T(8,128)(2,1)S(1)}, u32[]{:S(2)}, u32[]{:S(2)}) %all-to-all-start) | async-done | bytes 786464 | tf_op jit(solution)/shard_map/cond/branch_0_fun/all_to_all | solution.py:281
  51.5 0.0 copy-start.11
  51.5 2.5 %col_forward.1 = bf16[512,640]{1,0:T(8,128)(2,1)S(1)} custom-call(bf16[512,768]{1,0:T(8,128)(2,1)S(1)} %bitcast.20, bf16[512,512]{1,0:T(8,128)(2,1)S(1)} %get-tuple-element.25.bias_ref, bf16[512,256]{1,0:T(8,128)(2,1)S(1)} %copy-done.9, bf16[512,128]{1,0:T(8,128)(2,1)} %get-tuple-element.75.stat_ref), custom_call_target="tpu_custom_call" | custom-call | flops 268435456 | bytes 2359296 | tf_op jit(solution)/shard_map/cond/branch_0_fun/col_forward/pallas_call | solution.py:269
  54.0 0.0 copy-done.11
  54.0 0.0 copy-start.12
  54.0 31.3 %all_to_all.47 = bf16[64,8,640]{2,1,0:T(8,128)(2,1)S(1)} all-to-all(bf16[64,8,640]{2,1,0:T(8,128)(2,1)S(1)} %bitcast.23), channel_id=1, replica_groups=mesh['seq'=64,'tp'=8] {'seq'}, dimensions={0} | all-to-all | bytes 1310720 | tf_op jit(solution)/shard_map/all_to_all | solution.py:281
  85.3 0.0 copy-done.12
  85.3 3.6 %col_backward.1 = bf16[512,768]{1,0:T(8,128)(2,1)} custom-call(bf16[512,768]{1,0:T(8,128)(2,1)S(1)} %copy-done.12, bf16[512,640]{1,0:T(8,128)(2,1)S(1)} %bitcast.15, bf16[512,640]{1,0:T(8,128)(2,1)S(1)} %get-tuple-element.61.sent_ref, bf16[512,512]{1,0:T(8,128)(2,1)} %get-tuple-element.63.bias_t_ref), custom_call_target="tpu_custom_call" | custom-call | flops 671088640 | bytes 3407872 | tf_op jit(solution)/shard_map/col_backward/pallas_call | solution.py:269
  88.9 0.0 copy-start.8
  88.9 8.6 %all-to-all-start.4 = ((bf16[64,8,768]{2,1,0:T(8,128)(2,1)}), bf16[64,8,768]{2,1,0:T(8,128)(2,1)S(1)}, u32[]{:S(2)}, u32[]{:S(2)}) async-start(bf16[64,8,768]{2,1,0:T(8,128)(2,1)} %bitcast.10), calls=%async_computation.4 | async-start | bytes 1572864 | tf_op jit(solution)/shard_map/all_to_all | solution.py:281
  97.5 0.0 copy-done.8
  97.5 0.0 copy-start.1
  97.5 1.2 copy-done.1
  98.7 4.1 %row_merge.1 = (bf16[512,1024]{1,0:T(8,128)(2,1)S(1)}, bf16[512,1024]{1,0:T(8,128)(2,1)}, f32[512,128]{1,0:T(8,128)S(1)}) custom-call(s32[1]{0:T(128)} %bitcast.6.core_ref, f32[512,256]{1,0:T(8,128)} %get-tuple-element.59.out_ref, bf16[512,128]{1,0:T(8,128)(2,1)} %get-tuple-element.60.stat_ref, bf16[512,640]{1,0:T(8,128)(2,1)S(1)} %bitcast.16, ...), custom_call_target="tpu_custom_call" | custom-call | flops 536870912 | bytes 4980740 | tf_op jit(solution)/shard_map/row_merge/pallas_call | solution.py:269
  102.8 0.7 copy-done.6
  103.5 14.3 %collective-permute-start = (bf16[512,1024]{1,0:T(8,128)(2,1)}, bf16[512,1024]{1,0:T(8,128)(2,1)S(1)}, u32[]{:S(2)}, u32[]{:S(2)}) collective-permute-start(bf16[512,1024]{1,0:T(8,128)(2,1)} %get-tuple-element.67), channel_id=1, source_target_pairs={{0,1},{1,0},{2,3},{3,2},{4,5},{5,4},{6,7},{7,6},{8,9},{9,8},{10,11... | collective-permute-start | bytes 3145736 | tf_op jit(solution)/shard_map/ppermute | solution.py:348
  117.9 0.0 copy-start.7
  117.9 2.4 %collective-permute-done.got_ref = bf16[512,1024]{1,0:T(8,128)(2,1)S(1)} collective-permute-done((bf16[512,1024]{1,0:T(8,128)(2,1)}, bf16[512,1024]{1,0:T(8,128)(2,1)S(1)}, u32[]{:S(2)}, u32[]{:S(2)}) %collective-permute-start) | collective-permute-done | bytes 1048608 | tf_op jit(solution)/shard_map/ppermute | solution.py:348
  120.3 0.3 pair_sum.1
  120.6 0.0 copy-start.2
  120.6 0.8 copy-done.2
  121.4 2.5 %collective-permute-start.1 = (bf16[512,256]{1,0:T(8,128)(2,1)S(1)}, bf16[512,256]{1,0:T(8,128)(2,1)S(1)}, u32[]{:S(2)}, u32[]{:S(2)}) collective-permute-start(bf16[512,256]{1,0:T(8,128)(2,1)S(1)} %get-tuple-element.69), channel_id=1, source_target_pairs={{0,2},{1,3},{2,4},{3,5},{4,6},{5,7},{6,0},{7,1},{8,10},{9,11},{10,... | collective-permute-start | bytes 786440 | tf_op jit(solution)/shard_map/ppermute | solution.py:356
  124.0 4.3 %collective-permute-start.2 = (bf16[512,256]{1,0:T(8,128)(2,1)S(1)}, bf16[512,256]{1,0:T(8,128)(2,1)S(1)}, u32[]{:S(2)}, u32[]{:S(2)}) collective-permute-start(bf16[512,256]{1,0:T(8,128)(2,1)S(1)} %get-tuple-element.70), channel_id=1, source_target_pairs={{0,4},{1,5},{2,6},{3,7},{4,0},{5,1},{6,2},{7,3},{8,12},{9,13},{10,... | collective-permute-start | bytes 786440 | tf_op jit(solution)/shard_map/ppermute | solution.py:356
  128.3 1.9 %collective-permute-start.3 = (bf16[512,256]{1,0:T(8,128)(2,1)S(1)}, bf16[512,256]{1,0:T(8,128)(2,1)S(1)}, u32[]{:S(2)}, u32[]{:S(2)}) collective-permute-start(bf16[512,256]{1,0:T(8,128)(2,1)S(1)} %get-tuple-element.71), channel_id=1, source_target_pairs={{0,6},{1,7},{2,0},{3,1},{4,2},{5,3},{6,4},{7,5},{8,14},{9,15},{10,... | collective-permute-start | bytes 786440 | tf_op jit(solution)/shard_map/ppermute | solution.py:356
  130.2 0.0 copy-done.7
  130.2 2.7 %row_backward.1.grad_ref = f32[512,768]{1,0:T(8,128)S(1)} custom-call(bf16[512,256]{1,0:T(8,128)(2,1)} %q_ref.1, bf16[512,256]{1,0:T(8,128)(2,1)} %k_ref.1, bf16[512,256]{1,0:T(8,128)(2,1)} %v_ref.1, bf16[512,256]{1,0:T(8,128)(2,1)} %g_ref.3, f32[512,128]{1,0:T(8,128)S(1)} %copy-done.7), custom_call_target="tpu_custom_call" | custom-call | flops 671088640 | bytes 2883584 | tf_op jit(solution)/shard_map/row_backward/pallas_call | solution.py:269
  132.9 0.0 collective-permute-done.1.p1_ref
  132.9 3.6 %collective-permute-done.2.p2_ref = bf16[512,256]{1,0:T(8,128)(2,1)S(1)} collective-permute-done((bf16[512,256]{1,0:T(8,128)(2,1)S(1)}, bf16[512,256]{1,0:T(8,128)(2,1)S(1)}, u32[]{:S(2)}, u32[]{:S(2)}) %collective-permute-start.2) | collective-permute-done | bytes 262176 | tf_op jit(solution)/shard_map/ppermute | solution.py:356
  136.5 4.7 %collective-permute-done.3.p3_ref = bf16[512,256]{1,0:T(8,128)(2,1)S(1)} collective-permute-done((bf16[512,256]{1,0:T(8,128)(2,1)S(1)}, bf16[512,256]{1,0:T(8,128)(2,1)S(1)}, u32[]{:S(2)}, u32[]{:S(2)}) %collective-permute-start.3) | collective-permute-done | bytes 262176 | tf_op jit(solution)/shard_map/ppermute | solution.py:356
  141.3 0.7 copy-done.4
  142.0 0.0 all-to-all-done.4
  142.0 0.0 copy-done.3
  142.0 0.9 copy-done.5
  142.9 1.1 finish.1
  (5 shorter events, 0.0 us)
Async XLA Ops:
  0.6 0.9 copy-start
  1.5 20.9 %copy-start.9 = (bf16[512,256]{1,0:T(8,128)(2,1)S(1)}, bf16[512,256]{1,0:T(8,128)(2,1)}, u32[]{:S(2)}) copy-start(bf16[512,256]{1,0:T(8,128)(2,1)} %get-tuple-element.23.g_ref) | copy-start | bytes 786436 | tf_op jit(solution)/shard_map/cond
  1.5 20.9 %copy-start.13 = (bf16[512,256]{1,0:T(8,128)(2,1)S(1)}, bf16[512,256]{1,0:T(8,128)(2,1)}, u32[]{:S(2)}) copy-start(bf16[512,256]{1,0:T(8,128)(2,1)} %get-tuple-element.20.q_ref) | copy-start | bytes 786436 | tf_op jit(solution)/shard_map/cond
  1.6 20.9 %copy-start.15 = (bf16[512,256]{1,0:T(8,128)(2,1)S(1)}, bf16[512,256]{1,0:T(8,128)(2,1)}, u32[]{:S(2)}) copy-start(bf16[512,256]{1,0:T(8,128)(2,1)} %get-tuple-element.21.k_ref) | copy-start | bytes 786436 | tf_op jit(solution)/shard_map/cond
  1.6 20.9 %copy-start.17 = (bf16[512,256]{1,0:T(8,128)(2,1)S(1)}, bf16[512,256]{1,0:T(8,128)(2,1)}, u32[]{:S(2)}) copy-start(bf16[512,256]{1,0:T(8,128)(2,1)} %get-tuple-element.22.v_ref) | copy-start | bytes 786436 | tf_op jit(solution)/shard_map/cond
  3.7 47.8 %all-to-all-start = ((bf16[64,8,768]{2,1,0:T(8,128)(2,1)}), bf16[64,8,768]{2,1,0:T(8,128)(2,1)S(1)}, u32[]{:S(2)}, u32[]{:S(2)}) async-start(bf16[64,8,768]{2,1,0:T(8,128)(2,1)} %maximum_bitcast_fusion), calls=%async_computation | async-start | bytes 1572864 | tf_op jit(solution)/shard_map/cond/branch_0_fun/all_to_all | solution.py:281
  51.5 2.5 %copy-start.11 = (bf16[64,8,768]{2,1,0:T(8,128)(2,1)}, bf16[64,8,768]{2,1,0:T(8,128)(2,1)S(1)}, u32[]{:S(2)}) copy-start(bf16[64,8,768]{2,1,0:T(8,128)(2,1)S(1)} %all-to-all-done) | copy-start | bytes 2359300 | tf_op jit(solution)/shard_map/cond
  54.0 31.3 %copy-start.12 = (bf16[512,768]{1,0:T(8,128)(2,1)S(1)}, bf16[512,768]{1,0:T(8,128)(2,1)}, u32[]{:S(2)}) copy-start(bf16[512,768]{1,0:T(8,128)(2,1)} %get-tuple-element.62.y_ref) | copy-start | bytes 2359300
  88.9 8.6 %copy-start.8 = (bf16[512,256]{1,0:T(8,128)(2,1)S(1)}, bf16[512,256]{1,0:T(8,128)(2,1)}, u32[]{:S(2)}) copy-start(bf16[512,256]{1,0:T(8,128)(2,1)} %g_ref.3) | copy-start | bytes 786436
  88.9 53.1 %all-to-all-start.4 = ((bf16[64,8,768]{2,1,0:T(8,128)(2,1)}), bf16[64,8,768]{2,1,0:T(8,128)(2,1)S(1)}, u32[]{:S(2)}, u32[]{:S(2)}) async-start(bf16[64,8,768]{2,1,0:T(8,128)(2,1)} %bitcast.10), calls=%async_computation.4 | async-start | bytes 1572864 | tf_op jit(solution)/shard_map/all_to_all | solution.py:281
  97.5 1.2 copy-start.1
  102.8 0.7 copy-start.6
  103.5 16.8 %collective-permute-start = (bf16[512,1024]{1,0:T(8,128)(2,1)}, bf16[512,1024]{1,0:T(8,128)(2,1)S(1)}, u32[]{:S(2)}, u32[]{:S(2)}) collective-permute-start(bf16[512,1024]{1,0:T(8,128)(2,1)} %get-tuple-element.67), channel_id=1, source_target_pairs={{0,1},{1,0},{2,3},{3,2},{4,5},{5,4},{6,7},{7,6},{8,9},{9,8},{10,11... | collective-permute-start | bytes 3145736 | tf_op jit(solution)/shard_map/ppermute | solution.py:348
  117.9 12.3 %copy-start.7 = (f32[512,128]{1,0:T(8,128)S(1)}, f32[512,128]{1,0:T(8,128)}, u32[]{:S(2)}) copy-start(f32[512,128]{1,0:T(8,128)} %copy-done.6) | copy-start | bytes 786436
  120.6 0.8 copy-start.2
  121.4 20.6 %copy-start.3 = (f32[512,256]{1,0:T(8,128)S(1)}, f32[512,256]{1,0:T(8,128)}, u32[]{:S(2)}) copy-start(f32[512,256]{1,0:T(8,128)} %copy-done.2) | copy-start | bytes 1572868
  121.4 11.5 %collective-permute-start.1 = (bf16[512,256]{1,0:T(8,128)(2,1)S(1)}, bf16[512,256]{1,0:T(8,128)(2,1)S(1)}, u32[]{:S(2)}, u32[]{:S(2)}) collective-permute-start(bf16[512,256]{1,0:T(8,128)(2,1)S(1)} %get-tuple-element.69), channel_id=1, source_target_pairs={{0,2},{1,3},{2,4},{3,5},{4,6},{5,7},{6,0},{7,1},{8,10},{9,11},{10,... | collective-permute-start | bytes 786440 | tf_op jit(solution)/shard_map/ppermute | solution.py:356
  124.0 12.6 %collective-permute-start.2 = (bf16[512,256]{1,0:T(8,128)(2,1)S(1)}, bf16[512,256]{1,0:T(8,128)(2,1)S(1)}, u32[]{:S(2)}, u32[]{:S(2)}) collective-permute-start(bf16[512,256]{1,0:T(8,128)(2,1)S(1)} %get-tuple-element.70), channel_id=1, source_target_pairs={{0,4},{1,5},{2,6},{3,7},{4,0},{5,1},{6,2},{7,3},{8,12},{9,13},{10,... | collective-permute-start | bytes 786440 | tf_op jit(solution)/shard_map/ppermute | solution.py:356
  128.3 13.0 %collective-permute-start.3 = (bf16[512,256]{1,0:T(8,128)(2,1)S(1)}, bf16[512,256]{1,0:T(8,128)(2,1)S(1)}, u32[]{:S(2)}, u32[]{:S(2)}) collective-permute-start(bf16[512,256]{1,0:T(8,128)(2,1)S(1)} %get-tuple-element.71), channel_id=1, source_target_pairs={{0,6},{1,7},{2,0},{3,1},{4,2},{5,3},{6,4},{7,5},{8,14},{9,15},{10,... | collective-permute-start | bytes 786440 | tf_op jit(solution)/shard_map/ppermute | solution.py:356
  141.3 0.7 copy-start.4
  142.0 1.0 copy-start.5

commit v3 on v2

--- a/solution.py
+++ b/solution.py
@@ -55,7 +55,7 @@
     return tile[first : first + 1] + (tile[first + 1 : first + 2] + tile[first + 2 : first + 3])
 
 
-def row_forward(q_ref, k_ref, v_ref, g_ref, mask_ref, out_ref, stat_ref, bias_ref, bias_t_ref):
+def row_forward(q_ref, k_ref, v_ref, g_ref, mask_ref, out_ref, stat_ref, bias_ref):
     heads = q_ref.shape[1] // HEAD_DIM
     for start in range(0, COLS, BLOCK):
         rows = slice(start, start + BLOCK)
@@ -77,6 +77,10 @@
             tile = put_pieces(tile, lanes, 6 * h, m + jnp.log(total))
             tile = put_pieces(tile, lanes, 6 * h + 3, dots)
         stat_ref[rows, :] = tile.astype(bf16)
+    pattern(mask_ref, bias_ref)
+
+
+def pattern(mask_ref, bias_ref, turned=False):
     total_rows = mask_ref.shape[0]
     width = COLS // total_rows
     mask = mask_ref[...].astype(f32).astype(bf16)
@@ -85,20 +89,41 @@
         == lax.broadcasted_iota(jnp.int32, (COLS, total_rows), 1)
     )
     spread = jnp.where(spread, 1.0, 0.0).astype(bf16)
-    first = lax.broadcasted_iota(jnp.int32, (COLS, COLS), 0)
-    second = lax.broadcasted_iota(jnp.int32, (COLS, COLS), 1)
-    same = (first % width) == (second % width)
-    whole = dot_nt(dot_nn(spread, mask).astype(bf16), spread)
-    whole_t = dot_nt(spread, dot_nn(spread, mask).astype(bf16))
-    bias_ref[...] = jnp.where((whole > 0.5) & same & (second < first), 0.0, NEG).astype(bf16)
-    bias_t_ref[...] = jnp.where((whole_t > 0.5) & same & (first < second), 0.0, NEG).astype(bf16)
-
-
-def col_forward_joined(key_ref, rest_ref, bias_ref, g_ref, stat_ref, send_ref, y_ref):
+    query = lax.broadcasted_iota(jnp.int32, (COLS, COLS), int(turned))
+    key = lax.broadcasted_iota(jnp.int32, (COLS, COLS), 1 - int(turned))
+    same = (query % width) == (key % width)
+    rows = dot_nn(spread, mask).astype(bf16)
+    whole = dot_nt(spread, rows) if turned else dot_nt(rows, spread)
+    bias_ref[...] = jnp.where((whole > 0.5) & same & (key < query), 0.0, NEG).astype(bf16)
+
+
+def pattern_turned(mask_ref, *refs):
+    *_, bias_ref = refs
+    pattern(mask_ref, bias_ref, turned=True)
+
+
+def pack(pieces, refs):
+    *ins, out_ref, sems = refs
+    copies = []
+    at = 0
+    for n, (ref, (first, width)) in enumerate(zip(ins, pieces)):
+        copies.append(
+            pltpu.make_async_copy(
+                ref.at[:, first : first + width], out_ref.at[:, at : at + width], sems.at[n]
+            )
+        )
+        at += width
+    for copy in copies:
+        copy.start()
+    for copy in copies:
+        copy.wait()
+
+
+def col_forward_joined(first_ref, rest_ref, bias_ref, g_ref, stat_ref, send_ref, y_ref):
     features = g_ref.shape[1]
     y_ref[:, :features] = rest_ref[:, :features]
-    y_ref[:, features : 2 * features] = key_ref[...]
-    y_ref[:, 2 * features :] = rest_ref[:, features:]
+    y_ref[:, features : features + HEAD_DIM] = first_ref[...]
+    y_ref[:, features + HEAD_DIM :] = rest_ref[:, features:]
     col_forward(y_ref, bias_ref, g_ref, stat_ref, send_ref)
 
 
@@ -110,7 +135,7 @@
         rows = slice(start, start + BLOCK)
         keys = slice(0, start + BLOCK)
         lanes = lanes_like(BLOCK)
-        tile = stat_ref[rows, :].astype(f32)
+        tile = jnp.zeros((BLOCK, 128), f32)
         for h in range(heads):
             q = y_ref[rows, head(h)]
             k = y_ref[keys, head(heads + h)]
@@ -122,6 +147,7 @@
             out = dot_nn(p.astype(bf16), v) / total
             send_ref[rows, head(heads + h)] = out.astype(bf16)
             tile = put_pieces(tile, lanes, CSTAT + 3 * h, m + jnp.log(total))
+        tile = jnp.where(lanes < CSTAT, stat_ref[rows, :].astype(f32), tile)
         send_ref[rows, 2 * features :] = tile.astype(bf16)
 
 
@@ -182,14 +208,14 @@
     out_ref[:, head(h)] = grad_q.astype(kind)
 
 
-def row_merge(core_ref, out_ref, stat_ref, got_ref, g_ref, weight_ref, keep_ref, give_ref, merged_ref):
+def row_merge(core_ref, out_ref, sent_ref, got_ref, g_ref, weight_ref, att_ref, give_ref, merged_ref):
     features = g_ref.shape[1]
     heads = features // HEAD_DIM
     lanes = lanes_like(COLS)
-    row_tile = stat_ref[...].astype(f32)
     col_tile = got_ref[:, 2 * features :].astype(f32)
     merged = jnp.zeros((COLS, 128), f32)
     parts = []
+    row_tile = sent_ref[:, 2 * features :].astype(f32)
     for h in range(heads):
         row_lse = take_lanes(row_tile, 6 * h)
         col_lse = take_lanes(col_tile, CSTAT + 3 * h)
@@ -206,12 +232,19 @@
         merged = jnp.where(lanes == 2 * h, top + jnp.log(both), merged)
         merged = jnp.where(lanes == 2 * h + 1, dots, merged)
     merged_ref[...] = merged
-    att = jnp.concatenate(parts, axis=1)
-    core = core_ref[0]
+    att_ref[...] = jnp.concatenate(parts, axis=1)
+    project(1 - core_ref[0], att_ref, weight_ref, give_ref)
+
+
+def project(core, att_ref, weight_ref, part_ref):
+    features = att_ref.shape[1]
     for n in range(weight_ref.shape[1] // (2 * features)):
-        for ref, side in ((keep_ref, core), (give_ref, 1 - core)):
-            at = pl.ds(pl.multiple_of((2 * n + side) * features, 128), features)
-            ref[:, n * features : (n + 1) * features] = dot_nn(att, weight_ref[:, at]).astype(bf16)
+        at = pl.ds(pl.multiple_of((2 * n + core) * features, 128), features)
+        part_ref[:, n * features : (n + 1) * features] = dot_nn(att_ref[...], weight_ref[:, at]).astype(bf16)
+
+
+def project_own(core_ref, att_ref, weight_ref, part_ref):
+    project(core_ref[0], att_ref, weight_ref, part_ref)
 
 
 def pair_sum(x_ref, keep_ref, got_ref, own_ref, *send_refs):
@@ -221,6 +254,14 @@
         chip = lax.rem(x_ref[0] + n, count)
         at = pl.ds(pl.multiple_of(chip * features, 128), features)
         ref[...] = (keep_ref[:, at].astype(f32) + got_ref[:, at].astype(f32)).astype(ref.dtype)
+
+
+def project_sum(own_ref, *refs):
+    *part_refs, out_ref = refs
+    total = own_ref[...]
+    for ref in part_refs:
+        total = total + ref[...].astype(f32)
+    out_ref[...] = total.astype(bf16)
 
 
 def row_backward(q_ref, k_ref, v_ref, g_ref, merged_ref, grad_ref):
@@ -249,31 +290,29 @@
         )
 
 
-def finish(grad_ref, back_ref, own_ref, p1_ref, p2_ref, p3_ref, projected_ref, q_ref, k_ref, v_ref):
+def finish(grad_ref, back_ref, q_ref, k_ref, v_ref):
     features = q_ref.shape[1]
     for n, ref in enumerate((q_ref, k_ref, v_ref)):
         at = slice(n * features, (n + 1) * features)
         ref[...] = (grad_ref[:, at] + back_ref[:, at].astype(f32)).astype(bf16)
-    total = own_ref[...]
-    for ref in (p1_ref, p2_ref, p3_ref):
-        total = total + ref[...].astype(f32)
-    projected_ref[...] = total.astype(bf16)
-
-
-def call(kernel, outs, cost, *args):
+
+
+def call(kernel, outs, cost, *args, far=(), far_out=(), scratch=(), room=16):
     vmem = pl.BlockSpec(memory_space=pltpu.VMEM)
     smem = pl.BlockSpec(memory_space=pltpu.SMEM)
+    hbm = pl.BlockSpec(memory_space=pltpu.HBM)
     flops, exps = cost
     moved = sum(a.size * a.dtype.itemsize for a in args)
     moved += sum(o.size * o.dtype.itemsize for o in outs)
     return pl.pallas_call(
         kernel,
         out_shape=outs,
-        in_specs=[smem if a.ndim == 1 else vmem for a in args],
-        out_specs=[vmem] * len(outs),
+        in_specs=[smem if a.ndim == 1 else hbm if n in far else vmem for n, a in enumerate(args)],
+        out_specs=[hbm if n in far_out else vmem for n in range(len(outs))],
+        scratch_shapes=scratch,
         cost_estimate=pl.CostEstimate(flops=flops, bytes_accessed=moved, transcendentals=exps),
-        compiler_params=pltpu.CompilerParams(vmem_limit_bytes=16 * 1024 * 1024),
-        name=kernel.__name__,
+        compiler_params=pltpu.CompilerParams(vmem_limit_bytes=room * 1024 * 1024),
+        name=getattr(kernel, "__name__", "pack"),
     )(*args)
 
 
@@ -296,73 +335,99 @@
     def forward(queries, key_vectors, value_vectors, attn_grad, mask):
         return call(
             row_forward,
-            [arr(features, f32), arr(128, bf16), arr(COLS, bf16), arr(COLS, bf16)],
+            [arr(features, f32), arr(128, bf16), arr(COLS, bf16)],
             (2 * product, exps),
             queries, key_vectors, value_vectors, attn_grad, mask,
         )
 
+
+    def packed(*pieces):
+        def kernel(*refs):
+            pack([p[1:] for p in pieces], refs)
+
+        return call(
+            kernel,
+            [arr(sum(p[2] for p in pieces), bf16)],
+            (0, 0),
+            *[p[0] for p in pieces],
+            far=range(len(pieces)),
+            scratch=[pltpu.SemaphoreType.DMA((len(pieces),))],
+        )[0]
+
     def at_once(queries, key_vectors, value_vectors, attn_grad, mask):
-        qkv = exchange(jnp.concatenate([queries, key_vectors, value_vectors], axis=1))
-        row_out, row_stat, bias, bias_t = forward(queries, key_vectors, value_vectors, attn_grad, mask)
+        qkv = exchange(
+            packed((queries, 0, features), (key_vectors, 0, features), (value_vectors, 0, features))
+        )
+        row_out, row_stat, bias = forward(queries, key_vectors, value_vectors, attn_grad, mask)
         (sent,) = call(
             col_forward,
             [arr(2 * features + 128, bf16)],
             (2 * product, exps),
             qkv, bias, attn_grad, row_stat,
         )
-        return qkv, sent, row_out, row_stat, bias_t
+        return qkv, sent, row_out
 
     def in_two(queries, key_vectors, value_vectors, attn_grad, mask):
-        keys = exchange(key_vectors)
-        row_out, row_stat, bias, bias_t = forward(queries, key_vectors, value_vectors, attn_grad, mask)
-        rest, keys = lax.optimization_barrier((jnp.concatenate([queries, value_vectors], axis=1), keys))
+        first = exchange(packed((key_vectors, 0, HEAD_DIM)))
+        row_out, row_stat, bias = forward(queries, key_vectors, value_vectors, attn_grad, mask)
+        rest = packed(
+            (queries, 0, features),
+            (key_vectors, HEAD_DIM, features - HEAD_DIM),
+            (value_vectors, 0, features),
+        )
+        rest, first = lax.optimization_barrier((rest, first))
         rest = exchange(rest)
         sent, qkv = call(
             col_forward_joined,
             [arr(2 * features + 128, bf16), arr(3 * features, bf16)],
             (2 * product, exps),
-            keys, rest, bias, attn_grad, row_stat,
-        )
-        return qkv, sent, row_out, row_stat, bias_t
+            first, rest, bias, attn_grad, row_stat,
+        )
+        return qkv, sent, row_out
 
     place = lax.axis_index("tp")
     core = lax.rem(place, 2)
-    qkv, sent, row_out, row_stat, bias_t = lax.cond(
+    qkv, sent, row_out = lax.cond(
         core == 1, in_two, at_once, queries, key_vectors, value_vectors, attn_grad, mask
     )
     got = exchange(sent)
+    (bias_t,) = call(pattern_turned, [arr(COLS, bf16)], (2 * tokens * tokens * 64, 0), mask, out_weight, row_out, qkv, sent)
     (col_grads,) = call(
         col_backward, [arr(3 * features, bf16)], (5 * product, exps), qkv, got, sent, bias_t
     )
     back = exchange(col_grads)
     got, col_grads = lax.optimization_barrier((got, col_grads))
     half = out_weight.shape[1] // 2
-    keep, give, merged = call(
+    att, give, merged = call(
         row_merge,
-        [arr(half, bf16), arr(half, bf16), arr(128, f32)],
-        (2 * tokens * features * out_weight.shape[1], tokens),
-        core.reshape(1), row_out, row_stat, got, attn_grad, out_weight,
+        [arr(features, bf16), arr(half, bf16), arr(128, f32)],
+        (2 * tokens * features * half, tokens),
+        core.reshape(1), row_out, sent, got, attn_grad, out_weight,
     )
     count = lax.axis_size("tp")
     chips = count // 2
     pair = lax.ppermute(give, "tp", [(t, t ^ 1) for t in range(count)])
+    (keep,) = call(
+        project_own, [arr(half, bf16)], (2 * tokens * features * half, 0), core.reshape(1), att, out_weight
+    )
     own, *sends = call(
         pair_sum,
         [arr(features, f32)] + [arr(features, bf16)] * (chips - 1),
         (tokens * half, 0),
         (place // 2).reshape(1), keep, pair,
     )
+    far_first = sorted(range(1, chips), key=lambda n: -min(n, chips - n))
     parts = [
-        lax.ppermute(x, "tp", [(t, (t + 2 * n) % count) for t in range(count)])
-        for n, x in enumerate(sends, 1)
+        lax.ppermute(sends[n - 1], "tp", [(t, (t + 2 * n) % count) for t in range(count)])
+        for n in far_first
     ]
     (row_grads,) = call(
         row_backward, [arr(3 * features, f32)], (5 * product, exps),
         queries, key_vectors, value_vectors, attn_grad, merged,
     )
-    return tuple(
-        call(finish, [arr(features, bf16)] * 4, (6 * tokens * features, 0), row_grads, back, own, *parts)
-    )
+    (projected,) = call(project_sum, [arr(features, bf16)], (4 * tokens * features, 0), own, *parts)
+    grads = call(finish, [arr(features, bf16)] * 3, (3 * tokens * features, 0), row_grads, back)
+    return (projected, *grads)
 
 
 def solution(mesh):

time: 146 us -> 141 us (0.966)
  blocking collectives: 31.3 us -> 0 us
  waiting for transfers between devices: 36.8 us -> 57.5 us
  starting transfers between devices: 50.4 us -> 58.6 us
  local copies, waits for them, and re-layouts: 5.29 us -> 0.93 us
  Pallas kernels: 17.3 us -> 21.5 us
  other arithmetic: 2.13 us -> 0 us
    all_to_all x1 -> x0, blocking collectives: 31.3 us -> none  [exchange(): return lax.all_to_all(x, 'seq', split_axis=0, concat_axis=0, tiled=True)]
    all_to_all x2 -> x3, waiting for transfers between devices: 26 us -> 47.8 us  [exchange(): return lax.all_to_all(x, 'seq', split_axis=0, concat_axis=0, tiled=True)]
    all_to_all x2 -> x3, starting transfers between devices: 27.3 us -> 33.5 us  [exchange(): return lax.all_to_all(x, 'seq', split_axis=0, concat_axis=0, tiled=True)]
    unnamed x20 -> x12, local copies, waits for them, and re-layouts: 5.26 us -> 0.91 us
    pallas_call x7 -> x11, Pallas kernels: 17.3 us -> 21.5 us  [call(): pl.pallas_call(kernel, out_shape=outs, in_specs=[smem if a.ndim == 1 else...]
    all_to_all x1 -> x0, other arithmetic: 2.13 us -> none  [exchange(): return lax.all_to_all(x, 'seq', split_axis=0, concat_axis=0, tiled=True)]
    ppermute x1, starting transfers between devices: 14.3 us -> 15.9 us  [local(): pair = lax.ppermute(give, 'tp', [(t, t ^ 1) for t in range(count)])]
  transfers between devices with their start and end apart: 6 -> 7, of which waited for: 4 -> 6; matrix products, arithmetic and copies ran while one was open for 0% -> 0% of each run, Pallas kernels for 7% -> 9%
where the time goes in v3:
time: 141 us; the launch traced here: 139 us
  starting transfers between devices  58.6 us (42%)
  waiting for transfers between devices  57.5 us (41%)
  Pallas kernels  21.5 us (15%)
    all_to_all x3, waiting for transfers between devices, exchange(): return lax.all_to_all(x, 'seq', split_axis=0, concat_axis=0, tiled=True)  47.8 us
    all_to_all x3, starting transfers between devices, exchange(): return lax.all_to_all(x, 'seq', split_axis=0, concat_axis=0, tiled=True)  33.5 us
    pallas_call x11, Pallas kernels, call(): pl.pallas_call(kernel, out_shape=outs, in_specs=[smem if a.ndim == 1 else...  21.5 us
    ppermute x1, starting transfers between devices, local(): pair = lax.ppermute(give, 'tp', [(t, t ^ 1) for t in range(count)])  15.9 us
    ppermute x3, starting transfers between devices, local(): lax.ppermute(sends[n - 1], 'tp', [(t, (t + 2 * n) % count) for t in range...  9.26 us
    ppermute x3, waiting for transfers between devices, local(): lax.ppermute(sends[n - 1], 'tp', [(t, (t + 2 * n) % count) for t in range...  7.62 us
  transfers between devices with their start and end apart: 7, of which 6 were waited for; matrix products, arithmetic and copies ran while one was open for 0% of the time, Pallas kernels for 9%

profile of v3, /device:TPU:6, one launch (start us, length us, event | category | flops | bytes accessed | tf_op | source)
XLA Modules:
  0.0 139.5 jit_solution(9756960426919029739)
XLA Ops:
  0.6 0.0 copy-start
  0.7 0.9 copy-done
  1.5 51.3 %conditional.1 = (bf16[512,768]{1,0:T(8,128)(2,1)S(1)}, bf16[512,640]{1,0:T(8,128)(2,1)}, f32[512,256]{1,0:T(8,128)}) conditional(s32[]{:T(128)} %convert_element_type.3, (bf16[512,256]{1,0:T(8,128)(2,1)}, bf16[512,256]{1,0:T(8,128)(2,1)}, bf16[512,256]{1,0:T(8,128)(2,1)}, bf16[512,256]{1,0:T(8,128)(2,1)}, s32[64,64]{1,0:T(8,128)S(1)}) %tuple.18, ...), branch_computations={%region_0.1_spmd, %region_1.2_spmd} | conditional | flops 536870912 | bytes 13779144 | solution.py:390
  1.5 0.0 copy-start.3
  1.5 0.0 copy-start.6
  1.6 0.0 copy-start.9
  1.6 0.0 copy-start.12
  1.6 2.1 %kernel.3 = bf16[512,768]{1,0:T(8,128)(2,1)} custom-call(bf16[512,256]{1,0:T(8,128)(2,1)} %get-tuple-element.20.refs_0_.q_ref, bf16[512,256]{1,0:T(8,128)(2,1)} %get-tuple-element.21.refs_1_.k_ref, bf16[512,256]{1,0:T(8,128)(2,1)} %get-tuple-element.22.refs_2_.v_ref), custom_call_target="tpu_custom_call" | custom-call | bytes 1572864 | tf_op jit(solution)/shard_map/cond/branch_0_fun/kernel/pallas_call | solution.py:307
  3.7 18.7 %all-to-all-start = ((bf16[64,8,768]{2,1,0:T(8,128)(2,1)}), bf16[64,8,768]{2,1,0:T(8,128)(2,1)S(1)}, u32[]{:S(2)}, u32[]{:S(2)}) async-start(bf16[64,8,768]{2,1,0:T(8,128)(2,1)} %bitcast), calls=%async_computation | async-start | bytes 1572864 | tf_op jit(solution)/shard_map/cond/branch_0_fun/all_to_all | solution.py:320
  22.5 0.0 copy-done.3
  22.5 0.0 copy-done.6
  22.5 0.0 copy-done.9
  22.5 0.0 copy-done.12
  22.5 2.5 %row_forward.2 = (f32[512,256]{1,0:T(8,128)}, bf16[512,128]{1,0:T(8,128)(2,1)S(1)}, bf16[512,512]{1,0:T(8,128)(2,1)S(1)}) custom-call(bf16[512,256]{1,0:T(8,128)(2,1)S(1)} %copy-done.9, bf16[512,256]{1,0:T(8,128)(2,1)S(1)} %copy-done.3, bf16[512,256]{1,0:T(8,128)(2,1)S(1)} %copy-done.12, bf16[512,256]{1,0:T(8,128)(2,1)S(1)} %copy-done.6, ...), custom_call_target="tpu_custom_call" | custom-call | flops 268435456 | bytes 2244608 | tf_op jit(solution)/shard_map/cond/branch_0_fun/row_forward/pallas_call | solution.py:307
  25.0 25.5 %all-to-all-done = bf16[64,8,768]{2,1,0:T(8,128)(2,1)S(1)} async-done(((bf16[64,8,768]{2,1,0:T(8,128)(2,1)}), bf16[64,8,768]{2,1,0:T(8,128)(2,1)S(1)}, u32[]{:S(2)}, u32[]{:S(2)}) %all-to-all-start) | async-done | bytes 786464 | tf_op jit(solution)/shard_map/cond/branch_0_fun/all_to_all | solution.py:320
  50.5 2.3 %col_forward.1 = bf16[512,640]{1,0:T(8,128)(2,1)} custom-call(bf16[512,768]{1,0:T(8,128)(2,1)S(1)} %bitcast.19, bf16[512,512]{1,0:T(8,128)(2,1)S(1)} %get-tuple-element.25.bias_ref, bf16[512,256]{1,0:T(8,128)(2,1)S(1)} %copy-done.6, bf16[512,128]{1,0:T(8,128)(2,1)S(1)} %get-tuple-element.26.stat_ref), custom_call_target="tpu_custom_call" | custom-call | flops 268435456 | bytes 2359296 | tf_op jit(solution)/shard_map/cond/branch_0_fun/col_forward/pallas_call | solution.py:307
  52.8 0.0 copy-start.1
  52.8 7.3 %all-to-all-start.3 = ((bf16[64,8,640]{2,1,0:T(8,128)(2,1)}), bf16[64,8,640]{2,1,0:T(8,128)(2,1)S(1)}, u32[]{:S(2)}, u32[]{:S(2)}) async-start(bf16[64,8,640]{2,1,0:T(8,128)(2,1)} %bitcast.9), calls=%async_computation.3 | async-start | bytes 1310720 | tf_op jit(solution)/shard_map/all_to_all | solution.py:320
  60.2 0.0 copy-done.1
  60.2 1.7 %pattern_turned.1.bias_t_ref = bf16[512,512]{1,0:T(8,128)(2,1)S(1)} custom-call(s32[64,64]{1,0:T(8,128)S(1)} %dynamic-slice_bitcast_fusion.mask_ref, bf16[256,2048]{1,0:T(8,128)(2,1)S(1)} %copy-done.1, f32[512,256]{1,0:T(8,128)} %get-tuple-element.58.refs_1_.out_ref, bf16[512,768]{1,0:T(8,128)(2,1)S(1)} %get-tuple-element.60.refs_2_.y_ref, ...), custom_call_target="tpu_custom_call" | custom-call | flops 33554432 | bytes 3555328 | tf_op jit(solution)/shard_map/pattern_turned/pallas_call | solution.py:307
  61.9 22.3 %all-to-all-done.3 = bf16[64,8,640]{2,1,0:T(8,128)(2,1)S(1)} async-done(((bf16[64,8,640]{2,1,0:T(8,128)(2,1)}), bf16[64,8,640]{2,1,0:T(8,128)(2,1)S(1)}, u32[]{:S(2)}, u32[]{:S(2)}) %all-to-all-start.3) | async-done | bytes 655392 | tf_op jit(solution)/shard_map/all_to_all | solution.py:320
  84.2 3.6 %col_backward.1 = bf16[512,768]{1,0:T(8,128)(2,1)} custom-call(bf16[512,768]{1,0:T(8,128)(2,1)S(1)} %get-tuple-element.60.refs_2_.y_ref, bf16[512,640]{1,0:T(8,128)(2,1)S(1)} %bitcast.14, bf16[512,640]{1,0:T(8,128)(2,1)} %get-tuple-element.59.refs_3_.sent_ref, bf16[512,512]{1,0:T(8,128)(2,1)S(1)} %pattern_turned.1.bias_t_ref), custom_call_target="tpu_custom_call" | custom-call | flops 671088640 | bytes 3407872 | tf_op jit(solution)/shard_map/col_backward/pallas_call | solution.py:307
  87.8 0.0 copy-start.5
  87.8 7.4 %all-to-all-start.4 = ((bf16[64,8,768]{2,1,0:T(8,128)(2,1)}), bf16[64,8,768]{2,1,0:T(8,128)(2,1)S(1)}, u32[]{:S(2)}, u32[]{:S(2)}) async-start(bf16[64,8,768]{2,1,0:T(8,128)(2,1)} %bitcast.11), calls=%async_computation.4 | async-start | bytes 1572864 | tf_op jit(solution)/shard_map/all_to_all | solution.py:320
  95.3 0.0 copy-done.5
  95.3 3.9 %row_merge.1 = (bf16[512,256]{1,0:T(8,128)(2,1)S(1)}, bf16[512,1024]{1,0:T(8,128)(2,1)}, f32[512,128]{1,0:T(8,128)S(1)}) custom-call(s32[1]{0:T(128)} %bitcast.7.core_ref, f32[512,256]{1,0:T(8,128)} %get-tuple-element.58.refs_1_.out_ref, bf16[512,640]{1,0:T(8,128)(2,1)} %get-tuple-element.59.refs_3_.sent_ref, bf16[512,640]{1,0:T(8,128)(2,1)S(1)} %bitcast.15, ...), custom_call_target="tpu_custom_call" | custom-call | flops 268435456 | bytes 4718596 | tf_op jit(solution)/shard_map/row_merge/pallas_call | solution.py:307
  99.2 15.9 %collective-permute-start = (bf16[512,1024]{1,0:T(8,128)(2,1)}, bf16[512,1024]{1,0:T(8,128)(2,1)}, u32[]{:S(2)}, u32[]{:S(2)}) collective-permute-start(bf16[512,1024]{1,0:T(8,128)(2,1)} %get-tuple-element.63), channel_id=1, source_target_pairs={{0,1},{1,0},{2,3},{3,2},{4,5},{5,4},{6,7},{7,6},{8,9},{9,8},{10,11... | collective-permute-start | bytes 3145736 | tf_op jit(solution)/shard_map/ppermute | solution.py:409
  115.1 0.5 project_own.1.keep_ref
  115.6 0.0 copy-start.2
  115.6 0.0 copy-start.8
  115.6 0.0 copy-start.11
  115.6 2.1 %collective-permute-done.got_ref = bf16[512,1024]{1,0:T(8,128)(2,1)} collective-permute-done((bf16[512,1024]{1,0:T(8,128)(2,1)}, bf16[512,1024]{1,0:T(8,128)(2,1)}, u32[]{:S(2)}, u32[]{:S(2)}) %collective-permute-start) | collective-permute-done | bytes 1048608 | tf_op jit(solution)/shard_map/ppermute | solution.py:409
  117.7 1.5 %pair_sum.1 = (f32[512,256]{1,0:T(8,128)S(1)}, bf16[512,256]{1,0:T(8,128)(2,1)S(1)}, bf16[512,256]{1,0:T(8,128)(2,1)S(1)}, bf16[512,256]{1,0:T(8,128)(2,1)S(1)}) custom-call(s32[1]{0:T(128)} %bitcast.6.x_ref, bf16[512,1024]{1,0:T(8,128)(2,1)S(1)} %project_own.1.keep_ref, bf16[512,1024]{1,0:T(8,128)(2,1)} %collective-permute-done.got_ref), custom_call_target="tpu_custom_call" | custom-call | flops 524288 | bytes 3407876 | tf_op jit(solution)/shard_map/pair_sum/pallas_call | solution.py:307
  119.2 3.3 %collective-permute-start.1 = (bf16[512,256]{1,0:T(8,128)(2,1)S(1)}, bf16[512,256]{1,0:T(8,128)(2,1)S(1)}, u32[]{:S(2)}, u32[]{:S(2)}) collective-permute-start(bf16[512,256]{1,0:T(8,128)(2,1)S(1)} %get-tuple-element.65), channel_id=1, source_target_pairs={{0,4},{1,5},{2,6},{3,7},{4,0},{5,1},{6,2},{7,3},{8,12},{9,13},{10,... | collective-permute-start | bytes 786440 | tf_op jit(solution)/shard_map/ppermute | solution.py:421
  122.5 4.0 %collective-permute-start.2 = (bf16[512,256]{1,0:T(8,128)(2,1)S(1)}, bf16[512,256]{1,0:T(8,128)(2,1)S(1)}, u32[]{:S(2)}, u32[]{:S(2)}) collective-permute-start(bf16[512,256]{1,0:T(8,128)(2,1)S(1)} %get-tuple-element.66), channel_id=1, source_target_pairs={{0,2},{1,3},{2,4},{3,5},{4,6},{5,7},{6,0},{7,1},{8,10},{9,11},{10,... | collective-permute-start | bytes 786440 | tf_op jit(solution)/shard_map/ppermute | solution.py:421
  126.5 1.9 %collective-permute-start.3 = (bf16[512,256]{1,0:T(8,128)(2,1)S(1)}, bf16[512,256]{1,0:T(8,128)(2,1)S(1)}, u32[]{:S(2)}, u32[]{:S(2)}) collective-permute-start(bf16[512,256]{1,0:T(8,128)(2,1)S(1)} %get-tuple-element.67), channel_id=1, source_target_pairs={{0,6},{1,7},{2,0},{3,1},{4,2},{5,3},{6,4},{7,5},{8,14},{9,15},{10,... | collective-permute-start | bytes 786440 | tf_op jit(solution)/shard_map/ppermute | solution.py:421
  128.5 0.0 copy-done.2
  128.5 0.0 copy-done.8
  128.5 0.0 copy-done.11
  128.5 1.5 %row_backward.1.grad_ref = f32[512,768]{1,0:T(8,128)S(1)} custom-call(bf16[512,256]{1,0:T(8,128)(2,1)S(1)} %copy-done.8, bf16[512,256]{1,0:T(8,128)(2,1)S(1)} %copy-done.2, bf16[512,256]{1,0:T(8,128)(2,1)S(1)} %copy-done.11, bf16[512,256]{1,0:T(8,128)(2,1)S(1)} %copy-done.5, f32[512,128]{1,0:T(8,128)S(1)} %get-tuple-element.68.merged_ref), custom_call_target="tpu_custom_call" | custom-call | flops 671088640 | bytes 2883584 | tf_op jit(solution)/shard_map/row_backward/pallas_call | solution.py:307
  130.0 1.4 collective-permute-done.1.refs_0_
  131.4 3.2 %collective-permute-done.2.refs_1_ = bf16[512,256]{1,0:T(8,128)(2,1)S(1)} collective-permute-done((bf16[512,256]{1,0:T(8,128)(2,1)S(1)}, bf16[512,256]{1,0:T(8,128)(2,1)S(1)}, u32[]{:S(2)}, u32[]{:S(2)}) %collective-permute-start.2) | collective-permute-done | bytes 262176 | tf_op jit(solution)/shard_map/ppermute | solution.py:421
  134.6 3.1 %collective-permute-done.3.refs_2_ = bf16[512,256]{1,0:T(8,128)(2,1)S(1)} collective-permute-done((bf16[512,256]{1,0:T(8,128)(2,1)S(1)}, bf16[512,256]{1,0:T(8,128)(2,1)S(1)}, u32[]{:S(2)}, u32[]{:S(2)}) %collective-permute-start.3) | collective-permute-done | bytes 262176 | tf_op jit(solution)/shard_map/ppermute | solution.py:421
  137.7 0.8 project_sum.1
  138.5 0.0 all-to-all-done.4
  138.5 1.0 finish.1
  (1 shorter events, 0.0 us)
Async XLA Ops:
  0.6 0.9 copy-start
  1.5 20.9 %copy-start.3 = (bf16[512,256]{1,0:T(8,128)(2,1)S(1)}, bf16[512,256]{1,0:T(8,128)(2,1)}, u32[]{:S(2)}) copy-start(bf16[512,256]{1,0:T(8,128)(2,1)} %get-tuple-element.21.refs_1_.k_ref) | copy-start | bytes 786436 | tf_op jit(solution)/shard_map/cond
  1.5 20.9 %copy-start.6 = (bf16[512,256]{1,0:T(8,128)(2,1)S(1)}, bf16[512,256]{1,0:T(8,128)(2,1)}, u32[]{:S(2)}) copy-start(bf16[512,256]{1,0:T(8,128)(2,1)} %get-tuple-element.23.g_ref) | copy-start | bytes 786436 | tf_op jit(solution)/shard_map/cond
  1.6 20.9 %copy-start.9 = (bf16[512,256]{1,0:T(8,128)(2,1)S(1)}, bf16[512,256]{1,0:T(8,128)(2,1)}, u32[]{:S(2)}) copy-start(bf16[512,256]{1,0:T(8,128)(2,1)} %get-tuple-element.20.refs_0_.q_ref) | copy-start | bytes 786436 | tf_op jit(solution)/shard_map/cond
  1.6 20.9 %copy-start.12 = (bf16[512,256]{1,0:T(8,128)(2,1)S(1)}, bf16[512,256]{1,0:T(8,128)(2,1)}, u32[]{:S(2)}) copy-start(bf16[512,256]{1,0:T(8,128)(2,1)} %get-tuple-element.22.refs_2_.v_ref) | copy-start | bytes 786436 | tf_op jit(solution)/shard_map/cond
  3.7 46.8 %all-to-all-start = ((bf16[64,8,768]{2,1,0:T(8,128)(2,1)}), bf16[64,8,768]{2,1,0:T(8,128)(2,1)S(1)}, u32[]{:S(2)}, u32[]{:S(2)}) async-start(bf16[64,8,768]{2,1,0:T(8,128)(2,1)} %bitcast), calls=%async_computation | async-start | bytes 1572864 | tf_op jit(solution)/shard_map/cond/branch_0_fun/all_to_all | solution.py:320
  52.8 7.3 %copy-start.1 = (bf16[256,2048]{1,0:T(8,128)(2,1)S(1)}, bf16[256,2048]{1,0:T(8,128)(2,1)}, u32[]{:S(2)}) copy-start(bf16[256,2048]{1,0:T(8,128)(2,1)} %weight_ref.3) | copy-start | bytes 3145732
  52.8 31.4 %all-to-all-start.3 = ((bf16[64,8,640]{2,1,0:T(8,128)(2,1)}), bf16[64,8,640]{2,1,0:T(8,128)(2,1)S(1)}, u32[]{:S(2)}, u32[]{:S(2)}) async-start(bf16[64,8,640]{2,1,0:T(8,128)(2,1)} %bitcast.9), calls=%async_computation.3 | async-start | bytes 1310720 | tf_op jit(solution)/shard_map/all_to_all | solution.py:320
  87.8 7.4 %copy-start.5 = (bf16[512,256]{1,0:T(8,128)(2,1)S(1)}, bf16[512,256]{1,0:T(8,128)(2,1)}, u32[]{:S(2)}) copy-start(bf16[512,256]{1,0:T(8,128)(2,1)} %g_ref.3) | copy-start | bytes 786436
  87.8 50.7 %all-to-all-start.4 = ((bf16[64,8,768]{2,1,0:T(8,128)(2,1)}), bf16[64,8,768]{2,1,0:T(8,128)(2,1)S(1)}, u32[]{:S(2)}, u32[]{:S(2)}) async-start(bf16[64,8,768]{2,1,0:T(8,128)(2,1)} %bitcast.11), calls=%async_computation.4 | async-start | bytes 1572864 | tf_op jit(solution)/shard_map/all_to_all | solution.py:320
  99.2 18.5 %collective-permute-start = (bf16[512,1024]{1,0:T(8,128)(2,1)}, bf16[512,1024]{1,0:T(8,128)(2,1)}, u32[]{:S(2)}, u32[]{:S(2)}) collective-permute-start(bf16[512,1024]{1,0:T(8,128)(2,1)} %get-tuple-element.63), channel_id=1, source_target_pairs={{0,1},{1,0},{2,3},{3,2},{4,5},{5,4},{6,7},{7,6},{8,9},{9,8},{10,11... | collective-permute-start | bytes 3145736 | tf_op jit(solution)/shard_map/ppermute | solution.py:409
  115.6 12.9 %copy-start.2 = (bf16[512,256]{1,0:T(8,128)(2,1)S(1)}, bf16[512,256]{1,0:T(8,128)(2,1)}, u32[]{:S(2)}) copy-start(bf16[512,256]{1,0:T(8,128)(2,1)} %k_ref.1) | copy-start | bytes 786436
  115.6 12.9 %copy-start.8 = (bf16[512,256]{1,0:T(8,128)(2,1)S(1)}, bf16[512,256]{1,0:T(8,128)(2,1)}, u32[]{:S(2)}) copy-start(bf16[512,256]{1,0:T(8,128)(2,1)} %q_ref.1) | copy-start | bytes 786436
  115.6 12.9 %copy-start.11 = (bf16[512,256]{1,0:T(8,128)(2,1)S(1)}, bf16[512,256]{1,0:T(8,128)(2,1)}, u32[]{:S(2)}) copy-start(bf16[512,256]{1,0:T(8,128)(2,1)} %v_ref.1) | copy-start | bytes 786436
  119.2 12.2 %collective-permute-start.1 = (bf16[512,256]{1,0:T(8,128)(2,1)S(1)}, bf16[512,256]{1,0:T(8,128)(2,1)S(1)}, u32[]{:S(2)}, u32[]{:S(2)}) collective-permute-start(bf16[512,256]{1,0:T(8,128)(2,1)S(1)} %get-tuple-element.65), channel_id=1, source_target_pairs={{0,4},{1,5},{2,6},{3,7},{4,0},{5,1},{6,2},{7,3},{8,12},{9,13},{10,... | collective-permute-start | bytes 786440 | tf_op jit(solution)/shard_map/ppermute | solution.py:421
  122.5 12.1 %collective-permute-start.2 = (bf16[512,256]{1,0:T(8,128)(2,1)S(1)}, bf16[512,256]{1,0:T(8,128)(2,1)S(1)}, u32[]{:S(2)}, u32[]{:S(2)}) collective-permute-start(bf16[512,256]{1,0:T(8,128)(2,1)S(1)} %get-tuple-element.66), channel_id=1, source_target_pairs={{0,2},{1,3},{2,4},{3,5},{4,6},{5,7},{6,0},{7,1},{8,10},{9,11},{10,... | collective-permute-start | bytes 786440 | tf_op jit(solution)/shard_map/ppermute | solution.py:421
  126.5 11.1 %collective-permute-start.3 = (bf16[512,256]{1,0:T(8,128)(2,1)S(1)}, bf16[512,256]{1,0:T(8,128)(2,1)S(1)}, u32[]{:S(2)}, u32[]{:S(2)}) collective-permute-start(bf16[512,256]{1,0:T(8,128)(2,1)S(1)} %get-tuple-element.67), channel_id=1, source_target_pairs={{0,6},{1,7},{2,0},{3,1},{4,2},{5,3},{6,4},{7,5},{8,14},{9,15},{10,... | collective-permute-start | bytes 786440 | tf_op jit(solution)/shard_map/ppermute | solution.py:421

commit v4 on v3

--- a/solution.py
+++ b/solution.py
@@ -55,7 +55,7 @@
     return tile[first : first + 1] + (tile[first + 1 : first + 2] + tile[first + 2 : first + 3])
 
 
-def row_forward(q_ref, k_ref, v_ref, g_ref, mask_ref, out_ref, stat_ref, bias_ref):
+def row_forward(q_ref, k_ref, v_ref, g_ref, mask_ref, out_ref, stat_ref, bias_ref, bias_t_ref):
     heads = q_ref.shape[1] // HEAD_DIM
     for start in range(0, COLS, BLOCK):
         rows = slice(start, start + BLOCK)
@@ -78,6 +78,7 @@
             tile = put_pieces(tile, lanes, 6 * h + 3, dots)
         stat_ref[rows, :] = tile.astype(bf16)
     pattern(mask_ref, bias_ref)
+    pattern(mask_ref, bias_t_ref, turned=True)
 
 
 def pattern(mask_ref, bias_ref, turned=False):
@@ -95,11 +96,6 @@
     rows = dot_nn(spread, mask).astype(bf16)
     whole = dot_nt(spread, rows) if turned else dot_nt(rows, spread)
     bias_ref[...] = jnp.where((whole > 0.5) & same & (key < query), 0.0, NEG).astype(bf16)
-
-
-def pattern_turned(mask_ref, *refs):
-    *_, bias_ref = refs
-    pattern(mask_ref, bias_ref, turned=True)
 
 
 def pack(pieces, refs):
@@ -122,8 +118,8 @@
 def col_forward_joined(first_ref, rest_ref, bias_ref, g_ref, stat_ref, send_ref, y_ref):
     features = g_ref.shape[1]
     y_ref[:, :features] = rest_ref[:, :features]
-    y_ref[:, features : features + HEAD_DIM] = first_ref[...]
-    y_ref[:, features + HEAD_DIM :] = rest_ref[:, features:]
+    y_ref[:, features : 2 * features] = first_ref[...]
+    y_ref[:, 2 * features :] = rest_ref[:, features:]
     col_forward(y_ref, bias_ref, g_ref, stat_ref, send_ref)
 
 
@@ -151,7 +147,10 @@
         send_ref[rows, 2 * features :] = tile.astype(bf16)
 
 
-def col_backward(y_ref, got_ref, sent_ref, bias_t_ref, send_ref):
+def col_backward(y_ref, got_ref, sent_ref, bias_hbm, send_hbm, bias_t_ref, send_ref, sems):
+    fetch = pltpu.make_async_copy(bias_hbm, bias_t_ref, sems.at[0])
+    fetch.start()
+    stores = []
     features = y_ref.shape[1] // 3
     heads = features // HEAD_DIM
     lanes = lanes_like(COLS)
@@ -187,17 +186,29 @@
             h,
             heads,
             bf16,
-        )
-
-
-def gradients(q, k, v, g, lse, dots, masked, out_ref, h, heads, kind):
+            fetch if h == 0 else None,
+        )
+        for n in range(3):
+            at = head(n * heads + h)
+            stores.append(
+                pltpu.make_async_copy(send_ref.at[:, at], send_hbm.at[:, at], sems.at[len(stores) + 1])
+            )
+            stores[-1].start()
+    for copy in stores:
+        copy.wait()
+
+
+def gradients(q, k, v, g, lse, dots, masked, out_ref, h, heads, kind, fetch=None):
     grad_q = None
     for start in range(COLS - BLOCK, -1, -BLOCK):
         keys = slice(start, start + BLOCK)
         rows = slice(start, COLS)
-        s = masked(dot_nt(k(keys), q(rows)) * SCALE, keys, rows)
-        p = jnp.exp(s - lse[:, start:])
+        s = dot_nt(k(keys), q(rows)) * SCALE
         d = dot_nt(v(keys), g(rows))
+        if fetch is not None:
+            fetch.wait()
+            fetch = None
+        p = jnp.exp(masked(s, keys, rows) - lse[:, start:])
         ds = (p * (d - dots[:, start:])).astype(bf16)
         out_ref[keys, head(2 * heads + h)] = dot_nn(p.astype(bf16), g(rows)).astype(kind)
         out_ref[keys, head(heads + h)] = (dot_nn(ds, q(rows)) * SCALE).astype(kind)
@@ -335,7 +346,7 @@
     def forward(queries, key_vectors, value_vectors, attn_grad, mask):
         return call(
             row_forward,
-            [arr(features, f32), arr(128, bf16), arr(COLS, bf16)],
+            [arr(features, f32), arr(128, bf16), arr(COLS, bf16), arr(COLS, bf16)],
             (2 * product, exps),
             queries, key_vectors, value_vectors, attn_grad, mask,
         )
@@ -358,21 +369,20 @@
         qkv = exchange(
             packed((queries, 0, features), (key_vectors, 0, features), (value_vectors, 0, features))
         )
-        row_out, row_stat, bias = forward(queries, key_vectors, value_vectors, attn_grad, mask)
+        row_out, row_stat, bias, bias_t = forward(queries, key_vectors, value_vectors, attn_grad, mask)
         (sent,) = call(
             col_forward,
             [arr(2 * features + 128, bf16)],
             (2 * product, exps),
             qkv, bias, attn_grad, row_stat,
         )
-        return qkv, sent, row_out
+        return qkv, sent, row_out, bias_t
 
     def in_two(queries, key_vectors, value_vectors, attn_grad, mask):
-        first = exchange(packed((key_vectors, 0, HEAD_DIM)))
-        row_out, row_stat, bias = forward(queries, key_vectors, value_vectors, attn_grad, mask)
+        first = exchange(key_vectors)
+        row_out, row_stat, bias, bias_t = forward(queries, key_vectors, value_vectors, attn_grad, mask)
         rest = packed(
             (queries, 0, features),
-            (key_vectors, HEAD_DIM, features - HEAD_DIM),
             (value_vectors, 0, features),
         )
         rest, first = lax.optimization_barrier((rest, first))
@@ -383,17 +393,22 @@
             (2 * product, exps),
             first, rest, bias, attn_grad, row_stat,
         )
-        return qkv, sent, row_out
+        return qkv, sent, row_out, bias_t
 
     place = lax.axis_index("tp")
     core = lax.rem(place, 2)
-    qkv, sent, row_out = lax.cond(
+    qkv, sent, row_out, bias_t = lax.cond(
         core == 1, in_two, at_once, queries, key_vectors, value_vectors, attn_grad, mask
     )
     got = exchange(sent)
-    (bias_t,) = call(pattern_turned, [arr(COLS, bf16)], (2 * tokens * tokens * 64, 0), mask, out_weight, row_out, qkv, sent)
     (col_grads,) = call(
-        col_backward, [arr(3 * features, bf16)], (5 * product, exps), qkv, got, sent, bias_t
+        col_backward, [arr(3 * features, bf16)], (5 * product, exps), qkv, got, sent, bias_t,
+        far=(3,), far_out=(0,),
+        scratch=[
+            pltpu.VMEM((COLS, COLS), bf16),
+            pltpu.VMEM((tokens, 3 * features), bf16),
+            pltpu.SemaphoreType.DMA((1 + 3 * heads,)),
+        ],
     )
     back = exchange(col_grads)
     got, col_grads = lax.optimization_barrier((got, col_grads))

time: 141 us -> 140 us (level)
  blocking collectives: 0 us -> 31.3 us
  waiting for transfers between devices: 57.5 us -> 35.6 us
  starting transfers between devices: 58.6 us -> 51 us
  Pallas kernels: 21.5 us -> 18.3 us
    all_to_all x0 -> x1, blocking collectives: none -> 31.3 us  [exchange(): return lax.all_to_all(x, 'seq', split_axis=0, concat_axis=0, tiled=True)]
    all_to_all x3 -> x2, waiting for transfers between devices: 47.8 us -> 25.9 us  [exchange(): return lax.all_to_all(x, 'seq', split_axis=0, concat_axis=0, tiled=True)]
    all_to_all x3 -> x2, starting transfers between devices: 33.5 us -> 26.3 us  [exchange(): return lax.all_to_all(x, 'seq', split_axis=0, concat_axis=0, tiled=True)]
    pallas_call x11 -> x10, Pallas kernels: 21.5 us -> 18.3 us  [call(): pl.pallas_call(kernel, out_shape=outs, in_specs=[smem if a.ndim == 1 else...]
  transfers between devices with their start and end apart: 7 -> 6, of which waited for: 6 -> 5; matrix products, arithmetic and copies ran while one was open for 0% -> 0% of each run, Pallas kernels for 9% -> 8%
where the time goes in v4:
time: 140 us; the launch traced here: 138 us
  starting transfers between devices  51 us (36%)
  waiting for transfers between devices  35.6 us (25%)
  blocking collectives  31.3 us (22%)
  Pallas kernels  18.3 us (13%)
    all_to_all x1, blocking collectives, exchange(): return lax.all_to_all(x, 'seq', split_axis=0, concat_axis=0, tiled=True)  31.3 us
    all_to_all x2, starting transfers between devices, exchange(): return lax.all_to_all(x, 'seq', split_axis=0, concat_axis=0, tiled=True)  26.3 us
    all_to_all x2, waiting for transfers between devices, exchange(): return lax.all_to_all(x, 'seq', split_axis=0, concat_axis=0, tiled=True)  25.9 us
    pallas_call x10, Pallas kernels, call(): pl.pallas_call(kernel, out_shape=outs, in_specs=[smem if a.ndim == 1 else...  18.3 us
    ppermute x1, starting transfers between devices, local(): pair = lax.ppermute(give, 'tp', [(t, t ^ 1) for t in range(count)])  15.5 us
    ppermute x3, starting transfers between devices, local(): lax.ppermute(sends[n - 1], 'tp', [(t, (t + 2 * n) % count) for t in range...  9.26 us
    ppermute x3, waiting for transfers between devices, local(): lax.ppermute(sends[n - 1], 'tp', [(t, (t + 2 * n) % count) for t in range...  7.62 us
  transfers between devices with their start and end apart: 6, of which 5 were waited for; matrix products, arithmetic and copies ran while one was open for 0% of the time, Pallas kernels for 8%

profile of v4, /device:TPU:6, one launch (start us, length us, event | category | flops | bytes accessed | tf_op | source)
XLA Modules:
  0.0 138.2 jit_solution(17726799398061223063)
XLA Ops:
  0.6 0.0 copy-start
  0.7 0.9 copy-done
  1.5 51.4 %conditional.1 = (bf16[512,768]{1,0:T(8,128)(2,1)}, bf16[512,640]{1,0:T(8,128)(2,1)S(1)}, f32[512,256]{1,0:T(8,128)}, bf16[512,512]{1,0:T(8,128)(2,1)}) conditional(s32[]{:T(128)} %convert_element_type.3, (bf16[512,256]{1,0:T(8,128)(2,1)}, bf16[512,256]{1,0:T(8,128)(2,1)}, bf16[512,256]{1,0:T(8,128)(2,1)}, bf16[512,256]{1,0:T(8,128)(2,1)}, ...), branch_computations={%region_0.1_spmd, %region_1.2_spmd} | conditional | flops 536870912 | bytes 16400588 | solution.py:400
  1.6 0.0 copy-start.12
  1.6 0.0 copy-start.15
  1.6 2.1 %kernel.2 = bf16[512,768]{1,0:T(8,128)(2,1)} custom-call(bf16[512,256]{1,0:T(8,128)(2,1)} %get-tuple-element.20.refs_0_.q_ref, bf16[512,256]{1,0:T(8,128)(2,1)} %get-tuple-element.21.refs_1_.k_ref, bf16[512,256]{1,0:T(8,128)(2,1)} %get-tuple-element.22.refs_2_.v_ref), custom_call_target="tpu_custom_call" | custom-call | bytes 1572864 | tf_op jit(solution)/shard_map/cond/branch_0_fun/kernel/pallas_call | solution.py:318
  3.7 18.7 %all-to-all-start = ((bf16[64,8,768]{2,1,0:T(8,128)(2,1)}), bf16[64,8,768]{2,1,0:T(8,128)(2,1)S(1)}, u32[]{:S(2)}, u32[]{:S(2)}) async-start(bf16[64,8,768]{2,1,0:T(8,128)(2,1)} %bitcast), calls=%async_computation | async-start | bytes 1572864 | tf_op jit(solution)/shard_map/cond/branch_0_fun/all_to_all | solution.py:331
  22.4 0.0 copy-done.4
  22.4 0.0 copy-done.9
  22.5 0.0 copy-done.12
  22.5 0.0 copy-done.15
  22.5 3.1 %row_forward.2 = (f32[512,256]{1,0:T(8,128)}, bf16[512,128]{1,0:T(8,128)(2,1)S(1)}, bf16[512,512]{1,0:T(8,128)(2,1)S(1)}, bf16[512,512]{1,0:T(8,128)(2,1)}) custom-call(bf16[512,256]{1,0:T(8,128)(2,1)S(1)} %copy-done.9, bf16[512,256]{1,0:T(8,128)(2,1)S(1)} %copy-done.12, bf16[512,256]{1,0:T(8,128)(2,1)S(1)} %copy-done.15, bf16[512,256]{1,0:T(8,128)(2,1)S(1)} %copy-done.4, ...), custom_call_target="tpu_custom_call" | custom-call | flops 268435456 | bytes 2768896 | tf_op jit(solution)/shard_map/cond/branch_0_fun/row_forward/pallas_call | solution.py:318
  25.6 25.9 %all-to-all-done = bf16[64,8,768]{2,1,0:T(8,128)(2,1)S(1)} async-done(((bf16[64,8,768]{2,1,0:T(8,128)(2,1)}), bf16[64,8,768]{2,1,0:T(8,128)(2,1)S(1)}, u32[]{:S(2)}, u32[]{:S(2)}) %all-to-all-start) | async-done | bytes 786464 | tf_op jit(solution)/shard_map/cond/branch_0_fun/all_to_all | solution.py:331
  51.5 1.5 %col_forward.1 = bf16[512,640]{1,0:T(8,128)(2,1)S(1)} custom-call(bf16[512,768]{1,0:T(8,128)(2,1)S(1)} %bitcast.20, bf16[512,512]{1,0:T(8,128)(2,1)S(1)} %get-tuple-element.25.bias_ref, bf16[512,256]{1,0:T(8,128)(2,1)S(1)} %copy-done.4, bf16[512,128]{1,0:T(8,128)(2,1)S(1)} %get-tuple-element.26.stat_ref), custom_call_target="tpu_custom_call" | custom-call | flops 268435456 | bytes 2359296 | tf_op jit(solution)/shard_map/cond/branch_0_fun/col_forward/pallas_call | solution.py:318
  53.0 0.0 copy-done.6
  53.0 0.0 copy-start.2
  53.0 0.0 copy-start.7
  53.0 0.0 copy-start.17
  53.0 31.3 %all_to_all.47 = bf16[64,8,640]{2,1,0:T(8,128)(2,1)S(1)} all-to-all(bf16[64,8,640]{2,1,0:T(8,128)(2,1)S(1)} %bitcast.19), channel_id=1, replica_groups=mesh['seq'=64,'tp'=8] {'seq'}, dimensions={0} | all-to-all | bytes 1310720 | tf_op jit(solution)/shard_map/all_to_all | solution.py:331
  84.4 0.0 copy-done.2
  84.4 0.0 copy-done.7
  84.4 0.0 copy-done.17
  84.4 2.5 %col_backward.1 = bf16[512,768]{1,0:T(8,128)(2,1)} custom-call(bf16[512,768]{1,0:T(8,128)(2,1)S(1)} %copy-done.7, bf16[512,640]{1,0:T(8,128)(2,1)S(1)} %bitcast.14, bf16[512,640]{1,0:T(8,128)(2,1)S(1)} %get-tuple-element.62.sent_ref, bf16[512,512]{1,0:T(8,128)(2,1)S(1)} %copy-done.17), custom_call_target="tpu_custom_call" | custom-call | flops 671088640 | bytes 3407872 | tf_op jit(solution)/shard_map/col_backward/pallas_call | solution.py:318
  86.9 0.0 copy-start.1
  86.9 0.0 copy-start.3
  86.9 7.5 %all-to-all-start.4 = ((bf16[64,8,768]{2,1,0:T(8,128)(2,1)}), bf16[64,8,768]{2,1,0:T(8,128)(2,1)S(1)}, u32[]{:S(2)}, u32[]{:S(2)}) async-start(bf16[64,8,768]{2,1,0:T(8,128)(2,1)} %bitcast.11), calls=%async_computation.4 | async-start | bytes 1572864 | tf_op jit(solution)/shard_map/all_to_all | solution.py:331
  94.4 0.0 copy-done.1
  94.4 0.0 copy-done.3
  94.4 3.9 %row_merge.1 = (bf16[512,256]{1,0:T(8,128)(2,1)S(1)}, bf16[512,1024]{1,0:T(8,128)(2,1)}, f32[512,128]{1,0:T(8,128)S(1)}) custom-call(s32[1]{0:T(128)} %bitcast.7.core_ref, f32[512,256]{1,0:T(8,128)} %get-tuple-element.61.out_ref, bf16[512,640]{1,0:T(8,128)(2,1)} %copy-done.2, bf16[512,640]{1,0:T(8,128)(2,1)S(1)} %bitcast.15, bf16[512,256]{1,0:T(8,128)(2,1)S(1)} %copy-done.3, ...), custom_call_target="tpu_custom_call" | custom-call | flops 268435456 | bytes 4718596 | tf_op jit(solution)/shard_map/row_merge/pallas_call | solution.py:318
  98.3 15.5 %collective-permute-start = (bf16[512,1024]{1,0:T(8,128)(2,1)}, bf16[512,1024]{1,0:T(8,128)(2,1)}, u32[]{:S(2)}, u32[]{:S(2)}) collective-permute-start(bf16[512,1024]{1,0:T(8,128)(2,1)} %get-tuple-element.67), channel_id=1, source_target_pairs={{0,1},{1,0},{2,3},{3,2},{4,5},{5,4},{6,7},{7,6},{8,9},{9,8},{10,11... | collective-permute-start | bytes 3145736 | tf_op jit(solution)/shard_map/ppermute | solution.py:424
  113.9 0.5 project_own.1.keep_ref
  114.3 0.0 copy-start.8
  114.3 0.0 copy-start.11
  114.4 0.0 copy-start.14
  114.4 2.1 %collective-permute-done.got_ref = bf16[512,1024]{1,0:T(8,128)(2,1)} collective-permute-done((bf16[512,1024]{1,0:T(8,128)(2,1)}, bf16[512,1024]{1,0:T(8,128)(2,1)}, u32[]{:S(2)}, u32[]{:S(2)}) %collective-permute-start) | collective-permute-done | bytes 1048608 | tf_op jit(solution)/shard_map/ppermute | solution.py:424
  116.5 1.5 %pair_sum.1 = (f32[512,256]{1,0:T(8,128)S(1)}, bf16[512,256]{1,0:T(8,128)(2,1)S(1)}, bf16[512,256]{1,0:T(8,128)(2,1)S(1)}, bf16[512,256]{1,0:T(8,128)(2,1)S(1)}) custom-call(s32[1]{0:T(128)} %bitcast.6.x_ref, bf16[512,1024]{1,0:T(8,128)(2,1)S(1)} %project_own.1.keep_ref, bf16[512,1024]{1,0:T(8,128)(2,1)} %collective-permute-done.got_ref), custom_call_target="tpu_custom_call" | custom-call | flops 524288 | bytes 3407876 | tf_op jit(solution)/shard_map/pair_sum/pallas_call | solution.py:318
  118.0 3.3 %collective-permute-start.1 = (bf16[512,256]{1,0:T(8,128)(2,1)S(1)}, bf16[512,256]{1,0:T(8,128)(2,1)S(1)}, u32[]{:S(2)}, u32[]{:S(2)}) collective-permute-start(bf16[512,256]{1,0:T(8,128)(2,1)S(1)} %get-tuple-element.69), channel_id=1, source_target_pairs={{0,4},{1,5},{2,6},{3,7},{4,0},{5,1},{6,2},{7,3},{8,12},{9,13},{10,... | collective-permute-start | bytes 786440 | tf_op jit(solution)/shard_map/ppermute | solution.py:436
  121.3 4.0 %collective-permute-start.2 = (bf16[512,256]{1,0:T(8,128)(2,1)S(1)}, bf16[512,256]{1,0:T(8,128)(2,1)S(1)}, u32[]{:S(2)}, u32[]{:S(2)}) collective-permute-start(bf16[512,256]{1,0:T(8,128)(2,1)S(1)} %get-tuple-element.70), channel_id=1, source_target_pairs={{0,2},{1,3},{2,4},{3,5},{4,6},{5,7},{6,0},{7,1},{8,10},{9,11},{10,... | collective-permute-start | bytes 786440 | tf_op jit(solution)/shard_map/ppermute | solution.py:436
  125.3 1.9 %collective-permute-start.3 = (bf16[512,256]{1,0:T(8,128)(2,1)S(1)}, bf16[512,256]{1,0:T(8,128)(2,1)S(1)}, u32[]{:S(2)}, u32[]{:S(2)}) collective-permute-start(bf16[512,256]{1,0:T(8,128)(2,1)S(1)} %get-tuple-element.71), channel_id=1, source_target_pairs={{0,6},{1,7},{2,0},{3,1},{4,2},{5,3},{6,4},{7,5},{8,14},{9,15},{10,... | collective-permute-start | bytes 786440 | tf_op jit(solution)/shard_map/ppermute | solution.py:436
  127.3 0.0 copy-done.8
  127.3 0.0 copy-done.11
  127.3 1.5 %row_backward.1.grad_ref = f32[512,768]{1,0:T(8,128)S(1)} custom-call(bf16[512,256]{1,0:T(8,128)(2,1)S(1)} %copy-done.8, bf16[512,256]{1,0:T(8,128)(2,1)S(1)} %copy-done.11, bf16[512,256]{1,0:T(8,128)(2,1)S(1)} %copy-done.14, bf16[512,256]{1,0:T(8,128)(2,1)S(1)} %copy-done.3, f32[512,128]{1,0:T(8,128)S(1)} %get-tuple-element.72.merged_ref), custom_call_target="tpu_custom_call" | custom-call | flops 671088640 | bytes 2883584 | tf_op jit(solution)/shard_map/row_backward/pallas_call | solution.py:318
  128.8 1.4 %collective-permute-done.1.refs_0_ = bf16[512,256]{1,0:T(8,128)(2,1)S(1)} collective-permute-done((bf16[512,256]{1,0:T(8,128)(2,1)S(1)}, bf16[512,256]{1,0:T(8,128)(2,1)S(1)}, u32[]{:S(2)}, u32[]{:S(2)}) %collective-permute-start.1) | collective-permute-done | bytes 262176 | tf_op jit(solution)/shard_map/ppermute | solution.py:436
  130.2 3.2 %collective-permute-done.2.refs_1_ = bf16[512,256]{1,0:T(8,128)(2,1)S(1)} collective-permute-done((bf16[512,256]{1,0:T(8,128)(2,1)S(1)}, bf16[512,256]{1,0:T(8,128)(2,1)S(1)}, u32[]{:S(2)}, u32[]{:S(2)}) %collective-permute-start.2) | collective-permute-done | bytes 262176 | tf_op jit(solution)/shard_map/ppermute | solution.py:436
  133.4 3.1 %collective-permute-done.3.refs_2_ = bf16[512,256]{1,0:T(8,128)(2,1)S(1)} collective-permute-done((bf16[512,256]{1,0:T(8,128)(2,1)S(1)}, bf16[512,256]{1,0:T(8,128)(2,1)S(1)}, u32[]{:S(2)}, u32[]{:S(2)}) %collective-permute-start.3) | collective-permute-done | bytes 262176 | tf_op jit(solution)/shard_map/ppermute | solution.py:436
  136.4 0.8 project_sum.1
  137.3 0.0 all-to-all-done.4
  137.3 1.0 finish.1
  (5 shorter events, 0.0 us)
Async XLA Ops:
  0.6 0.9 copy-start
  1.5 20.9 %copy-start.4 = (bf16[512,256]{1,0:T(8,128)(2,1)S(1)}, bf16[512,256]{1,0:T(8,128)(2,1)}, u32[]{:S(2)}) copy-start(bf16[512,256]{1,0:T(8,128)(2,1)} %get-tuple-element.23.g_ref) | copy-start | bytes 786436 | tf_op jit(solution)/shard_map/cond
  1.5 20.9 %copy-start.9 = (bf16[512,256]{1,0:T(8,128)(2,1)S(1)}, bf16[512,256]{1,0:T(8,128)(2,1)}, u32[]{:S(2)}) copy-start(bf16[512,256]{1,0:T(8,128)(2,1)} %get-tuple-element.20.refs_0_.q_ref) | copy-start | bytes 786436 | tf_op jit(solution)/shard_map/cond
  1.6 20.9 %copy-start.12 = (bf16[512,256]{1,0:T(8,128)(2,1)S(1)}, bf16[512,256]{1,0:T(8,128)(2,1)}, u32[]{:S(2)}) copy-start(bf16[512,256]{1,0:T(8,128)(2,1)} %get-tuple-element.21.refs_1_.k_ref) | copy-start | bytes 786436 | tf_op jit(solution)/shard_map/cond
  1.6 20.9 %copy-start.15 = (bf16[512,256]{1,0:T(8,128)(2,1)S(1)}, bf16[512,256]{1,0:T(8,128)(2,1)}, u32[]{:S(2)}) copy-start(bf16[512,256]{1,0:T(8,128)(2,1)} %get-tuple-element.22.refs_2_.v_ref) | copy-start | bytes 786436 | tf_op jit(solution)/shard_map/cond
  3.7 47.8 %all-to-all-start = ((bf16[64,8,768]{2,1,0:T(8,128)(2,1)}), bf16[64,8,768]{2,1,0:T(8,128)(2,1)S(1)}, u32[]{:S(2)}, u32[]{:S(2)}) async-start(bf16[64,8,768]{2,1,0:T(8,128)(2,1)} %bitcast), calls=%async_computation | async-start | bytes 1572864 | tf_op jit(solution)/shard_map/cond/branch_0_fun/all_to_all | solution.py:331
  51.5 1.5 %copy-start.6 = (bf16[64,8,768]{2,1,0:T(8,128)(2,1)}, bf16[64,8,768]{2,1,0:T(8,128)(2,1)S(1)}, u32[]{:S(2)}) copy-start(bf16[64,8,768]{2,1,0:T(8,128)(2,1)S(1)} %all-to-all-done) | copy-start | bytes 2359300 | tf_op jit(solution)/shard_map/cond
  53.0 31.4 %copy-start.2 = (bf16[512,640]{1,0:T(8,128)(2,1)}, bf16[512,640]{1,0:T(8,128)(2,1)S(1)}, u32[]{:S(2)}) copy-start(bf16[512,640]{1,0:T(8,128)(2,1)S(1)} %get-tuple-element.62.sent_ref) | copy-start | bytes 1966084
  53.0 31.4 %copy-start.7 = (bf16[512,768]{1,0:T(8,128)(2,1)S(1)}, bf16[512,768]{1,0:T(8,128)(2,1)}, u32[]{:S(2)}) copy-start(bf16[512,768]{1,0:T(8,128)(2,1)} %get-tuple-element.63.y_ref) | copy-start | bytes 2359300
  53.0 31.4 %copy-start.17 = (bf16[512,512]{1,0:T(8,128)(2,1)S(1)}, bf16[512,512]{1,0:T(8,128)(2,1)}, u32[]{:S(2)}) copy-start(bf16[512,512]{1,0:T(8,128)(2,1)} %get-tuple-element.64.bias_hbm) | copy-start | bytes 1572868
  86.9 7.5 %copy-start.1 = (bf16[256,2048]{1,0:T(8,128)(2,1)S(1)}, bf16[256,2048]{1,0:T(8,128)(2,1)}, u32[]{:S(2)}) copy-start(bf16[256,2048]{1,0:T(8,128)(2,1)} %weight_ref.3) | copy-start | bytes 3145732
  86.9 7.5 %copy-start.3 = (bf16[512,256]{1,0:T(8,128)(2,1)S(1)}, bf16[512,256]{1,0:T(8,128)(2,1)}, u32[]{:S(2)}) copy-start(bf16[512,256]{1,0:T(8,128)(2,1)} %g_ref.3) | copy-start | bytes 786436
  86.9 50.3 %all-to-all-start.4 = ((bf16[64,8,768]{2,1,0:T(8,128)(2,1)}), bf16[64,8,768]{2,1,0:T(8,128)(2,1)S(1)}, u32[]{:S(2)}, u32[]{:S(2)}) async-start(bf16[64,8,768]{2,1,0:T(8,128)(2,1)} %bitcast.11), calls=%async_computation.4 | async-start | bytes 1572864 | tf_op jit(solution)/shard_map/all_to_all | solution.py:331
  98.3 18.1 %collective-permute-start = (bf16[512,1024]{1,0:T(8,128)(2,1)}, bf16[512,1024]{1,0:T(8,128)(2,1)}, u32[]{:S(2)}, u32[]{:S(2)}) collective-permute-start(bf16[512,1024]{1,0:T(8,128)(2,1)} %get-tuple-element.67), channel_id=1, source_target_pairs={{0,1},{1,0},{2,3},{3,2},{4,5},{5,4},{6,7},{7,6},{8,9},{9,8},{10,11... | collective-permute-start | bytes 3145736 | tf_op jit(solution)/shard_map/ppermute | solution.py:424
  114.3 12.9 %copy-start.8 = (bf16[512,256]{1,0:T(8,128)(2,1)S(1)}, bf16[512,256]{1,0:T(8,128)(2,1)}, u32[]{:S(2)}) copy-start(bf16[512,256]{1,0:T(8,128)(2,1)} %q_ref.1) | copy-start | bytes 786436
  114.3 12.9 %copy-start.11 = (bf16[512,256]{1,0:T(8,128)(2,1)S(1)}, bf16[512,256]{1,0:T(8,128)(2,1)}, u32[]{:S(2)}) copy-start(bf16[512,256]{1,0:T(8,128)(2,1)} %k_ref.1) | copy-start | bytes 786436
  114.4 12.9 %copy-start.14 = (bf16[512,256]{1,0:T(8,128)(2,1)S(1)}, bf16[512,256]{1,0:T(8,128)(2,1)}, u32[]{:S(2)}) copy-start(bf16[512,256]{1,0:T(8,128)(2,1)} %v_ref.1) | copy-start | bytes 786436
  118.0 12.2 %collective-permute-start.1 = (bf16[512,256]{1,0:T(8,128)(2,1)S(1)}, bf16[512,256]{1,0:T(8,128)(2,1)S(1)}, u32[]{:S(2)}, u32[]{:S(2)}) collective-permute-start(bf16[512,256]{1,0:T(8,128)(2,1)S(1)} %get-tuple-element.69), channel_id=1, source_target_pairs={{0,4},{1,5},{2,6},{3,7},{4,0},{5,1},{6,2},{7,3},{8,12},{9,13},{10,... | collective-permute-start | bytes 786440 | tf_op jit(solution)/shard_map/ppermute | solution.py:436
  121.3 12.1 %collective-permute-start.2 = (bf16[512,256]{1,0:T(8,128)(2,1)S(1)}, bf16[512,256]{1,0:T(8,128)(2,1)S(1)}, u32[]{:S(2)}, u32[]{:S(2)}) collective-permute-start(bf16[512,256]{1,0:T(8,128)(2,1)S(1)} %get-tuple-element.70), channel_id=1, source_target_pairs={{0,2},{1,3},{2,4},{3,5},{4,6},{5,7},{6,0},{7,1},{8,10},{9,11},{10,... | collective-permute-start | bytes 786440 | tf_op jit(solution)/shard_map/ppermute | solution.py:436
  125.3 11.1 %collective-permute-start.3 = (bf16[512,256]{1,0:T(8,128)(2,1)S(1)}, bf16[512,256]{1,0:T(8,128)(2,1)S(1)}, u32[]{:S(2)}, u32[]{:S(2)}) collective-permute-start(bf16[512,256]{1,0:T(8,128)(2,1)S(1)} %get-tuple-element.71), channel_id=1, source_target_pairs={{0,6},{1,7},{2,0},{3,1},{4,2},{5,3},{6,4},{7,5},{8,14},{9,15},{10,... | collective-permute-start | bytes 786440 | tf_op jit(solution)/shard_map/ppermute | solution.py:436

commit v5 on v4

--- a/solution.py
+++ b/solution.py
@@ -10,6 +10,7 @@
 TILE = 128
 SCALE = HEAD_DIM ** (-0.5)
 NEG = -1e30
+FORWARD_BLOCK = 512
 BLOCK = 256
 CSTAT = 64
 
@@ -57,14 +58,14 @@
 
 def row_forward(q_ref, k_ref, v_ref, g_ref, mask_ref, out_ref, stat_ref, bias_ref, bias_t_ref):
     heads = q_ref.shape[1] // HEAD_DIM
-    for start in range(0, COLS, BLOCK):
-        rows = slice(start, start + BLOCK)
-        keys = slice(0, start + BLOCK)
-        allowed = lax.broadcasted_iota(jnp.int32, (BLOCK, start + BLOCK), 1) <= (
-            lax.broadcasted_iota(jnp.int32, (BLOCK, start + BLOCK), 0) + start
-        )
-        lanes = lanes_like(BLOCK)
-        tile = jnp.zeros((BLOCK, 128), f32)
+    for start in range(0, COLS, FORWARD_BLOCK):
+        rows = slice(start, start + FORWARD_BLOCK)
+        keys = slice(0, start + FORWARD_BLOCK)
+        allowed = lax.broadcasted_iota(jnp.int32, (FORWARD_BLOCK, start + FORWARD_BLOCK), 1) <= (
+            lax.broadcasted_iota(jnp.int32, (FORWARD_BLOCK, start + FORWARD_BLOCK), 0) + start
+        )
+        lanes = lanes_like(FORWARD_BLOCK)
+        tile = jnp.zeros((FORWARD_BLOCK, 128), f32)
         for h in range(heads):
             s = dot_nt(q_ref[rows, head(h)], k_ref[keys, head(h)]) * SCALE
             s = jnp.where(allowed, s, NEG)
@@ -118,8 +119,8 @@
 def col_forward_joined(first_ref, rest_ref, bias_ref, g_ref, stat_ref, send_ref, y_ref):
     features = g_ref.shape[1]
     y_ref[:, :features] = rest_ref[:, :features]
-    y_ref[:, features : 2 * features] = first_ref[...]
-    y_ref[:, 2 * features :] = rest_ref[:, features:]
+    y_ref[:, features : features + HEAD_DIM] = first_ref[...]
+    y_ref[:, features + HEAD_DIM :] = rest_ref[:, features:]
     col_forward(y_ref, bias_ref, g_ref, stat_ref, send_ref)
 
 
@@ -127,20 +128,21 @@
     features = g_ref.shape[1]
     heads = features // HEAD_DIM
     send_ref[:, :features] = g_ref[...]
-    for start in range(0, COLS, BLOCK):
-        rows = slice(start, start + BLOCK)
-        keys = slice(0, start + BLOCK)
-        lanes = lanes_like(BLOCK)
-        tile = jnp.zeros((BLOCK, 128), f32)
-        for h in range(heads):
-            q = y_ref[rows, head(h)]
-            k = y_ref[keys, head(heads + h)]
-            v = y_ref[keys, head(2 * heads + h)]
-            s = dot_nt(q, k) * SCALE + bias_ref[rows, keys].astype(f32)
-            m = jnp.max(s, axis=1, keepdims=True)
-            p = jnp.exp(s - m)
-            total = jnp.sum(p, axis=1, keepdims=True)
-            out = dot_nn(p.astype(bf16), v) / total
+    for start in range(0, COLS, FORWARD_BLOCK):
+        rows = slice(start, start + FORWARD_BLOCK)
+        keys = slice(0, start + FORWARD_BLOCK)
+        lanes = lanes_like(FORWARD_BLOCK)
+        tile = jnp.zeros((FORWARD_BLOCK, 128), f32)
+        scores = [
+            dot_nt(y_ref[rows, head(h)], y_ref[keys, head(heads + h)]) * SCALE
+            + bias_ref[rows, keys].astype(f32)
+            for h in range(heads)
+        ]
+        tops = [jnp.max(x, axis=1, keepdims=True) for x in scores]
+        weights = [jnp.exp(x - m) for x, m in zip(scores, tops)]
+        totals = [jnp.sum(p, axis=1, keepdims=True) for p in weights]
+        for h, (m, p, total) in enumerate(zip(tops, weights, totals)):
+            out = dot_nn(p.astype(bf16), y_ref[keys, head(2 * heads + h)]) / total
             send_ref[rows, head(heads + h)] = out.astype(bf16)
             tile = put_pieces(tile, lanes, CSTAT + 3 * h, m + jnp.log(total))
         tile = jnp.where(lanes < CSTAT, stat_ref[rows, :].astype(f32), tile)
@@ -163,6 +165,7 @@
         product = got_ref[:, head(h)].astype(f32) * sent_ref[:, head(heads + h)].astype(f32)
         tile = jnp.where(lanes == 32 + h, jnp.sum(product, axis=1, keepdims=True), tile)
     tile = tile.T
+    lses, dots = [], []
     for h in range(heads):
         row_lse = take_rows(tile, 6 * h)
         row_dots = take_rows(tile, 6 * h + 3)
@@ -172,51 +175,65 @@
         row_factor = jnp.exp(row_lse - top)
         col_factor = jnp.exp(col_lse - top)
         both = row_factor + col_factor
-        lse = top + jnp.log(both)
-        dots = (row_dots * row_factor + col_dots * col_factor) / both
-        gradients(
-            lambda at: y_ref[at, head(h)],
-            lambda at: y_ref[at, head(heads + h)],
-            lambda at: y_ref[at, head(2 * heads + h)],
-            lambda at: got_ref[at, head(h)],
-            lse,
-            dots,
-            lambda s, keys, rows: s + bias_t_ref[keys, rows].astype(f32),
-            send_ref,
-            h,
-            heads,
-            bf16,
-            fetch if h == 0 else None,
-        )
-        for n in range(3):
-            at = head(n * heads + h)
-            stores.append(
-                pltpu.make_async_copy(send_ref.at[:, at], send_hbm.at[:, at], sems.at[len(stores) + 1])
+        lses.append(top + jnp.log(both))
+        dots.append((row_dots * row_factor + col_dots * col_factor) / both)
+
+    def store(rows, lanes):
+        stores.append(
+            pltpu.make_async_copy(
+                send_ref.at[rows, lanes], send_hbm.at[rows, lanes], sems.at[len(stores) + 1]
             )
-            stores[-1].start()
+        )
+        stores[-1].start()
+
+    def part(ref, n):
+        return lambda at, h: ref[at, head(n * heads + h)]
+
+    gradients(
+        part(y_ref, 0),
+        part(y_ref, 1),
+        part(y_ref, 2),
+        part(got_ref, 0),
+        lses,
+        dots,
+        lambda s, keys, rows: s + bias_t_ref[keys, rows].astype(f32),
+        send_ref,
+        heads,
+        bf16,
+        fetch.wait,
+        store,
+    )
     for copy in stores:
         copy.wait()
 
 
-def gradients(q, k, v, g, lse, dots, masked, out_ref, h, heads, kind, fetch=None):
-    grad_q = None
+def gradients(q, k, v, g, lses, dots, masked, out_ref, heads, kind, ready=None, store=None):
+    features = heads * HEAD_DIM
+    grad_q = [None] * heads
     for start in range(COLS - BLOCK, -1, -BLOCK):
         keys = slice(start, start + BLOCK)
         rows = slice(start, COLS)
-        s = dot_nt(k(keys), q(rows)) * SCALE
-        d = dot_nt(v(keys), g(rows))
-        if fetch is not None:
-            fetch.wait()
-            fetch = None
-        p = jnp.exp(masked(s, keys, rows) - lse[:, start:])
-        ds = (p * (d - dots[:, start:])).astype(bf16)
-        out_ref[keys, head(2 * heads + h)] = dot_nn(p.astype(bf16), g(rows)).astype(kind)
-        out_ref[keys, head(heads + h)] = (dot_nn(ds, q(rows)) * SCALE).astype(kind)
-        term = dot_tn(ds, k(keys)) * SCALE
-        if grad_q is not None:
-            term = term + jnp.concatenate([jnp.zeros((BLOCK, HEAD_DIM), f32), grad_q], axis=0)
-        grad_q = term
-    out_ref[:, head(h)] = grad_q.astype(kind)
+        products = [
+            (dot_nt(k(keys, h), q(rows, h)) * SCALE, dot_nt(v(keys, h), g(rows, h))) for h in range(heads)
+        ]
+        if ready is not None:
+            ready()
+            ready = None
+        for h, (s, d) in enumerate(products):
+            p = jnp.exp(masked(s, keys, rows) - lses[h][:, start:])
+            ds = (p * (d - dots[h][:, start:])).astype(bf16)
+            out_ref[keys, head(2 * heads + h)] = dot_nn(p.astype(bf16), g(rows, h)).astype(kind)
+            out_ref[keys, head(heads + h)] = (dot_nn(ds, q(rows, h)) * SCALE).astype(kind)
+            term = dot_tn(ds, k(keys, h)) * SCALE
+            if grad_q[h] is not None:
+                term = term + jnp.concatenate([jnp.zeros((BLOCK, HEAD_DIM), f32), grad_q[h]], axis=0)
+            grad_q[h] = term
+        if store is not None:
+            store(keys, slice(features, 3 * features))
+    for h in range(heads):
+        out_ref[:, head(h)] = grad_q[h].astype(kind)
+    if store is not None:
+        store(slice(0, COLS), slice(0, features))
 
 
 def row_merge(core_ref, out_ref, sent_ref, got_ref, g_ref, weight_ref, att_ref, give_ref, merged_ref):
@@ -285,20 +302,21 @@
         )
         return jnp.where(allowed, s, NEG)
 
-    for h in range(heads):
-        gradients(
-            lambda at: q_ref[at, head(h)],
-            lambda at: k_ref[at, head(h)],
-            lambda at: v_ref[at, head(h)],
-            lambda at: g_ref[at, head(h)],
-            tile[2 * h : 2 * h + 1],
-            tile[2 * h + 1 : 2 * h + 2],
-            masked,
-            grad_ref,
-            h,
-            heads,
-            f32,
-        )
+    def part(ref):
+        return lambda at, h: ref[at, head(h)]
+
+    gradients(
+        part(q_ref),
+        part(k_ref),
+        part(v_ref),
+        part(g_ref),
+        [tile[2 * h : 2 * h + 1] for h in range(heads)],
+        [tile[2 * h + 1 : 2 * h + 2] for h in range(heads)],
+        masked,
+        grad_ref,
+        heads,
+        f32,
+    )
 
 
 def finish(grad_ref, back_ref, q_ref, k_ref, v_ref):
@@ -379,10 +397,11 @@
         return qkv, sent, row_out, bias_t
 
     def in_two(queries, key_vectors, value_vectors, attn_grad, mask):
-        first = exchange(key_vectors)
+        first = exchange(key_vectors[:, :HEAD_DIM])
         row_out, row_stat, bias, bias_t = forward(queries, key_vectors, value_vectors, attn_grad, mask)
         rest = packed(
             (queries, 0, features),
+            (key_vectors, HEAD_DIM, features - HEAD_DIM),
             (value_vectors, 0, features),
         )
         rest, first = lax.optimization_barrier((rest, first))
@@ -407,7 +426,7 @@
         scratch=[
             pltpu.VMEM((COLS, COLS), bf16),
             pltpu.VMEM((tokens, 3 * features), bf16),
-            pltpu.SemaphoreType.DMA((1 + 3 * heads,)),
+            pltpu.SemaphoreType.DMA((2 + COLS // BLOCK,)),
         ],
     )
     back = exchange(col_grads)

time: 140 us -> 139 us (level)
  no operation moved by 1% of the time
where the time goes in v5:
time: 139 us; the launch traced here: 138 us
  starting transfers between devices  51.3 us (37%)
  waiting for transfers between devices  35.3 us (25%)
  blocking collectives  31.4 us (23%)
  Pallas kernels  17.8 us (13%)
    all_to_all x1, blocking collectives, exchange(): return lax.all_to_all(x, 'seq', split_axis=0, concat_axis=0, tiled=True)  31.4 us
    all_to_all x2, starting transfers between devices, exchange(): return lax.all_to_all(x, 'seq', split_axis=0, concat_axis=0, tiled=True)  26 us
    all_to_all x2, waiting for transfers between devices, exchange(): return lax.all_to_all(x, 'seq', split_axis=0, concat_axis=0, tiled=True)  25.5 us
    pallas_call x10, Pallas kernels, call(): pl.pallas_call(kernel, out_shape=outs, in_specs=[smem if a.ndim == 1 else...  17.8 us
    ppermute x1, starting transfers between devices, local(): pair = lax.ppermute(give, 'tp', [(t, t ^ 1) for t in range(count)])  16.2 us
    ppermute x3, starting transfers between devices, local(): lax.ppermute(sends[n - 1], 'tp', [(t, (t + 2 * n) % count) for t in range...  9.1 us
    ppermute x3, waiting for transfers between devices, local(): lax.ppermute(sends[n - 1], 'tp', [(t, (t + 2 * n) % count) for t in range...  7.78 us
  transfers between devices with their start and end apart: 6, of which 5 were waited for; matrix products, arithmetic and copies ran while one was open for 0% of the time, Pallas kernels for 8%

profile of v5, /device:TPU:6, one launch (start us, length us, event | category | flops | bytes accessed | tf_op | source)
XLA Modules:
  0.0 137.8 jit_solution(12401911344604317990)
XLA Ops:
  0.6 0.0 copy-start
  0.7 0.9 copy-done
  1.5 50.1 %conditional.1 = (bf16[512,768]{1,0:T(8,128)(2,1)}, bf16[512,640]{1,0:T(8,128)(2,1)S(1)}, f32[512,256]{1,0:T(8,128)}, bf16[512,512]{1,0:T(8,128)(2,1)}) conditional(s32[]{:T(128)} %convert_element_type.3, (bf16[512,256]{1,0:T(8,128)(2,1)}, bf16[512,256]{1,0:T(8,128)(2,1)}, bf16[512,256]{1,0:T(8,128)(2,1)}, bf16[512,256]{1,0:T(8,128)(2,1)}, ...), branch_computations={%region_0.1_spmd, %region_1.2_spmd} | conditional | flops 536870912 | bytes 16400588 | solution.py:419
  1.5 0.0 copy-start.4
  1.6 0.0 copy-start.12
  1.6 0.0 copy-start.15
  1.6 2.1 %kernel.2 = bf16[512,768]{1,0:T(8,128)(2,1)} custom-call(bf16[512,256]{1,0:T(8,128)(2,1)} %get-tuple-element.20.refs_0_.q_ref, bf16[512,256]{1,0:T(8,128)(2,1)} %get-tuple-element.21.refs_1_.k_ref, bf16[512,256]{1,0:T(8,128)(2,1)} %get-tuple-element.22.refs_2_.v_ref), custom_call_target="tpu_custom_call" | custom-call | bytes 1572864 | tf_op jit(solution)/shard_map/cond/branch_0_fun/kernel/pallas_call | solution.py:336
  3.7 18.7 %all-to-all-start = ((bf16[64,8,768]{2,1,0:T(8,128)(2,1)}), bf16[64,8,768]{2,1,0:T(8,128)(2,1)S(1)}, u32[]{:S(2)}, u32[]{:S(2)}) async-start(bf16[64,8,768]{2,1,0:T(8,128)(2,1)} %bitcast), calls=%async_computation | async-start | bytes 1572864 | tf_op jit(solution)/shard_map/cond/branch_0_fun/all_to_all | solution.py:349
  22.5 0.0 copy-done.4
  22.5 0.0 copy-done.7
  22.5 0.0 copy-done.12
  22.5 0.0 copy-done.15
  22.5 2.5 %row_forward.2 = (f32[512,256]{1,0:T(8,128)}, bf16[512,128]{1,0:T(8,128)(2,1)S(1)}, bf16[512,512]{1,0:T(8,128)(2,1)S(1)}, bf16[512,512]{1,0:T(8,128)(2,1)}) custom-call(bf16[512,256]{1,0:T(8,128)(2,1)S(1)} %copy-done.12, bf16[512,256]{1,0:T(8,128)(2,1)S(1)} %copy-done.7, bf16[512,256]{1,0:T(8,128)(2,1)S(1)} %copy-done.15, bf16[512,256]{1,0:T(8,128)(2,1)S(1)} %copy-done.4, ...), custom_call_target="tpu_custom_call" | custom-call | flops 268435456 | bytes 2768896 | tf_op jit(solution)/shard_map/cond/branch_0_fun/row_forward/pallas_call | solution.py:336
  25.0 25.5 %all-to-all-done = bf16[64,8,768]{2,1,0:T(8,128)(2,1)S(1)} async-done(((bf16[64,8,768]{2,1,0:T(8,128)(2,1)}), bf16[64,8,768]{2,1,0:T(8,128)(2,1)S(1)}, u32[]{:S(2)}, u32[]{:S(2)}) %all-to-all-start) | async-done | bytes 786464 | tf_op jit(solution)/shard_map/cond/branch_0_fun/all_to_all | solution.py:349
  50.5 1.2 col_forward.1
  51.6 0.0 copy-done.9
  51.7 0.0 copy-start.2
  51.7 0.0 copy-start.10
  51.7 31.4 %all_to_all.47 = bf16[64,8,640]{2,1,0:T(8,128)(2,1)S(1)} all-to-all(bf16[64,8,640]{2,1,0:T(8,128)(2,1)S(1)} %bitcast.20), channel_id=1, replica_groups=mesh['seq'=64,'tp'=8] {'seq'}, dimensions={0} | all-to-all | bytes 1310720 | tf_op jit(solution)/shard_map/all_to_all | solution.py:349
  83.1 0.0 copy-done.2
  83.1 0.0 copy-done.10
  83.1 3.0 %col_backward.1 = bf16[512,768]{1,0:T(8,128)(2,1)} custom-call(bf16[512,768]{1,0:T(8,128)(2,1)S(1)} %copy-done.10, bf16[512,640]{1,0:T(8,128)(2,1)S(1)} %bitcast.15, bf16[512,640]{1,0:T(8,128)(2,1)S(1)} %get-tuple-element.62.sent_ref, bf16[512,512]{1,0:T(8,128)(2,1)} %get-tuple-element.64.bias_hbm), custom_call_target="tpu_custom_call" | custom-call | flops 671088640 | bytes 3407872 | tf_op jit(solution)/shard_map/col_backward/pallas_call | solution.py:336
  86.1 0.0 copy-start.1
  86.1 0.0 copy-start.3
  86.2 7.3 %all-to-all-start.4 = ((bf16[64,8,768]{2,1,0:T(8,128)(2,1)}), bf16[64,8,768]{2,1,0:T(8,128)(2,1)S(1)}, u32[]{:S(2)}, u32[]{:S(2)}) async-start(bf16[64,8,768]{2,1,0:T(8,128)(2,1)} %bitcast.11), calls=%async_computation.4 | async-start | bytes 1572864 | tf_op jit(solution)/shard_map/all_to_all | solution.py:349
  93.5 0.0 copy-done.1
  93.5 0.0 copy-done.3
  93.5 3.9 %row_merge.1 = (bf16[512,256]{1,0:T(8,128)(2,1)S(1)}, bf16[512,1024]{1,0:T(8,128)(2,1)}, f32[512,128]{1,0:T(8,128)S(1)}) custom-call(s32[1]{0:T(128)} %bitcast.7.core_ref, f32[512,256]{1,0:T(8,128)} %get-tuple-element.61.out_ref, bf16[512,640]{1,0:T(8,128)(2,1)} %copy-done.2, bf16[512,640]{1,0:T(8,128)(2,1)S(1)} %bitcast.16, bf16[512,256]{1,0:T(8,128)(2,1)S(1)} %copy-done.3, ...), custom_call_target="tpu_custom_call" | custom-call | flops 268435456 | bytes 4718596 | tf_op jit(solution)/shard_map/row_merge/pallas_call | solution.py:336
  97.4 16.2 %collective-permute-start = (bf16[512,1024]{1,0:T(8,128)(2,1)}, bf16[512,1024]{1,0:T(8,128)(2,1)}, u32[]{:S(2)}, u32[]{:S(2)}) collective-permute-start(bf16[512,1024]{1,0:T(8,128)(2,1)} %get-tuple-element.67), channel_id=1, source_target_pairs={{0,1},{1,0},{2,3},{3,2},{4,5},{5,4},{6,7},{7,6},{8,9},{9,8},{10,11... | collective-permute-start | bytes 3145736 | tf_op jit(solution)/shard_map/ppermute | solution.py:443
  113.6 0.5 project_own.1.keep_ref
  114.0 0.0 copy-start.6
  114.1 0.0 copy-start.11
  114.1 0.0 copy-start.14
  114.1 2.1 %collective-permute-done.got_ref = bf16[512,1024]{1,0:T(8,128)(2,1)} collective-permute-done((bf16[512,1024]{1,0:T(8,128)(2,1)}, bf16[512,1024]{1,0:T(8,128)(2,1)}, u32[]{:S(2)}, u32[]{:S(2)}) %collective-permute-start) | collective-permute-done | bytes 1048608 | tf_op jit(solution)/shard_map/ppermute | solution.py:443
  116.2 1.5 %pair_sum.1 = (f32[512,256]{1,0:T(8,128)S(1)}, bf16[512,256]{1,0:T(8,128)(2,1)S(1)}, bf16[512,256]{1,0:T(8,128)(2,1)S(1)}, bf16[512,256]{1,0:T(8,128)(2,1)S(1)}) custom-call(s32[1]{0:T(128)} %bitcast.6.x_ref, bf16[512,1024]{1,0:T(8,128)(2,1)S(1)} %project_own.1.keep_ref, bf16[512,1024]{1,0:T(8,128)(2,1)} %collective-permute-done.got_ref), custom_call_target="tpu_custom_call" | custom-call | flops 524288 | bytes 3407876 | tf_op jit(solution)/shard_map/pair_sum/pallas_call | solution.py:336
  117.7 3.2 %collective-permute-start.1 = (bf16[512,256]{1,0:T(8,128)(2,1)S(1)}, bf16[512,256]{1,0:T(8,128)(2,1)S(1)}, u32[]{:S(2)}, u32[]{:S(2)}) collective-permute-start(bf16[512,256]{1,0:T(8,128)(2,1)S(1)} %get-tuple-element.69), channel_id=1, source_target_pairs={{0,4},{1,5},{2,6},{3,7},{4,0},{5,1},{6,2},{7,3},{8,12},{9,13},{10,... | collective-permute-start | bytes 786440 | tf_op jit(solution)/shard_map/ppermute | solution.py:455
  120.8 4.0 %collective-permute-start.2 = (bf16[512,256]{1,0:T(8,128)(2,1)S(1)}, bf16[512,256]{1,0:T(8,128)(2,1)S(1)}, u32[]{:S(2)}, u32[]{:S(2)}) collective-permute-start(bf16[512,256]{1,0:T(8,128)(2,1)S(1)} %get-tuple-element.70), channel_id=1, source_target_pairs={{0,2},{1,3},{2,4},{3,5},{4,6},{5,7},{6,0},{7,1},{8,10},{9,11},{10,... | collective-permute-start | bytes 786440 | tf_op jit(solution)/shard_map/ppermute | solution.py:455
  124.9 1.9 %collective-permute-start.3 = (bf16[512,256]{1,0:T(8,128)(2,1)S(1)}, bf16[512,256]{1,0:T(8,128)(2,1)S(1)}, u32[]{:S(2)}, u32[]{:S(2)}) collective-permute-start(bf16[512,256]{1,0:T(8,128)(2,1)S(1)} %get-tuple-element.71), channel_id=1, source_target_pairs={{0,6},{1,7},{2,0},{3,1},{4,2},{5,3},{6,4},{7,5},{8,14},{9,15},{10,... | collective-permute-start | bytes 786440 | tf_op jit(solution)/shard_map/ppermute | solution.py:455
  126.8 0.0 copy-done.6
  126.8 0.0 copy-done.11
  126.8 0.0 copy-done.14
  126.8 1.4 row_backward.1.grad_ref
  128.2 1.7 %collective-permute-done.1.refs_0_ = bf16[512,256]{1,0:T(8,128)(2,1)S(1)} collective-permute-done((bf16[512,256]{1,0:T(8,128)(2,1)S(1)}, bf16[512,256]{1,0:T(8,128)(2,1)S(1)}, u32[]{:S(2)}, u32[]{:S(2)}) %collective-permute-start.1) | collective-permute-done | bytes 262176 | tf_op jit(solution)/shard_map/ppermute | solution.py:455
  129.9 3.2 %collective-permute-done.2.refs_1_ = bf16[512,256]{1,0:T(8,128)(2,1)S(1)} collective-permute-done((bf16[512,256]{1,0:T(8,128)(2,1)S(1)}, bf16[512,256]{1,0:T(8,128)(2,1)S(1)}, u32[]{:S(2)}, u32[]{:S(2)}) %collective-permute-start.2) | collective-permute-done | bytes 262176 | tf_op jit(solution)/shard_map/ppermute | solution.py:455
  133.1 2.9 %collective-permute-done.3.refs_2_ = bf16[512,256]{1,0:T(8,128)(2,1)S(1)} collective-permute-done((bf16[512,256]{1,0:T(8,128)(2,1)S(1)}, bf16[512,256]{1,0:T(8,128)(2,1)S(1)}, u32[]{:S(2)}, u32[]{:S(2)}) %collective-permute-start.3) | collective-permute-done | bytes 262176 | tf_op jit(solution)/shard_map/ppermute | solution.py:455
  136.0 0.8 project_sum.1
  136.8 0.0 all-to-all-done.4
  136.8 1.0 finish.1
  (3 shorter events, 0.0 us)
Async XLA Ops:
  0.6 0.9 copy-start
  1.5 20.9 %copy-start.4 = (bf16[512,256]{1,0:T(8,128)(2,1)S(1)}, bf16[512,256]{1,0:T(8,128)(2,1)}, u32[]{:S(2)}) copy-start(bf16[512,256]{1,0:T(8,128)(2,1)} %get-tuple-element.23.g_ref) | copy-start | bytes 786436 | tf_op jit(solution)/shard_map/cond
  1.5 20.9 %copy-start.7 = (bf16[512,256]{1,0:T(8,128)(2,1)S(1)}, bf16[512,256]{1,0:T(8,128)(2,1)}, u32[]{:S(2)}) copy-start(bf16[512,256]{1,0:T(8,128)(2,1)} %get-tuple-element.21.refs_1_.k_ref) | copy-start | bytes 786436 | tf_op jit(solution)/shard_map/cond
  1.6 20.9 %copy-start.12 = (bf16[512,256]{1,0:T(8,128)(2,1)S(1)}, bf16[512,256]{1,0:T(8,128)(2,1)}, u32[]{:S(2)}) copy-start(bf16[512,256]{1,0:T(8,128)(2,1)} %get-tuple-element.20.refs_0_.q_ref) | copy-start | bytes 786436 | tf_op jit(solution)/shard_map/cond
  1.6 20.9 %copy-start.15 = (bf16[512,256]{1,0:T(8,128)(2,1)S(1)}, bf16[512,256]{1,0:T(8,128)(2,1)}, u32[]{:S(2)}) copy-start(bf16[512,256]{1,0:T(8,128)(2,1)} %get-tuple-element.22.refs_2_.v_ref) | copy-start | bytes 786436 | tf_op jit(solution)/shard_map/cond
  3.7 46.8 %all-to-all-start = ((bf16[64,8,768]{2,1,0:T(8,128)(2,1)}), bf16[64,8,768]{2,1,0:T(8,128)(2,1)S(1)}, u32[]{:S(2)}, u32[]{:S(2)}) async-start(bf16[64,8,768]{2,1,0:T(8,128)(2,1)} %bitcast), calls=%async_computation | async-start | bytes 1572864 | tf_op jit(solution)/shard_map/cond/branch_0_fun/all_to_all | solution.py:349
  50.5 1.2 copy-start.9
  51.7 31.4 %copy-start.2 = (bf16[512,640]{1,0:T(8,128)(2,1)}, bf16[512,640]{1,0:T(8,128)(2,1)S(1)}, u32[]{:S(2)}) copy-start(bf16[512,640]{1,0:T(8,128)(2,1)S(1)} %get-tuple-element.62.sent_ref) | copy-start | bytes 1966084
  51.7 31.4 %copy-start.10 = (bf16[512,768]{1,0:T(8,128)(2,1)S(1)}, bf16[512,768]{1,0:T(8,128)(2,1)}, u32[]{:S(2)}) copy-start(bf16[512,768]{1,0:T(8,128)(2,1)} %get-tuple-element.63.y_ref) | copy-start | bytes 2359300
  86.1 7.3 %copy-start.1 = (bf16[256,2048]{1,0:T(8,128)(2,1)S(1)}, bf16[256,2048]{1,0:T(8,128)(2,1)}, u32[]{:S(2)}) copy-start(bf16[256,2048]{1,0:T(8,128)(2,1)} %weight_ref.3) | copy-start | bytes 3145732
  86.1 7.3 %copy-start.3 = (bf16[512,256]{1,0:T(8,128)(2,1)S(1)}, bf16[512,256]{1,0:T(8,128)(2,1)}, u32[]{:S(2)}) copy-start(bf16[512,256]{1,0:T(8,128)(2,1)} %g_ref.3) | copy-start | bytes 786436
  86.2 50.6 %all-to-all-start.4 = ((bf16[64,8,768]{2,1,0:T(8,128)(2,1)}), bf16[64,8,768]{2,1,0:T(8,128)(2,1)S(1)}, u32[]{:S(2)}, u32[]{:S(2)}) async-start(bf16[64,8,768]{2,1,0:T(8,128)(2,1)} %bitcast.11), calls=%async_computation.4 | async-start | bytes 1572864 | tf_op jit(solution)/shard_map/all_to_all | solution.py:349
  97.4 18.8 %collective-permute-start = (bf16[512,1024]{1,0:T(8,128)(2,1)}, bf16[512,1024]{1,0:T(8,128)(2,1)}, u32[]{:S(2)}, u32[]{:S(2)}) collective-permute-start(bf16[512,1024]{1,0:T(8,128)(2,1)} %get-tuple-element.67), channel_id=1, source_target_pairs={{0,1},{1,0},{2,3},{3,2},{4,5},{5,4},{6,7},{7,6},{8,9},{9,8},{10,11... | collective-permute-start | bytes 3145736 | tf_op jit(solution)/shard_map/ppermute | solution.py:443
  114.0 12.8 %copy-start.6 = (bf16[512,256]{1,0:T(8,128)(2,1)S(1)}, bf16[512,256]{1,0:T(8,128)(2,1)}, u32[]{:S(2)}) copy-start(bf16[512,256]{1,0:T(8,128)(2,1)} %k_ref.1) | copy-start | bytes 786436
  114.1 12.8 %copy-start.11 = (bf16[512,256]{1,0:T(8,128)(2,1)S(1)}, bf16[512,256]{1,0:T(8,128)(2,1)}, u32[]{:S(2)}) copy-start(bf16[512,256]{1,0:T(8,128)(2,1)} %q_ref.1) | copy-start | bytes 786436
  114.1 12.7 %copy-start.14 = (bf16[512,256]{1,0:T(8,128)(2,1)S(1)}, bf16[512,256]{1,0:T(8,128)(2,1)}, u32[]{:S(2)}) copy-start(bf16[512,256]{1,0:T(8,128)(2,1)} %v_ref.1) | copy-start | bytes 786436
  117.7 12.2 %collective-permute-start.1 = (bf16[512,256]{1,0:T(8,128)(2,1)S(1)}, bf16[512,256]{1,0:T(8,128)(2,1)S(1)}, u32[]{:S(2)}, u32[]{:S(2)}) collective-permute-start(bf16[512,256]{1,0:T(8,128)(2,1)S(1)} %get-tuple-element.69), channel_id=1, source_target_pairs={{0,4},{1,5},{2,6},{3,7},{4,0},{5,1},{6,2},{7,3},{8,12},{9,13},{10,... | collective-permute-start | bytes 786440 | tf_op jit(solution)/shard_map/ppermute | solution.py:455
  120.8 12.2 %collective-permute-start.2 = (bf16[512,256]{1,0:T(8,128)(2,1)S(1)}, bf16[512,256]{1,0:T(8,128)(2,1)S(1)}, u32[]{:S(2)}, u32[]{:S(2)}) collective-permute-start(bf16[512,256]{1,0:T(8,128)(2,1)S(1)} %get-tuple-element.70), channel_id=1, source_target_pairs={{0,2},{1,3},{2,4},{3,5},{4,6},{5,7},{6,0},{7,1},{8,10},{9,11},{10,... | collective-permute-start | bytes 786440 | tf_op jit(solution)/shard_map/ppermute | solution.py:455
  124.9 11.1 %collective-permute-start.3 = (bf16[512,256]{1,0:T(8,128)(2,1)S(1)}, bf16[512,256]{1,0:T(8,128)(2,1)S(1)}, u32[]{:S(2)}, u32[]{:S(2)}) collective-permute-start(bf16[512,256]{1,0:T(8,128)(2,1)S(1)} %get-tuple-element.71), channel_id=1, source_target_pairs={{0,6},{1,7},{2,0},{3,1},{4,2},{5,3},{6,4},{7,5},{8,14},{9,15},{10,... | collective-permute-start | bytes 786440 | tf_op jit(solution)/shard_map/ppermute | solution.py:455

commit v6 on v5

--- a/solution.py
+++ b/solution.py
@@ -100,20 +100,33 @@
 
 
 def pack(pieces, refs):
-    *ins, out_ref, sems = refs
-    copies = []
+    *ins, out_ref, held_ref, sems = refs
+    fetch, store = [], []
     at = 0
     for n, (ref, (first, width)) in enumerate(zip(ins, pieces)):
-        copies.append(
-            pltpu.make_async_copy(
-                ref.at[:, first : first + width], out_ref.at[:, at : at + width], sems.at[n]
-            )
-        )
+        held = held_ref.at[:, at : at + width]
+        fetch.append(pltpu.make_async_copy(ref.at[:, first : first + width], held, sems.at[2 * n]))
+        store.append(pltpu.make_async_copy(held, out_ref.at[:, at : at + width], sems.at[2 * n + 1]))
         at += width
-    for copy in copies:
+    for copy in fetch:
         copy.start()
-    for copy in copies:
+    for ready, copy in zip(fetch, store):
+        ready.wait()
+        copy.start()
+    for copy in store:
         copy.wait()
+
+
+def pack_first(core_ref, q_ref, k_ref, v_ref, first_ref, all_ref, held_ref, sems):
+    features = q_ref.shape[1]
+
+    @pl.when(core_ref[0] == 0)
+    def _():
+        pack([(0, features)] * 3, (q_ref, k_ref, v_ref, all_ref, held_ref, sems))
+
+    @pl.when(core_ref[0] != 0)
+    def _():
+        pack([(0, HEAD_DIM)], (k_ref, first_ref, held_ref, sems))
 
 
 def col_forward_joined(first_ref, rest_ref, bias_ref, g_ref, stat_ref, send_ref, y_ref):
@@ -353,8 +366,6 @@
     tokens, features = queries.shape
     heads = features // HEAD_DIM
     width = COLS // lax.axis_size("seq")
-    block = (lax.axis_index("seq") * width) // TILE
-    mask = lax.dynamic_index_in_dim(tile_column_mask, block, 0, keepdims=False)
     product = 2 * COLS * COLS * HEAD_DIM * heads
     exps = COLS * COLS * heads
 
@@ -380,13 +391,15 @@
             (0, 0),
             *[p[0] for p in pieces],
             far=range(len(pieces)),
-            scratch=[pltpu.SemaphoreType.DMA((len(pieces),))],
+            far_out=(0,),
+            scratch=[
+                pltpu.VMEM((tokens, sum(p[2] for p in pieces)), bf16),
+                pltpu.SemaphoreType.DMA((2 * len(pieces),)),
+            ],
         )[0]
 
-    def at_once(queries, key_vectors, value_vectors, attn_grad, mask):
-        qkv = exchange(
-            packed((queries, 0, features), (key_vectors, 0, features), (value_vectors, 0, features))
-        )
+    def at_once(queries, key_vectors, value_vectors, attn_grad, mask, first, every):
+        qkv = exchange(every)
         row_out, row_stat, bias, bias_t = forward(queries, key_vectors, value_vectors, attn_grad, mask)
         (sent,) = call(
             col_forward,
@@ -396,8 +409,8 @@
         )
         return qkv, sent, row_out, bias_t
 
-    def in_two(queries, key_vectors, value_vectors, attn_grad, mask):
-        first = exchange(key_vectors[:, :HEAD_DIM])
+    def in_two(queries, key_vectors, value_vectors, attn_grad, mask, first, every):
+        first = exchange(first)
         row_out, row_stat, bias, bias_t = forward(queries, key_vectors, value_vectors, attn_grad, mask)
         rest = packed(
             (queries, 0, features),
@@ -416,8 +429,18 @@
 
     place = lax.axis_index("tp")
     core = lax.rem(place, 2)
+    first, every = call(
+        pack_first,
+        [arr(HEAD_DIM, bf16), arr(3 * features, bf16)],
+        (0, 0),
+        core.reshape(1), queries, key_vectors, value_vectors,
+        far=(1, 2, 3), far_out=(0, 1),
+        scratch=[pltpu.VMEM((tokens, 3 * features), bf16), pltpu.SemaphoreType.DMA((6,))],
+    )
+    block, first = lax.optimization_barrier(((lax.axis_index("seq") * width) // TILE, first))
+    mask = lax.dynamic_index_in_dim(tile_column_mask, block, 0, keepdims=False)
     qkv, sent, row_out, bias_t = lax.cond(
-        core == 1, in_two, at_once, queries, key_vectors, value_vectors, attn_grad, mask
+        core == 1, in_two, at_once, queries, key_vectors, value_vectors, attn_grad, mask, first, every
     )
     got = exchange(sent)
     (col_grads,) = call(

time: 139 us -> 139 us (level)
  no operation moved by 1% of the time
where the time goes in v6:
time: 139 us; the launch traced here: 137 us
  starting transfers between devices  51.6 us (37%)
  waiting for transfers between devices  35.3 us (25%)
  blocking collectives  31.6 us (23%)
  Pallas kernels  17.7 us (13%)
    all_to_all x1, blocking collectives, exchange(): return lax.all_to_all(x, 'seq', split_axis=0, concat_axis=0, tiled=True)  31.6 us
    all_to_all x2, starting transfers between devices, exchange(): return lax.all_to_all(x, 'seq', split_axis=0, concat_axis=0, tiled=True)  26.2 us
    all_to_all x2, waiting for transfers between devices, exchange(): return lax.all_to_all(x, 'seq', split_axis=0, concat_axis=0, tiled=True)  25.4 us
    pallas_call x10, Pallas kernels, call(): pl.pallas_call(kernel, out_shape=outs, in_specs=[smem if a.ndim == 1 else...  17.7 us
    ppermute x1, starting transfers between devices, local(): pair = lax.ppermute(give, 'tp', [(t, t ^ 1) for t in range(count)])  16.2 us
    ppermute x3, starting transfers between devices, local(): lax.ppermute(sends[n - 1], 'tp', [(t, (t + 2 * n) % count) for t in range...  9.26 us
    ppermute x3, waiting for transfers between devices, local(): lax.ppermute(sends[n - 1], 'tp', [(t, (t + 2 * n) % count) for t in range...  7.77 us
  transfers between devices with their start and end apart: 6, of which 5 were waited for; matrix products, arithmetic and copies ran while one was open for 0% of the time, Pallas kernels for 8%

profile of v6, /device:TPU:6, one launch (start us, length us, event | category | flops | bytes accessed | tf_op | source)
XLA Modules:
  0.0 137.2 jit_solution(9271143021814250079)
XLA Ops:
  0.6 0.0 copy-start
  0.7 2.0 %pack_first.1 = (bf16[512,128]{1,0:T(8,128)(2,1)}, bf16[512,768]{1,0:T(8,128)(2,1)}) custom-call(s32[1]{0:T(128)} %bitcast.7.core_ref, bf16[512,256]{1,0:T(8,128)(2,1)} %q_ref.3, bf16[512,256]{1,0:T(8,128)(2,1)} %k_ref.3, bf16[512,256]{1,0:T(8,128)(2,1)} %v_ref.3), custom_call_target="tpu_custom_call" | custom-call | bytes 1703940 | tf_op jit(solution)/shard_map/pack_first/pallas_call | solution.py:349
  2.6 0.0 copy-done
  2.7 48.1 %conditional.1 = (bf16[512,768]{1,0:T(8,128)(2,1)}, bf16[512,640]{1,0:T(8,128)(2,1)S(1)}, f32[512,256]{1,0:T(8,128)}, bf16[512,512]{1,0:T(8,128)(2,1)}) conditional(s32[]{:T(128)} %convert_element_type.3, (bf16[512,768]{1,0:T(8,128)(2,1)}, bf16[512,256]{1,0:T(8,128)(2,1)}, bf16[512,256]{1,0:T(8,128)(2,1)}, bf16[512,256]{1,0:T(8,128)(2,1)}, ...), branch_computations={%region_0.1_spmd, %region_1.2_spmd} | conditional | flops 536870912 | bytes 14827724 | solution.py:442
  2.7 0.0 copy-start.4
  2.7 0.0 copy-start.9
  2.7 0.0 copy-start.12
  2.7 0.0 copy-start.15
  2.7 18.9 %all-to-all-start = ((bf16[64,8,768]{2,1,0:T(8,128)(2,1)}), bf16[64,8,768]{2,1,0:T(8,128)(2,1)S(1)}, u32[]{:S(2)}, u32[]{:S(2)}) async-start(bf16[64,8,768]{2,1,0:T(8,128)(2,1)} %bitcast), calls=%async_computation | async-start | bytes 1572864 | tf_op jit(solution)/shard_map/cond/branch_0_fun/all_to_all | solution.py:362
  21.6 0.0 copy-done.4
  21.6 0.0 copy-done.9
  21.6 0.0 copy-done.12
  21.6 0.0 copy-done.15
  21.6 2.5 %row_forward.2 = (f32[512,256]{1,0:T(8,128)}, bf16[512,128]{1,0:T(8,128)(2,1)S(1)}, bf16[512,512]{1,0:T(8,128)(2,1)S(1)}, bf16[512,512]{1,0:T(8,128)(2,1)}) custom-call(bf16[512,256]{1,0:T(8,128)(2,1)S(1)} %copy-done.9, bf16[512,256]{1,0:T(8,128)(2,1)S(1)} %copy-done.12, bf16[512,256]{1,0:T(8,128)(2,1)S(1)} %copy-done.15, bf16[512,256]{1,0:T(8,128)(2,1)S(1)} %copy-done.4, ...), custom_call_target="tpu_custom_call" | custom-call | flops 268435456 | bytes 2768896 | tf_op jit(solution)/shard_map/cond/branch_0_fun/row_forward/pallas_call | solution.py:349
  24.2 25.4 %all-to-all-done = bf16[64,8,768]{2,1,0:T(8,128)(2,1)S(1)} async-done(((bf16[64,8,768]{2,1,0:T(8,128)(2,1)}), bf16[64,8,768]{2,1,0:T(8,128)(2,1)S(1)}, u32[]{:S(2)}, u32[]{:S(2)}) %all-to-all-start) | async-done | bytes 786464 | tf_op jit(solution)/shard_map/cond/branch_0_fun/all_to_all | solution.py:362
  49.6 1.2 col_forward.1
  50.8 0.0 copy-done.6
  50.8 0.0 copy-start.2
  50.8 0.0 copy-start.7
  50.8 31.6 %all_to_all.47 = bf16[64,8,640]{2,1,0:T(8,128)(2,1)S(1)} all-to-all(bf16[64,8,640]{2,1,0:T(8,128)(2,1)S(1)} %bitcast.19), channel_id=1, replica_groups=mesh['seq'=64,'tp'=8] {'seq'}, dimensions={0} | all-to-all | bytes 1310720 | tf_op jit(solution)/shard_map/all_to_all | solution.py:362
  82.4 0.0 copy-done.2
  82.4 0.0 copy-done.7
  82.4 3.0 %col_backward.1 = bf16[512,768]{1,0:T(8,128)(2,1)} custom-call(bf16[512,768]{1,0:T(8,128)(2,1)S(1)} %copy-done.7, bf16[512,640]{1,0:T(8,128)(2,1)S(1)} %bitcast.14, bf16[512,640]{1,0:T(8,128)(2,1)S(1)} %get-tuple-element.76.sent_ref, bf16[512,512]{1,0:T(8,128)(2,1)} %get-tuple-element.78.bias_hbm), custom_call_target="tpu_custom_call" | custom-call | flops 671088640 | bytes 3407872 | tf_op jit(solution)/shard_map/col_backward/pallas_call | solution.py:349
  85.4 0.0 copy-start.1
  85.4 0.0 copy-start.3
  85.4 7.3 %all-to-all-start.4 = ((bf16[64,8,768]{2,1,0:T(8,128)(2,1)}), bf16[64,8,768]{2,1,0:T(8,128)(2,1)S(1)}, u32[]{:S(2)}, u32[]{:S(2)}) async-start(bf16[64,8,768]{2,1,0:T(8,128)(2,1)} %bitcast.11), calls=%async_computation.4 | async-start | bytes 1572864 | tf_op jit(solution)/shard_map/all_to_all | solution.py:362
  92.8 0.0 copy-done.1
  92.8 3.9 %row_merge.1 = (bf16[512,256]{1,0:T(8,128)(2,1)S(1)}, bf16[512,1024]{1,0:T(8,128)(2,1)}, f32[512,128]{1,0:T(8,128)S(1)}) custom-call(s32[1]{0:T(128)} %bitcast.7.core_ref, f32[512,256]{1,0:T(8,128)} %get-tuple-element.75.out_ref, bf16[512,640]{1,0:T(8,128)(2,1)} %copy-done.2, bf16[512,640]{1,0:T(8,128)(2,1)S(1)} %bitcast.15, bf16[512,256]{1,0:T(8,128)(2,1)S(1)} %copy-done.3, ...), custom_call_target="tpu_custom_call" | custom-call | flops 268435456 | bytes 4718596 | tf_op jit(solution)/shard_map/row_merge/pallas_call | solution.py:349
  96.7 16.2 %collective-permute-start = (bf16[512,1024]{1,0:T(8,128)(2,1)}, bf16[512,1024]{1,0:T(8,128)(2,1)}, u32[]{:S(2)}, u32[]{:S(2)}) collective-permute-start(bf16[512,1024]{1,0:T(8,128)(2,1)} %get-tuple-element.81), channel_id=1, source_target_pairs={{0,1},{1,0},{2,3},{3,2},{4,5},{5,4},{6,7},{7,6},{8,9},{9,8},{10,11... | collective-permute-start | bytes 3145736 | tf_op jit(solution)/shard_map/ppermute | solution.py:466
  112.9 0.5 project_own.1.keep_ref
  113.3 0.0 copy-start.8
  113.3 0.0 copy-start.11
  113.4 0.0 copy-start.14
  113.4 2.1 %collective-permute-done.got_ref = bf16[512,1024]{1,0:T(8,128)(2,1)} collective-permute-done((bf16[512,1024]{1,0:T(8,128)(2,1)}, bf16[512,1024]{1,0:T(8,128)(2,1)}, u32[]{:S(2)}, u32[]{:S(2)}) %collective-permute-start) | collective-permute-done | bytes 1048608 | tf_op jit(solution)/shard_map/ppermute | solution.py:466
  115.5 1.5 %pair_sum.1 = (f32[512,256]{1,0:T(8,128)S(1)}, bf16[512,256]{1,0:T(8,128)(2,1)S(1)}, bf16[512,256]{1,0:T(8,128)(2,1)S(1)}, bf16[512,256]{1,0:T(8,128)(2,1)S(1)}) custom-call(s32[1]{0:T(128)} %bitcast.6.x_ref, bf16[512,1024]{1,0:T(8,128)(2,1)S(1)} %project_own.1.keep_ref, bf16[512,1024]{1,0:T(8,128)(2,1)} %collective-permute-done.got_ref), custom_call_target="tpu_custom_call" | custom-call | flops 524288 | bytes 3407876 | tf_op jit(solution)/shard_map/pair_sum/pallas_call | solution.py:349
  117.0 3.3 %collective-permute-start.1 = (bf16[512,256]{1,0:T(8,128)(2,1)S(1)}, bf16[512,256]{1,0:T(8,128)(2,1)S(1)}, u32[]{:S(2)}, u32[]{:S(2)}) collective-permute-start(bf16[512,256]{1,0:T(8,128)(2,1)S(1)} %get-tuple-element.83), channel_id=1, source_target_pairs={{0,4},{1,5},{2,6},{3,7},{4,0},{5,1},{6,2},{7,3},{8,12},{9,13},{10,... | collective-permute-start | bytes 786440 | tf_op jit(solution)/shard_map/ppermute | solution.py:478
  120.3 4.0 %collective-permute-start.2 = (bf16[512,256]{1,0:T(8,128)(2,1)S(1)}, bf16[512,256]{1,0:T(8,128)(2,1)S(1)}, u32[]{:S(2)}, u32[]{:S(2)}) collective-permute-start(bf16[512,256]{1,0:T(8,128)(2,1)S(1)} %get-tuple-element.84), channel_id=1, source_target_pairs={{0,2},{1,3},{2,4},{3,5},{4,6},{5,7},{6,0},{7,1},{8,10},{9,11},{10,... | collective-permute-start | bytes 786440 | tf_op jit(solution)/shard_map/ppermute | solution.py:478
  124.3 1.9 %collective-permute-start.3 = (bf16[512,256]{1,0:T(8,128)(2,1)S(1)}, bf16[512,256]{1,0:T(8,128)(2,1)S(1)}, u32[]{:S(2)}, u32[]{:S(2)}) collective-permute-start(bf16[512,256]{1,0:T(8,128)(2,1)S(1)} %get-tuple-element.85), channel_id=1, source_target_pairs={{0,6},{1,7},{2,0},{3,1},{4,2},{5,3},{6,4},{7,5},{8,14},{9,15},{10,... | collective-permute-start | bytes 786440 | tf_op jit(solution)/shard_map/ppermute | solution.py:478
  126.2 0.0 copy-done.8
  126.3 0.0 copy-done.11
  126.3 0.0 copy-done.14
  126.3 1.4 %row_backward.1.grad_ref = f32[512,768]{1,0:T(8,128)S(1)} custom-call(bf16[512,256]{1,0:T(8,128)(2,1)S(1)} %copy-done.8, bf16[512,256]{1,0:T(8,128)(2,1)S(1)} %copy-done.11, bf16[512,256]{1,0:T(8,128)(2,1)S(1)} %copy-done.14, bf16[512,256]{1,0:T(8,128)(2,1)S(1)} %copy-done.3, f32[512,128]{1,0:T(8,128)S(1)} %get-tuple-element.86.merged_ref), custom_call_target="tpu_custom_call" | custom-call | flops 671088640 | bytes 2883584 | tf_op jit(solution)/shard_map/row_backward/pallas_call | solution.py:349
  127.7 1.5 %collective-permute-done.1.refs_0_ = bf16[512,256]{1,0:T(8,128)(2,1)S(1)} collective-permute-done((bf16[512,256]{1,0:T(8,128)(2,1)S(1)}, bf16[512,256]{1,0:T(8,128)(2,1)S(1)}, u32[]{:S(2)}, u32[]{:S(2)}) %collective-permute-start.1) | collective-permute-done | bytes 262176 | tf_op jit(solution)/shard_map/ppermute | solution.py:478
  129.2 3.2 %collective-permute-done.2.refs_1_ = bf16[512,256]{1,0:T(8,128)(2,1)S(1)} collective-permute-done((bf16[512,256]{1,0:T(8,128)(2,1)S(1)}, bf16[512,256]{1,0:T(8,128)(2,1)S(1)}, u32[]{:S(2)}, u32[]{:S(2)}) %collective-permute-start.2) | collective-permute-done | bytes 262176 | tf_op jit(solution)/shard_map/ppermute | solution.py:478
  132.4 3.1 %collective-permute-done.3.refs_2_ = bf16[512,256]{1,0:T(8,128)(2,1)S(1)} collective-permute-done((bf16[512,256]{1,0:T(8,128)(2,1)S(1)}, bf16[512,256]{1,0:T(8,128)(2,1)S(1)}, u32[]{:S(2)}, u32[]{:S(2)}) %collective-permute-start.3) | collective-permute-done | bytes 262176 | tf_op jit(solution)/shard_map/ppermute | solution.py:478
  135.4 0.8 project_sum.1
  136.3 0.0 all-to-all-done.4
  136.3 1.0 finish.1
  (3 shorter events, 0.0 us)
Async XLA Ops:
  0.6 2.0 %copy-start = (s32[4,64,64]{2,1,0:T(8,128)S(1)}, s32[4,64,64]{2,1,0:T(8,128)}, u32[]{:S(2)}) copy-start(s32[4,64,64]{2,1,0:T(8,128)} %param.13) | copy-start | bytes 196612
  2.7 18.9 %copy-start.4 = (bf16[512,256]{1,0:T(8,128)(2,1)S(1)}, bf16[512,256]{1,0:T(8,128)(2,1)}, u32[]{:S(2)}) copy-start(bf16[512,256]{1,0:T(8,128)(2,1)} %get-tuple-element.28.g_ref) | copy-start | bytes 786436 | tf_op jit(solution)/shard_map/cond
  2.7 18.9 %copy-start.9 = (bf16[512,256]{1,0:T(8,128)(2,1)S(1)}, bf16[512,256]{1,0:T(8,128)(2,1)}, u32[]{:S(2)}) copy-start(bf16[512,256]{1,0:T(8,128)(2,1)} %get-tuple-element.25.q_ref) | copy-start | bytes 786436 | tf_op jit(solution)/shard_map/cond
  2.7 18.9 %copy-start.12 = (bf16[512,256]{1,0:T(8,128)(2,1)S(1)}, bf16[512,256]{1,0:T(8,128)(2,1)}, u32[]{:S(2)}) copy-start(bf16[512,256]{1,0:T(8,128)(2,1)} %get-tuple-element.26.k_ref) | copy-start | bytes 786436 | tf_op jit(solution)/shard_map/cond
  2.7 18.9 %copy-start.15 = (bf16[512,256]{1,0:T(8,128)(2,1)S(1)}, bf16[512,256]{1,0:T(8,128)(2,1)}, u32[]{:S(2)}) copy-start(bf16[512,256]{1,0:T(8,128)(2,1)} %get-tuple-element.27.v_ref) | copy-start | bytes 786436 | tf_op jit(solution)/shard_map/cond
  2.7 46.9 %all-to-all-start = ((bf16[64,8,768]{2,1,0:T(8,128)(2,1)}), bf16[64,8,768]{2,1,0:T(8,128)(2,1)S(1)}, u32[]{:S(2)}, u32[]{:S(2)}) async-start(bf16[64,8,768]{2,1,0:T(8,128)(2,1)} %bitcast), calls=%async_computation | async-start | bytes 1572864 | tf_op jit(solution)/shard_map/cond/branch_0_fun/all_to_all | solution.py:362
  49.6 1.2 copy-start.6
  50.8 31.6 %copy-start.2 = (bf16[512,640]{1,0:T(8,128)(2,1)}, bf16[512,640]{1,0:T(8,128)(2,1)S(1)}, u32[]{:S(2)}) copy-start(bf16[512,640]{1,0:T(8,128)(2,1)S(1)} %get-tuple-element.76.sent_ref) | copy-start | bytes 1966084
  50.8 31.6 %copy-start.7 = (bf16[512,768]{1,0:T(8,128)(2,1)S(1)}, bf16[512,768]{1,0:T(8,128)(2,1)}, u32[]{:S(2)}) copy-start(bf16[512,768]{1,0:T(8,128)(2,1)} %get-tuple-element.77.y_ref) | copy-start | bytes 2359300
  85.4 7.3 %copy-start.1 = (bf16[256,2048]{1,0:T(8,128)(2,1)S(1)}, bf16[256,2048]{1,0:T(8,128)(2,1)}, u32[]{:S(2)}) copy-start(bf16[256,2048]{1,0:T(8,128)(2,1)} %weight_ref.3) | copy-start | bytes 3145732
  85.4 7.3 %copy-start.3 = (bf16[512,256]{1,0:T(8,128)(2,1)S(1)}, bf16[512,256]{1,0:T(8,128)(2,1)}, u32[]{:S(2)}) copy-start(bf16[512,256]{1,0:T(8,128)(2,1)} %g_ref.3) | copy-start | bytes 786436
  85.4 50.8 %all-to-all-start.4 = ((bf16[64,8,768]{2,1,0:T(8,128)(2,1)}), bf16[64,8,768]{2,1,0:T(8,128)(2,1)S(1)}, u32[]{:S(2)}, u32[]{:S(2)}) async-start(bf16[64,8,768]{2,1,0:T(8,128)(2,1)} %bitcast.11), calls=%async_computation.4 | async-start | bytes 1572864 | tf_op jit(solution)/shard_map/all_to_all | solution.py:362
  96.7 18.8 %collective-permute-start = (bf16[512,1024]{1,0:T(8,128)(2,1)}, bf16[512,1024]{1,0:T(8,128)(2,1)}, u32[]{:S(2)}, u32[]{:S(2)}) collective-permute-start(bf16[512,1024]{1,0:T(8,128)(2,1)} %get-tuple-element.81), channel_id=1, source_target_pairs={{0,1},{1,0},{2,3},{3,2},{4,5},{5,4},{6,7},{7,6},{8,9},{9,8},{10,11... | collective-permute-start | bytes 3145736 | tf_op jit(solution)/shard_map/ppermute | solution.py:466
  113.3 12.9 %copy-start.8 = (bf16[512,256]{1,0:T(8,128)(2,1)S(1)}, bf16[512,256]{1,0:T(8,128)(2,1)}, u32[]{:S(2)}) copy-start(bf16[512,256]{1,0:T(8,128)(2,1)} %q_ref.3) | copy-start | bytes 786436
  113.3 12.9 %copy-start.11 = (bf16[512,256]{1,0:T(8,128)(2,1)S(1)}, bf16[512,256]{1,0:T(8,128)(2,1)}, u32[]{:S(2)}) copy-start(bf16[512,256]{1,0:T(8,128)(2,1)} %k_ref.3) | copy-start | bytes 786436
  113.4 12.9 %copy-start.14 = (bf16[512,256]{1,0:T(8,128)(2,1)S(1)}, bf16[512,256]{1,0:T(8,128)(2,1)}, u32[]{:S(2)}) copy-start(bf16[512,256]{1,0:T(8,128)(2,1)} %v_ref.3) | copy-start | bytes 786436
  117.0 12.2 %collective-permute-start.1 = (bf16[512,256]{1,0:T(8,128)(2,1)S(1)}, bf16[512,256]{1,0:T(8,128)(2,1)S(1)}, u32[]{:S(2)}, u32[]{:S(2)}) collective-permute-start(bf16[512,256]{1,0:T(8,128)(2,1)S(1)} %get-tuple-element.83), channel_id=1, source_target_pairs={{0,4},{1,5},{2,6},{3,7},{4,0},{5,1},{6,2},{7,3},{8,12},{9,13},{10,... | collective-permute-start | bytes 786440 | tf_op jit(solution)/shard_map/ppermute | solution.py:478
  120.3 12.1 %collective-permute-start.2 = (bf16[512,256]{1,0:T(8,128)(2,1)S(1)}, bf16[512,256]{1,0:T(8,128)(2,1)S(1)}, u32[]{:S(2)}, u32[]{:S(2)}) collective-permute-start(bf16[512,256]{1,0:T(8,128)(2,1)S(1)} %get-tuple-element.84), channel_id=1, source_target_pairs={{0,2},{1,3},{2,4},{3,5},{4,6},{5,7},{6,0},{7,1},{8,10},{9,11},{10,... | collective-permute-start | bytes 786440 | tf_op jit(solution)/shard_map/ppermute | solution.py:478
  124.3 11.1 %collective-permute-start.3 = (bf16[512,256]{1,0:T(8,128)(2,1)S(1)}, bf16[512,256]{1,0:T(8,128)(2,1)S(1)}, u32[]{:S(2)}, u32[]{:S(2)}) collective-permute-start(bf16[512,256]{1,0:T(8,128)(2,1)S(1)} %get-tuple-element.85), channel_id=1, source_target_pairs={{0,6},{1,7},{2,0},{3,1},{4,2},{5,3},{6,4},{7,5},{8,14},{9,15},{10,... | collective-permute-start | bytes 786440 | tf_op jit(solution)/shard_map/ppermute | solution.py:478

commit v7 on v6

--- a/solution.py
+++ b/solution.py
@@ -473,10 +473,10 @@
         (tokens * half, 0),
         (place // 2).reshape(1), keep, pair,
     )
-    far_first = sorted(range(1, chips), key=lambda n: -min(n, chips - n))
+    near_first = sorted(range(1, chips), key=lambda n: min(n, chips - n))
     parts = [
         lax.ppermute(sends[n - 1], "tp", [(t, (t + 2 * n) % count) for t in range(count)])
-        for n in far_first
+        for n in near_first
     ]
     (row_grads,) = call(
         row_backward, [arr(3 * features, f32)], (5 * product, exps),

time: 139 us -> 139 us (level)
  transfers between devices with their start and end apart: 6 -> 6, of which waited for: 5 -> 3; matrix products, arithmetic and copies ran while one was open for 0% -> 0% of each run, Pallas kernels for 8% -> 8%
where the time goes in v7:
time: 139 us; the launch traced here: 138 us
  starting transfers between devices  51.5 us (37%)
  waiting for transfers between devices  36.4 us (26%)
  blocking collectives  31.6 us (23%)
  Pallas kernels  17.7 us (13%)
    all_to_all x1, blocking collectives, exchange(): return lax.all_to_all(x, 'seq', split_axis=0, concat_axis=0, tiled=True)  31.6 us
    all_to_all x2, starting transfers between devices, exchange(): return lax.all_to_all(x, 'seq', split_axis=0, concat_axis=0, tiled=True)  26.2 us
    all_to_all x2, waiting for transfers between devices, exchange(): return lax.all_to_all(x, 'seq', split_axis=0, concat_axis=0, tiled=True)  25.4 us
    pallas_call x10, Pallas kernels, call(): pl.pallas_call(kernel, out_shape=outs, in_specs=[smem if a.ndim == 1 else...  17.7 us
    ppermute x1, starting transfers between devices, local(): pair = lax.ppermute(give, 'tp', [(t, t ^ 1) for t in range(count)])  16.2 us
    ppermute x3, starting transfers between devices, local(): lax.ppermute(sends[n - 1], 'tp', [(t, (t + 2 * n) % count) for t in range...  9.18 us
    ppermute x3, waiting for transfers between devices, local(): lax.ppermute(sends[n - 1], 'tp', [(t, (t + 2 * n) % count) for t in range...  8.81 us
  transfers between devices with their start and end apart: 6, of which 3 were waited for; matrix products, arithmetic and copies ran while one was open for 0% of the time, Pallas kernels for 8%

profile of v7, /device:TPU:6, one launch (start us, length us, event | category | flops | bytes accessed | tf_op | source)
XLA Modules:
  0.0 138.2 jit_solution(5721892072207159169)
XLA Ops:
  0.6 0.0 copy-start
  0.7 2.0 %pack_first.1 = (bf16[512,128]{1,0:T(8,128)(2,1)}, bf16[512,768]{1,0:T(8,128)(2,1)}) custom-call(s32[1]{0:T(128)} %bitcast.7.core_ref, bf16[512,256]{1,0:T(8,128)(2,1)} %q_ref.3, bf16[512,256]{1,0:T(8,128)(2,1)} %k_ref.3, bf16[512,256]{1,0:T(8,128)(2,1)} %v_ref.3), custom_call_target="tpu_custom_call" | custom-call | bytes 1703940 | tf_op jit(solution)/shard_map/pack_first/pallas_call | solution.py:349
  2.6 0.0 copy-done
  2.7 48.1 %conditional.1 = (bf16[512,768]{1,0:T(8,128)(2,1)}, bf16[512,640]{1,0:T(8,128)(2,1)S(1)}, f32[512,256]{1,0:T(8,128)}, bf16[512,512]{1,0:T(8,128)(2,1)}) conditional(s32[]{:T(128)} %convert_element_type.3, (bf16[512,768]{1,0:T(8,128)(2,1)}, bf16[512,256]{1,0:T(8,128)(2,1)}, bf16[512,256]{1,0:T(8,128)(2,1)}, bf16[512,256]{1,0:T(8,128)(2,1)}, ...), branch_computations={%region_0.1_spmd, %region_1.2_spmd} | conditional | flops 536870912 | bytes 14827724 | solution.py:442
  2.7 0.0 copy-start.4
  2.7 0.0 copy-start.9
  2.7 0.0 copy-start.12
  2.7 0.0 copy-start.15
  2.7 18.9 %all-to-all-start = ((bf16[64,8,768]{2,1,0:T(8,128)(2,1)}), bf16[64,8,768]{2,1,0:T(8,128)(2,1)S(1)}, u32[]{:S(2)}, u32[]{:S(2)}) async-start(bf16[64,8,768]{2,1,0:T(8,128)(2,1)} %bitcast), calls=%async_computation | async-start | bytes 1572864 | tf_op jit(solution)/shard_map/cond/branch_0_fun/all_to_all | solution.py:362
  21.6 0.0 copy-done.4
  21.6 0.0 copy-done.9
  21.6 0.0 copy-done.12
  21.6 0.0 copy-done.15
  21.6 2.5 %row_forward.2 = (f32[512,256]{1,0:T(8,128)}, bf16[512,128]{1,0:T(8,128)(2,1)S(1)}, bf16[512,512]{1,0:T(8,128)(2,1)S(1)}, bf16[512,512]{1,0:T(8,128)(2,1)}) custom-call(bf16[512,256]{1,0:T(8,128)(2,1)S(1)} %copy-done.9, bf16[512,256]{1,0:T(8,128)(2,1)S(1)} %copy-done.12, bf16[512,256]{1,0:T(8,128)(2,1)S(1)} %copy-done.15, bf16[512,256]{1,0:T(8,128)(2,1)S(1)} %copy-done.4, ...), custom_call_target="tpu_custom_call" | custom-call | flops 268435456 | bytes 2768896 | tf_op jit(solution)/shard_map/cond/branch_0_fun/row_forward/pallas_call | solution.py:349
  24.2 25.4 %all-to-all-done = bf16[64,8,768]{2,1,0:T(8,128)(2,1)S(1)} async-done(((bf16[64,8,768]{2,1,0:T(8,128)(2,1)}), bf16[64,8,768]{2,1,0:T(8,128)(2,1)S(1)}, u32[]{:S(2)}, u32[]{:S(2)}) %all-to-all-start) | async-done | bytes 786464 | tf_op jit(solution)/shard_map/cond/branch_0_fun/all_to_all | solution.py:362
  49.6 1.2 col_forward.1
  50.8 0.0 copy-done.6
  50.8 0.0 copy-start.2
  50.8 0.0 copy-start.7
  50.8 31.6 %all_to_all.47 = bf16[64,8,640]{2,1,0:T(8,128)(2,1)S(1)} all-to-all(bf16[64,8,640]{2,1,0:T(8,128)(2,1)S(1)} %bitcast.19), channel_id=1, replica_groups=mesh['seq'=64,'tp'=8] {'seq'}, dimensions={0} | all-to-all | bytes 1310720 | tf_op jit(solution)/shard_map/all_to_all | solution.py:362
  82.4 0.0 copy-done.2
  82.4 0.0 copy-done.7
  82.4 3.0 %col_backward.1 = bf16[512,768]{1,0:T(8,128)(2,1)} custom-call(bf16[512,768]{1,0:T(8,128)(2,1)S(1)} %copy-done.7, bf16[512,640]{1,0:T(8,128)(2,1)S(1)} %bitcast.14, bf16[512,640]{1,0:T(8,128)(2,1)S(1)} %get-tuple-element.76.sent_ref, bf16[512,512]{1,0:T(8,128)(2,1)} %get-tuple-element.78.bias_hbm), custom_call_target="tpu_custom_call" | custom-call | flops 671088640 | bytes 3407872 | tf_op jit(solution)/shard_map/col_backward/pallas_call | solution.py:349
  85.4 0.0 copy-start.1
  85.4 0.0 copy-start.3
  85.4 7.3 %all-to-all-start.4 = ((bf16[64,8,768]{2,1,0:T(8,128)(2,1)}), bf16[64,8,768]{2,1,0:T(8,128)(2,1)S(1)}, u32[]{:S(2)}, u32[]{:S(2)}) async-start(bf16[64,8,768]{2,1,0:T(8,128)(2,1)} %bitcast.11), calls=%async_computation.4 | async-start | bytes 1572864 | tf_op jit(solution)/shard_map/all_to_all | solution.py:362
  92.8 0.0 copy-done.1
  92.8 0.0 copy-done.3
  92.8 3.9 %row_merge.1 = (bf16[512,256]{1,0:T(8,128)(2,1)S(1)}, bf16[512,1024]{1,0:T(8,128)(2,1)}, f32[512,128]{1,0:T(8,128)S(1)}) custom-call(s32[1]{0:T(128)} %bitcast.7.core_ref, f32[512,256]{1,0:T(8,128)} %get-tuple-element.75.out_ref, bf16[512,640]{1,0:T(8,128)(2,1)} %copy-done.2, bf16[512,640]{1,0:T(8,128)(2,1)S(1)} %bitcast.15, bf16[512,256]{1,0:T(8,128)(2,1)S(1)} %copy-done.3, ...), custom_call_target="tpu_custom_call" | custom-call | flops 268435456 | bytes 4718596 | tf_op jit(solution)/shard_map/row_merge/pallas_call | solution.py:349
  96.7 16.2 %collective-permute-start = (bf16[512,1024]{1,0:T(8,128)(2,1)}, bf16[512,1024]{1,0:T(8,128)(2,1)}, u32[]{:S(2)}, u32[]{:S(2)}) collective-permute-start(bf16[512,1024]{1,0:T(8,128)(2,1)} %get-tuple-element.81), channel_id=1, source_target_pairs={{0,1},{1,0},{2,3},{3,2},{4,5},{5,4},{6,7},{7,6},{8,9},{9,8},{10,11... | collective-permute-start | bytes 3145736 | tf_op jit(solution)/shard_map/ppermute | solution.py:466
  112.9 0.5 project_own.1.keep_ref
  113.3 0.0 copy-start.8
  113.3 0.0 copy-start.11
  113.4 0.0 copy-start.14
  113.4 2.1 %collective-permute-done.got_ref = bf16[512,1024]{1,0:T(8,128)(2,1)} collective-permute-done((bf16[512,1024]{1,0:T(8,128)(2,1)}, bf16[512,1024]{1,0:T(8,128)(2,1)}, u32[]{:S(2)}, u32[]{:S(2)}) %collective-permute-start) | collective-permute-done | bytes 1048608 | tf_op jit(solution)/shard_map/ppermute | solution.py:466
  115.5 1.5 %pair_sum.1 = (f32[512,256]{1,0:T(8,128)S(1)}, bf16[512,256]{1,0:T(8,128)(2,1)S(1)}, bf16[512,256]{1,0:T(8,128)(2,1)S(1)}, bf16[512,256]{1,0:T(8,128)(2,1)S(1)}) custom-call(s32[1]{0:T(128)} %bitcast.6.x_ref, bf16[512,1024]{1,0:T(8,128)(2,1)S(1)} %project_own.1.keep_ref, bf16[512,1024]{1,0:T(8,128)(2,1)} %collective-permute-done.got_ref), custom_call_target="tpu_custom_call" | custom-call | flops 524288 | bytes 3407876 | tf_op jit(solution)/shard_map/pair_sum/pallas_call | solution.py:349
  117.0 2.4 %collective-permute-start.1 = (bf16[512,256]{1,0:T(8,128)(2,1)S(1)}, bf16[512,256]{1,0:T(8,128)(2,1)S(1)}, u32[]{:S(2)}, u32[]{:S(2)}) collective-permute-start(bf16[512,256]{1,0:T(8,128)(2,1)S(1)} %get-tuple-element.83), channel_id=1, source_target_pairs={{0,2},{1,3},{2,4},{3,5},{4,6},{5,7},{6,0},{7,1},{8,10},{9,11},{10,... | collective-permute-start | bytes 786440 | tf_op jit(solution)/shard_map/ppermute | solution.py:478
  119.4 3.4 %collective-permute-start.2 = (bf16[512,256]{1,0:T(8,128)(2,1)S(1)}, bf16[512,256]{1,0:T(8,128)(2,1)S(1)}, u32[]{:S(2)}, u32[]{:S(2)}) collective-permute-start(bf16[512,256]{1,0:T(8,128)(2,1)S(1)} %get-tuple-element.84), channel_id=1, source_target_pairs={{0,6},{1,7},{2,0},{3,1},{4,2},{5,3},{6,4},{7,5},{8,14},{9,15},{10,... | collective-permute-start | bytes 786440 | tf_op jit(solution)/shard_map/ppermute | solution.py:478
  122.8 3.3 %collective-permute-start.3 = (bf16[512,256]{1,0:T(8,128)(2,1)S(1)}, bf16[512,256]{1,0:T(8,128)(2,1)S(1)}, u32[]{:S(2)}, u32[]{:S(2)}) collective-permute-start(bf16[512,256]{1,0:T(8,128)(2,1)S(1)} %get-tuple-element.85), channel_id=1, source_target_pairs={{0,4},{1,5},{2,6},{3,7},{4,0},{5,1},{6,2},{7,3},{8,12},{9,13},{10,... | collective-permute-start | bytes 786440 | tf_op jit(solution)/shard_map/ppermute | solution.py:478
  126.2 0.0 copy-done.8
  126.2 0.0 copy-done.11
  126.2 1.4 row_backward.1.grad_ref
  127.6 0.0 collective-permute-done.1.refs_0_
  127.6 8.8 %collective-permute-done.2.refs_1_ = bf16[512,256]{1,0:T(8,128)(2,1)S(1)} collective-permute-done((bf16[512,256]{1,0:T(8,128)(2,1)S(1)}, bf16[512,256]{1,0:T(8,128)(2,1)S(1)}, u32[]{:S(2)}, u32[]{:S(2)}) %collective-permute-start.2) | collective-permute-done | bytes 262176 | tf_op jit(solution)/shard_map/ppermute | solution.py:478
  136.4 0.0 collective-permute-done.3.refs_2_
  136.4 0.8 project_sum.1
  137.2 0.0 all-to-all-done.4
  137.2 1.0 finish.1
  (3 shorter events, 0.0 us)
Async XLA Ops:
  0.6 2.0 %copy-start = (s32[4,64,64]{2,1,0:T(8,128)S(1)}, s32[4,64,64]{2,1,0:T(8,128)}, u32[]{:S(2)}) copy-start(s32[4,64,64]{2,1,0:T(8,128)} %param.13) | copy-start | bytes 196612
  2.7 18.9 %copy-start.4 = (bf16[512,256]{1,0:T(8,128)(2,1)S(1)}, bf16[512,256]{1,0:T(8,128)(2,1)}, u32[]{:S(2)}) copy-start(bf16[512,256]{1,0:T(8,128)(2,1)} %get-tuple-element.28.g_ref) | copy-start | bytes 786436 | tf_op jit(solution)/shard_map/cond
  2.7 18.9 %copy-start.9 = (bf16[512,256]{1,0:T(8,128)(2,1)S(1)}, bf16[512,256]{1,0:T(8,128)(2,1)}, u32[]{:S(2)}) copy-start(bf16[512,256]{1,0:T(8,128)(2,1)} %get-tuple-element.25.q_ref) | copy-start | bytes 786436 | tf_op jit(solution)/shard_map/cond
  2.7 18.9 %copy-start.12 = (bf16[512,256]{1,0:T(8,128)(2,1)S(1)}, bf16[512,256]{1,0:T(8,128)(2,1)}, u32[]{:S(2)}) copy-start(bf16[512,256]{1,0:T(8,128)(2,1)} %get-tuple-element.26.k_ref) | copy-start | bytes 786436 | tf_op jit(solution)/shard_map/cond
  2.7 18.9 %copy-start.15 = (bf16[512,256]{1,0:T(8,128)(2,1)S(1)}, bf16[512,256]{1,0:T(8,128)(2,1)}, u32[]{:S(2)}) copy-start(bf16[512,256]{1,0:T(8,128)(2,1)} %get-tuple-element.27.v_ref) | copy-start | bytes 786436 | tf_op jit(solution)/shard_map/cond
  2.7 46.9 %all-to-all-start = ((bf16[64,8,768]{2,1,0:T(8,128)(2,1)}), bf16[64,8,768]{2,1,0:T(8,128)(2,1)S(1)}, u32[]{:S(2)}, u32[]{:S(2)}) async-start(bf16[64,8,768]{2,1,0:T(8,128)(2,1)} %bitcast), calls=%async_computation | async-start | bytes 1572864 | tf_op jit(solution)/shard_map/cond/branch_0_fun/all_to_all | solution.py:362
  49.6 1.2 copy-start.6
  50.8 31.6 %copy-start.2 = (bf16[512,640]{1,0:T(8,128)(2,1)}, bf16[512,640]{1,0:T(8,128)(2,1)S(1)}, u32[]{:S(2)}) copy-start(bf16[512,640]{1,0:T(8,128)(2,1)S(1)} %get-tuple-element.76.sent_ref) | copy-start | bytes 1966084
  50.8 31.6 %copy-start.7 = (bf16[512,768]{1,0:T(8,128)(2,1)S(1)}, bf16[512,768]{1,0:T(8,128)(2,1)}, u32[]{:S(2)}) copy-start(bf16[512,768]{1,0:T(8,128)(2,1)} %get-tuple-element.77.y_ref) | copy-start | bytes 2359300
  85.4 7.3 %copy-start.1 = (bf16[256,2048]{1,0:T(8,128)(2,1)S(1)}, bf16[256,2048]{1,0:T(8,128)(2,1)}, u32[]{:S(2)}) copy-start(bf16[256,2048]{1,0:T(8,128)(2,1)} %weight_ref.3) | copy-start | bytes 3145732
  85.4 7.3 %copy-start.3 = (bf16[512,256]{1,0:T(8,128)(2,1)S(1)}, bf16[512,256]{1,0:T(8,128)(2,1)}, u32[]{:S(2)}) copy-start(bf16[512,256]{1,0:T(8,128)(2,1)} %g_ref.3) | copy-start | bytes 786436
  85.4 51.8 %all-to-all-start.4 = ((bf16[64,8,768]{2,1,0:T(8,128)(2,1)}), bf16[64,8,768]{2,1,0:T(8,128)(2,1)S(1)}, u32[]{:S(2)}, u32[]{:S(2)}) async-start(bf16[64,8,768]{2,1,0:T(8,128)(2,1)} %bitcast.11), calls=%async_computation.4 | async-start | bytes 1572864 | tf_op jit(solution)/shard_map/all_to_all | solution.py:362
  96.7 18.8 %collective-permute-start = (bf16[512,1024]{1,0:T(8,128)(2,1)}, bf16[512,1024]{1,0:T(8,128)(2,1)}, u32[]{:S(2)}, u32[]{:S(2)}) collective-permute-start(bf16[512,1024]{1,0:T(8,128)(2,1)} %get-tuple-element.81), channel_id=1, source_target_pairs={{0,1},{1,0},{2,3},{3,2},{4,5},{5,4},{6,7},{7,6},{8,9},{9,8},{10,11... | collective-permute-start | bytes 3145736 | tf_op jit(solution)/shard_map/ppermute | solution.py:466
  113.3 12.8 %copy-start.8 = (bf16[512,256]{1,0:T(8,128)(2,1)S(1)}, bf16[512,256]{1,0:T(8,128)(2,1)}, u32[]{:S(2)}) copy-start(bf16[512,256]{1,0:T(8,128)(2,1)} %q_ref.3) | copy-start | bytes 786436
  113.3 12.8 %copy-start.11 = (bf16[512,256]{1,0:T(8,128)(2,1)S(1)}, bf16[512,256]{1,0:T(8,128)(2,1)}, u32[]{:S(2)}) copy-start(bf16[512,256]{1,0:T(8,128)(2,1)} %k_ref.3) | copy-start | bytes 786436
  113.4 12.8 %copy-start.14 = (bf16[512,256]{1,0:T(8,128)(2,1)S(1)}, bf16[512,256]{1,0:T(8,128)(2,1)}, u32[]{:S(2)}) copy-start(bf16[512,256]{1,0:T(8,128)(2,1)} %v_ref.3) | copy-start | bytes 786436
  117.0 10.6 %collective-permute-start.1 = (bf16[512,256]{1,0:T(8,128)(2,1)S(1)}, bf16[512,256]{1,0:T(8,128)(2,1)S(1)}, u32[]{:S(2)}, u32[]{:S(2)}) collective-permute-start(bf16[512,256]{1,0:T(8,128)(2,1)S(1)} %get-tuple-element.83), channel_id=1, source_target_pairs={{0,2},{1,3},{2,4},{3,5},{4,6},{5,7},{6,0},{7,1},{8,10},{9,11},{10,... | collective-permute-start | bytes 786440 | tf_op jit(solution)/shard_map/ppermute | solution.py:478
  119.4 17.0 %collective-permute-start.2 = (bf16[512,256]{1,0:T(8,128)(2,1)S(1)}, bf16[512,256]{1,0:T(8,128)(2,1)S(1)}, u32[]{:S(2)}, u32[]{:S(2)}) collective-permute-start(bf16[512,256]{1,0:T(8,128)(2,1)S(1)} %get-tuple-element.84), channel_id=1, source_target_pairs={{0,6},{1,7},{2,0},{3,1},{4,2},{5,3},{6,4},{7,5},{8,14},{9,15},{10,... | collective-permute-start | bytes 786440 | tf_op jit(solution)/shard_map/ppermute | solution.py:478
  122.8 13.6 %collective-permute-start.3 = (bf16[512,256]{1,0:T(8,128)(2,1)S(1)}, bf16[512,256]{1,0:T(8,128)(2,1)S(1)}, u32[]{:S(2)}, u32[]{:S(2)}) collective-permute-start(bf16[512,256]{1,0:T(8,128)(2,1)S(1)} %get-tuple-element.85), channel_id=1, source_target_pairs={{0,4},{1,5},{2,6},{3,7},{4,0},{5,1},{6,2},{7,3},{8,12},{9,13},{10,... | collective-permute-start | bytes 786440 | tf_op jit(solution)/shard_map/ppermute | solution.py:478
